TPU v7x, 32 devices: a whole 2x2x4 slice. The times are simulated.
32 devices in a mesh: replica: 4 (over x, core), group: 8 (over z, y).
Axes of the slice: x: 2, y: 2, z: 4, core: 2. Of those that a mesh axis runs over, the one named last changes fastest.
Arguments:
- block_input: bfloat16 [24576, 768], P(('replica', 'group')), may hold values from -6 to 6
- out_grad: bfloat16 [24576, 768], P(('replica', 'group')), may hold values from -6 to 6
- image_pos: int32 [24576, 2], P(('replica', 'group')), may hold values from 0 to 197, as said below
- routes: int32 [24576, 2], P(('replica', 'group')), may hold values from 0 to 3, all different within a row; in each aligned block of 768 rows (0 to 767, 768 to 1535, ...) at most 480 rows name the same one
- norm_weight: float32 [4, 768], P(None, 'group'), as said below
- norm_moment: float32 [4, 768], P(None, 'group')
- norm_squares: float32 [4, 768], P(None, 'group'), as said below
- qkv_weight: float32 [768, 2304], P('group'), may hold values from -0.21875 to 0.21875
- qkv_moment: float32 [768, 2304], P('group')
- qkv_squares: float32 [768, 2304], P('group'), as said below
- proj_weight: float32 [768, 768], P('group'), may hold values from -1.75 to 1.75
- proj_moment: float32 [768, 768], P('group')
- proj_squares: float32 [768, 768], P('group'), as said below
- router_weight: float32 [768, 4], P('group'), may hold values from -0.15625 to 0.15625
- router_moment: float32 [768, 4], P('group')
- router_squares: float32 [768, 4], P('group'), as said below
- inner_weight: float32 [4, 768, 3072], P(None, 'group'), may hold values from -0.21875 to 0.21875
- inner_moment: float32 [4, 768, 3072], P(None, 'group')
- inner_squares: float32 [4, 768, 3072], P(None, 'group'), as said below
- outer_weight: float32 [4, 3072, 768], P(None, None, 'group'), may hold values from -0.4375 to 0.4375
- outer_moment: float32 [4, 3072, 768], P(None, None, 'group')
- outer_squares: float32 [4, 3072, 768], P(None, None, 'group'), as said below
Outputs:
- block_output: bfloat16 [24576, 768], P(('replica', 'group'))
- input_grad: bfloat16 [24576, 768], P(('replica', 'group'))
- norm_drift: float32 [4, 768], P(None, 'group')
- norm_energy: float32 [4, 768], P(None, 'group')
- norm_after: float32 [4, 768], P(None, 'group')
- qkv_drift: float32 [768, 2304], P('group')
- qkv_energy: float32 [768, 2304], P('group')
- qkv_after: float32 [768, 2304], P('group')
- proj_drift: float32 [768, 768], P('group')
- proj_energy: float32 [768, 768], P('group')
- proj_after: float32 [768, 768], P('group')
- router_drift: float32 [768, 4], P('group')
- router_energy: float32 [768, 4], P('group')
- router_after: float32 [768, 4], P('group')
- inner_drift: float32 [4, 768, 3072], P(None, 'group')
- inner_energy: float32 [4, 768, 3072], P(None, 'group')
- inner_after: float32 [4, 768, 3072], P(None, 'group')
- outer_drift: float32 [4, 3072, 768], P(None, None, 'group')
- outer_energy: float32 [4, 3072, 768], P(None, None, 'group')
- outer_after: float32 [4, 3072, 768], P(None, None, 'group')
Inputs may be any that keep to these rules, and one draw needn't show every extreme that they name: `image_pos`: rows are laid out image after image in row order; images hold 98 to 197 tokens; column 1 is the length of the row's image and the same on all its rows; column 0 rises by one from row to row and returns to 0 where the next image begins; no image begins at a row that is a multiple of 768 other than row 0; the first image may begin before row 0 and the last may end after the last row. `routes`: a token's two experts differ; within the rows of one device no expert is named by more than 480 tokens. `norm_weight`: rows 0 and 2 are gains, rows 1 and 3 biases. `norm_squares`: positive. `qkv_squares`: positive. `proj_squares`: positive. `router_squares`: positive. `inner_squares`: positive. `outer_squares`: positive.
All inputs are finite; a program needn't handle non-finite values.
Results may differ from a plain program's by a relative error of at most 0.025.
Values may be sent and summed in bfloat16 or wider, within the bound.
No kernel may reach another device: no remote copies, remote signals or barrier semaphores. Data moves between devices by JAX's collectives and lax.ppermute only.
A program may use at most 384 MiB of HBM per device.

v0:
```python
from functools import partial

import jax
import jax.numpy as jnp
from jax import lax
from jax.sharding import PartitionSpec as P

HEADS = 12
IMG = 197
STEP = 10


NORM_EPS = 1e-06
MASKED = -1e30
RATES = (0.5, 0.08, 0.6, 0.06, 0.08, 0.15)


def extended(cells, sides, width):
    for axis, dim in sides:
        count = lax.axis_size(axis)
        ends = count - 1
        head = lax.slice_in_dim(cells, 0, width, axis=dim)
        tail = lax.slice_in_dim(cells, cells.shape[dim] - width, cells.shape[dim], axis=dim)
        cells = jnp.concatenate(
            [
                lax.ppermute(tail, axis, [(i, (i + 1) % count) for i in range(ends)]),
                cells,
                lax.ppermute(head, axis, [((i + 1) % count, i) for i in range(ends)]),
            ],
            axis=dim,
        )
    return cells


def standardize(values):
    centre = jnp.mean(values, axis=-1, keepdims=True)
    shifted = values - centre
    row_scale = lax.rsqrt(jnp.mean(shifted * shifted, axis=-1, keepdims=True) + NORM_EPS)
    return (shifted * row_scale, row_scale)


def norm_back(grad_norm, normed, row_scale, gain_row):
    grad_hat = grad_norm * gain_row
    centred = grad_hat - jnp.mean(grad_hat, axis=-1, keepdims=True)
    return row_scale * (centred - normed * jnp.mean(grad_hat * normed, axis=-1, keepdims=True))


def window_mask(positions, first_row, row_count, all_rows):
    halo_width = IMG - 1
    key_count = row_count + 2 * halo_width
    query_index = lax.broadcasted_iota(jnp.int32, (row_count, key_count), 0)
    key_index = lax.broadcasted_iota(jnp.int32, (row_count, key_count), 1)
    offset = key_index - halo_width - query_index + positions[:, 0:1]
    global_key = first_row - halo_width + key_index
    return (
        (offset >= 0) & (offset < positions[:, 1:2]) & (global_key >= 0) & (global_key < all_rows)
    )


def route_slots(routes, expert_count, capacity):
    row_count, route_count = routes.shape
    chosen = routes[:, :, None] == jnp.arange(expert_count, dtype=jnp.int32)[None, None, :]
    chosen_int = chosen.astype(jnp.int32)
    per_expert = jnp.sum(chosen_int, axis=1)
    before = jnp.cumsum(per_expert, axis=0) - per_expert
    slot_rank = jnp.sum(chosen_int * before[:, None, :], axis=-1)
    slot_index = routes * capacity + slot_rank
    flat_slots = slot_index.reshape(-1)
    row_ids = jnp.repeat(jnp.arange(row_count, dtype=jnp.int32), route_count)
    source_row = jnp.zeros((expert_count * capacity,), jnp.int32).at[flat_slots].set(row_ids)
    occupied = jnp.zeros((expert_count * capacity,), jnp.bool_).at[flat_slots].set(True)
    return (chosen, slot_index, source_row, occupied)


def attention_scores(queries, keys_win, allowed, score_scale):
    raw = (
        jnp.einsum("qhd,khd->hqk", queries, keys_win, preferred_element_type=jnp.float32)
        * score_scale
    )
    return jnp.where(allowed[None], raw, MASKED)


def adam_step(weight, moment, squares, gradient, rate_value):
    drift = 0.9 * moment + 0.1 * gradient
    energy = 0.999 * squares + 0.001 * gradient * gradient
    first_hat = drift / (1.0 - 0.9**STEP)
    second_hat = energy / (1.0 - 0.999**STEP)
    after = weight - rate_value * (first_hat / (jnp.sqrt(second_hat) + 1e-08) + 0.1 * weight)
    return (drift, energy, after)


def fetch_all(rounded):
    return (
        lax.all_gather(rounded[0], "group", axis=1, tiled=True),
        lax.all_gather(rounded[1], "group", axis=0, tiled=True),
        lax.all_gather(rounded[2], "group", axis=0, tiled=True),
        lax.all_gather(rounded[3], "group", axis=0, tiled=True),
        lax.all_gather(rounded[4], "group", axis=1, tiled=True),
        lax.all_gather(rounded[5], "group", axis=2, tiled=True),
    )


def per_device(
    block_input,
    out_grad,
    image_pos,
    routes,
    norm_weight,
    norm_moment,
    norm_squares,
    qkv_weight,
    qkv_moment,
    qkv_squares,
    proj_weight,
    proj_moment,
    proj_squares,
    router_weight,
    router_moment,
    router_squares,
    inner_weight,
    inner_moment,
    inner_squares,
    outer_weight,
    outer_moment,
    outer_squares,
):
    row_count, model_width = block_input.shape
    head_size = model_width // HEADS
    halo_width = IMG - 1
    capacity = 5 * row_count // 8
    score_scale = head_size ** (-0.5)
    expert_count = inner_weight.shape[0]
    group_size = lax.axis_size("group")
    masters = (norm_weight, qkv_weight, proj_weight, router_weight, inner_weight, outer_weight)
    rounded = tuple((master.astype(jnp.bfloat16) for master in masters))
    gathered = fetch_all(rounded)
    dense = gathered[:4]
    device_pos = lax.axis_index(("replica", "group"))
    all_rows = row_count * lax.axis_size("replica") * group_size
    norm_full = dense[0].astype(jnp.float32)
    x_float = block_input.astype(jnp.float32)
    normed_one, scale_one = standardize(x_float)
    first_in = (normed_one * norm_full[0] + norm_full[1]).astype(jnp.bfloat16)
    qkv_rows = jnp.dot(first_in, dense[1], preferred_element_type=jnp.float32).astype(jnp.bfloat16)
    kv_window = extended(qkv_rows[:, model_width:], ((("replica", "group"), 0),), IMG - 1)
    queries = qkv_rows[:, :model_width].reshape(row_count, HEADS, head_size)
    keys_win = kv_window[:, :model_width].reshape(-1, HEADS, head_size)
    values_win = kv_window[:, model_width:].reshape(-1, HEADS, head_size)
    allowed = window_mask(image_pos, device_pos * row_count, row_count, all_rows)
    attn_scores = attention_scores(queries, keys_win, allowed, score_scale)
    row_peak = jnp.max(attn_scores, axis=-1, keepdims=True)
    expo_scores = jnp.exp(attn_scores - row_peak)
    exp_total = jnp.sum(expo_scores, axis=-1, keepdims=True)
    log_total = row_peak + jnp.log(exp_total)
    attn_probs = (expo_scores / exp_total).astype(jnp.bfloat16)
    context = jnp.einsum("hqk,khd->qhd", attn_probs, values_win, preferred_element_type=jnp.float32)
    context = context.reshape(row_count, model_width).astype(jnp.bfloat16)
    residual = x_float + jnp.dot(context, dense[2], preferred_element_type=jnp.float32)
    normed_two, scale_two = standardize(residual)
    second_in = (normed_two * norm_full[2] + norm_full[3]).astype(jnp.bfloat16)
    router_logits = jnp.dot(second_in, dense[3], preferred_element_type=jnp.float32)
    logit_peak = jnp.max(router_logits, axis=-1, keepdims=True)
    logit_expo = jnp.exp(router_logits - logit_peak)
    gate_probs = logit_expo / jnp.sum(logit_expo, axis=-1, keepdims=True)
    chosen, slot_index, source_row, occupied = route_slots(routes, expert_count, capacity)
    gate_values = jnp.sum(jnp.where(chosen, gate_probs[:, None, :], 0.0), axis=-1)
    slot_gate = (
        jnp.zeros((expert_count * capacity,), jnp.float32)
        .at[slot_index.reshape(-1)]
        .set(gate_values.reshape(-1))
    )
    slot_input = jnp.where(occupied[:, None], second_in[source_row], jnp.zeros((), jnp.bfloat16))
    slot_input = slot_input.reshape(expert_count, capacity, model_width)
    gelu_exact = partial(jax.nn.gelu, approximate=False)
    pre_act = jnp.einsum(
        "ecd,edf->ecf", slot_input, gathered[4], preferred_element_type=jnp.float32
    )
    activated = gelu_exact(pre_act).astype(jnp.bfloat16)
    expert_out = jnp.einsum(
        "ecf,efd->ecd", activated, gathered[5], preferred_element_type=jnp.float32
    )
    token_out = expert_out.reshape(-1, model_width)[slot_index]
    block_output = (residual + jnp.sum(gate_values[:, :, None] * token_out, axis=1)).astype(
        jnp.bfloat16
    )
    grad_out = out_grad.astype(jnp.float32)
    gate_grad = jnp.sum(grad_out[:, None, :] * token_out, axis=-1)
    slot_grad = jnp.where(occupied[:, None], slot_gate[:, None] * grad_out[source_row], 0.0)
    slot_grad = slot_grad.astype(jnp.bfloat16).reshape(expert_count, capacity, model_width)
    back_all = fetch_all(rounded)
    dense_back = back_all[:4]
    outer_grad = jnp.einsum(
        "ecf,ecd->efd", activated, slot_grad, preferred_element_type=jnp.float32
    )
    act_grad = jnp.einsum(
        "ecd,efd->ecf", slot_grad, back_all[5], preferred_element_type=jnp.float32
    )
    pre_grad = jax.vjp(gelu_exact, pre_act)[1](act_grad)[0].astype(jnp.bfloat16)
    inner_grad = jnp.einsum(
        "ecd,ecf->edf", slot_input, pre_grad, preferred_element_type=jnp.float32
    )
    slot_in_grad = jnp.einsum(
        "ecf,edf->ecd", pre_grad, back_all[4], preferred_element_type=jnp.float32
    )
    norm_back_full = dense_back[0].astype(jnp.float32)
    second_grad = jnp.sum(slot_in_grad.reshape(-1, model_width)[slot_index], axis=1)
    prob_grad = jnp.sum(jnp.where(chosen, gate_grad[:, :, None], 0.0), axis=1)
    logit_grad = gate_probs * (prob_grad - jnp.sum(gate_probs * prob_grad, axis=-1, keepdims=True))
    logit_grad = logit_grad.astype(jnp.bfloat16)
    router_grad = jnp.dot(second_in.T, logit_grad, preferred_element_type=jnp.float32)
    second_grad = second_grad + jnp.dot(
        logit_grad, dense_back[3].T, preferred_element_type=jnp.float32
    )
    gain_two_grad = jnp.sum(second_grad * normed_two, axis=0)
    bias_two_grad = jnp.sum(second_grad, axis=0)
    resid_grad = grad_out + norm_back(second_grad, normed_two, scale_two, norm_back_full[2])
    branch_grad = resid_grad.astype(jnp.bfloat16)
    proj_grad = jnp.dot(context.T, branch_grad, preferred_element_type=jnp.float32)
    context_grad = jnp.dot(branch_grad, dense_back[2].T, preferred_element_type=jnp.float32)
    context_grad = context_grad.astype(jnp.bfloat16).reshape(row_count, HEADS, head_size)
    again_scores = attention_scores(queries, keys_win, allowed, score_scale)
    probs_back = jnp.exp(again_scores - log_total)
    probs_round = probs_back.astype(jnp.bfloat16)
    prob_back_grad = jnp.einsum(
        "qhd,khd->hqk", context_grad, values_win, preferred_element_type=jnp.float32
    )
    score_grad = probs_back * (
        prob_back_grad - jnp.sum(probs_back * prob_back_grad, axis=-1, keepdims=True)
    )
    score_grad = score_grad.astype(jnp.bfloat16)
    query_grad = (
        jnp.einsum("hqk,khd->qhd", score_grad, keys_win, preferred_element_type=jnp.float32)
        * score_scale
    )
    key_grad = (
        jnp.einsum("hqk,qhd->khd", score_grad, queries, preferred_element_type=jnp.float32)
        * score_scale
    )
    value_grad = jnp.einsum(
        "hqk,qhd->khd", probs_round, context_grad, preferred_element_type=jnp.float32
    )
    window_grad = jnp.concatenate(
        [key_grad.reshape(-1, model_width), value_grad.reshape(-1, model_width)], axis=1
    )
    edge_rims = jnp.concatenate(
        [window_grad[:halo_width], window_grad[halo_width + row_count :]], axis=0
    )
    padded_rims = extended(
        edge_rims.astype(jnp.bfloat16), ((("replica", "group"), 0),), halo_width
    ).astype(edge_rims.dtype)
    from_below = padded_rims[:halo_width]
    from_above = padded_rims[3 * halo_width :]
    own_grad = window_grad[halo_width : halo_width + row_count]
    own_grad = own_grad.at[:halo_width].add(from_below)
    own_grad = own_grad.at[row_count - halo_width :].add(from_above)
    qkv_grad_rows = jnp.concatenate(
        [query_grad.reshape(row_count, model_width), own_grad], axis=1
    ).astype(jnp.bfloat16)
    qkv_grad = jnp.dot(first_in.T, qkv_grad_rows, preferred_element_type=jnp.float32)
    first_grad = jnp.dot(qkv_grad_rows, dense_back[1].T, preferred_element_type=jnp.float32)
    gain_one_grad = jnp.sum(first_grad * normed_one, axis=0)
    bias_one_grad = jnp.sum(first_grad, axis=0)
    input_grad = (
        resid_grad + norm_back(first_grad, normed_one, scale_one, norm_back_full[0])
    ).astype(jnp.bfloat16)
    norm_grad = jnp.stack([gain_one_grad, bias_one_grad, gain_two_grad, bias_two_grad], axis=0)
    summed = (
        lax.psum_scatter(
            norm_grad.astype(jnp.bfloat16), "group", scatter_dimension=1, tiled=True
        ).astype(jnp.float32),
        lax.psum_scatter(
            qkv_grad.astype(jnp.bfloat16), "group", scatter_dimension=0, tiled=True
        ).astype(jnp.float32),
        lax.psum_scatter(
            proj_grad.astype(jnp.bfloat16), "group", scatter_dimension=0, tiled=True
        ).astype(jnp.float32),
        lax.psum_scatter(
            router_grad.astype(jnp.bfloat16), "group", scatter_dimension=0, tiled=True
        ).astype(jnp.float32),
        lax.psum_scatter(
            inner_grad.astype(jnp.bfloat16), "group", scatter_dimension=1, tiled=True
        ).astype(jnp.float32),
        lax.psum_scatter(
            outer_grad.astype(jnp.bfloat16), "group", scatter_dimension=2, tiled=True
        ).astype(jnp.float32),
    )
    summed = (
        lax.psum(summed[0].astype(jnp.bfloat16), "replica").astype(jnp.float32),
        lax.psum(summed[1].astype(jnp.bfloat16), "replica").astype(jnp.float32),
        lax.psum(summed[2].astype(jnp.bfloat16), "replica").astype(jnp.float32),
        lax.psum(summed[3].astype(jnp.bfloat16), "replica").astype(jnp.float32),
        lax.psum(summed[4].astype(jnp.bfloat16), "replica").astype(jnp.float32),
        lax.psum(summed[5].astype(jnp.bfloat16), "replica").astype(jnp.float32),
    )
    norm_drift, norm_energy, norm_after = adam_step(
        norm_weight, norm_moment, norm_squares, summed[0], RATES[0]
    )
    qkv_drift, qkv_energy, qkv_after = adam_step(
        qkv_weight, qkv_moment, qkv_squares, summed[1], RATES[1]
    )
    proj_drift, proj_energy, proj_after = adam_step(
        proj_weight, proj_moment, proj_squares, summed[2], RATES[2]
    )
    router_drift, router_energy, router_after = adam_step(
        router_weight, router_moment, router_squares, summed[3], RATES[3]
    )
    inner_drift, inner_energy, inner_after = adam_step(
        inner_weight, inner_moment, inner_squares, summed[4], RATES[4]
    )
    outer_drift, outer_energy, outer_after = adam_step(
        outer_weight, outer_moment, outer_squares, summed[5], RATES[5]
    )
    return (
        block_output,
        input_grad,
        norm_drift,
        norm_energy,
        norm_after,
        qkv_drift,
        qkv_energy,
        qkv_after,
        proj_drift,
        proj_energy,
        proj_after,
        router_drift,
        router_energy,
        router_after,
        inner_drift,
        inner_energy,
        inner_after,
        outer_drift,
        outer_energy,
        outer_after,
    )


def solution(mesh):
    return jax.shard_map(
        per_device,
        mesh=mesh,
        in_specs=(
            P(("replica", "group"), None),
            P(("replica", "group"), None),
            P(("replica", "group"), None),
            P(("replica", "group"), None),
            P(None, "group"),
            P(None, "group"),
            P(None, "group"),
            P("group", None),
            P("group", None),
            P("group", None),
            P("group", None),
            P("group", None),
            P("group", None),
            P("group", None),
            P("group", None),
            P("group", None),
            P(None, "group", None),
            P(None, "group", None),
            P(None, "group", None),
            P(None, None, "group"),
            P(None, None, "group"),
            P(None, None, "group"),
        ),
        out_specs=(
            P(("replica", "group"), None),
            P(("replica", "group"), None),
            P(None, "group"),
            P(None, "group"),
            P(None, "group"),
            P("group", None),
            P("group", None),
            P("group", None),
            P("group", None),
            P("group", None),
            P("group", None),
            P("group", None),
            P("group", None),
            P("group", None),
            P(None, "group", None),
            P(None, "group", None),
            P(None, "group", None),
            P(None, None, "group"),
            P(None, None, "group"),
            P(None, None, "group"),
        ),
        check_vma=False,
    )
```

profile of v0, /device:TPU:23, one launch (start us, length us, event | category | flops | bytes accessed | tf_op | source)
XLA Modules:
  0.0 2172.5 jit_solution(9812754320549902282)
XLA Ops:
  20.7 11.5 all-gather
  43.6 31.2 %all-gather.7.cloned.1.call-done = bf16[768,2304]{1,0:T(8,128)(2,1)} async-done(((bf16[96,2304]{1,0:T(8,128)(2,1)}), bf16[768,2304]{1,0:T(8,128)(2,1)}) %all-gather.7.cloned.1.call-update) | async-done | bytes 3538960 | tf_op jit(solution)/shard_map/all_gather | solution.py:95
  89.5 11.2 scatter_custom_fusion
  102.4 21.2 all-gather.1
  142.1 17.8 concatenate.20
  170.9 19.2 fusion.94
  190.1 16.8 fusion
  207.0 18.8 fusion.42
  246.1 247.4 %all-gather.11.cloned.1.call-done = bf16[4,768,3072]{2,1,0:T(8,128)(2,1)} async-done(((bf16[4,96,3072]{2,1,0:T(8,128)(2,1)}), bf16[4,768,3072]{2,1,0:T(8,128)(2,1)}) %all-gather.11.cloned.1.call-update) | async-done | bytes 18874384 | tf_op jit(solution)/shard_map/all_gather | solution.py:98
  493.5 25.3 %fusion.14 = (u8[480,3072]{1,0:T(8,128)(4,1)S(1)}, u8[480,3072]{1,0:T(8,128)(4,1)}, f32[4,480,3072]{2,1,0:T(8,128)}) fusion(bf16[4,768,3072]{2,1,0:T(8,128)(2,1)} %all-gather.11.cloned.1.call-done, bf16[4,480,768]{2,1,0:T(8,128)(2,1)} %bitcast.91, pred[4,480]{1,0:T(4,128)(4,1)S(1)} %copy-done.63), kind=kOutput, calls=%fused_computation.53 | convolution fusion | flops 9134899200 | bytes 48367488 | tf_op jit(solution)/shard_map/ecd,edf->ecf/dot_general | solution.py:175
  518.8 56.6 %multiply_convert_fusion.1 = (bf16[4,480,3072]{2,1,0:T(8,128)(2,1)}, f32[4,480,3072]{2,1,0:T(8,128)}) fusion(f32[4,480,3072]{2,1,0:T(8,128)} %get-tuple-element.221, u8[480,3072]{1,0:T(8,128)(4,1)} %get-tuple-element.165, u8[480,3072]{1,0:T(8,128)(4,1)S(1)} %get-tuple-element.164), kind=kLoop, calls=%fused_computation.23 | loop fusion | flops 412876800 | bytes 61931520 | tf_op jit(solution)/shard_map/convert_element_type | solution.py:178
  575.4 282.5 %all-gather.13.cloned.1.call-done = bf16[4,3072,768]{1,2,0:T(8,128)(2,1)} async-done(((bf16[4,3072,96]{1,2,0:T(8,128)(2,1)}), bf16[4,3072,768]{1,2,0:T(8,128)(2,1)}) %all-gather.13.cloned.1.call-update) | async-done | bytes 18874384 | tf_op jit(solution)/shard_map/all_gather | solution.py:99
  857.9 17.5 fusion.98
  891.8 13.4 multiply_reduce_fusion.1
  906.1 33.6 %add_convert_fusion = bf16[4,480,3072]{2,1,0:T(8,128)(2,1)} fusion(f32[4,480,3072]{2,1,0:T(8,128)} %get-tuple-element.208, f32[4,480,3072]{2,1,0:T(8,128)} %get-tuple-element.221, bf16[4,3072,768]{1,2,0:T(8,128)(2,1)} %all-gather.13.cloned.1.call-done, f32[4,480,768]{2,1,0:T(8,128)} %bitcast.88, f32[4,480]{1,0:T(4,128)S(1)} %mul.429, ...), kind=kOutput, calls=%fused_computation.22 | convolution fusion | flops 9146695680 | bytes 83764608 | tf_op jit(solution)/shard_map/ecd,efd->ecf/dot_general | solution.py:195
  939.7 17.5 fusion.99
  957.1 9.6 gather_fusion.3
  1000.3 18.2 fusion.8
  1018.5 31.4 %multiply_reduce_fusion = (f32[12,768]{1,0:T(8,128)S(1)}, f32[12,768,1160]{1,2,0:T(8,128)}) fusion(f32[12,768,1160]{1,2,0:T(8,128)} %get-tuple-element.218, f32[12,768]{1,0:T(8,128)S(1)} %copy-done.22, bf16[768,12,64]{0,2,1:T(8,128)(2,1)S(1)} %bitcast.87, bf16[1160,12,64]{0,2,1:T(8,128)(2,1)S(1)} %bitcast.85), kind=kOutput, calls=%fused_computation.8 | convolution fusion | flops 1400454144 | bytes 88559616 | tf_op jit(solution)/shard_map/qhd,khd->hqk/dot_general | solution.py:224
  1059.4 35.2 %multiply_convert_fusion = bf16[12,768,1160]{1,2,0:T(8,128)(2,1)} fusion(f32[12,768,1160]{1,2,0:T(8,128)} %get-tuple-element.226, f32[12,768,1160]{1,2,0:T(8,128)} %get-tuple-element.218, f32[12,768]{1,0:T(8,128)S(1)} %get-tuple-element.225, f32[12,768]{1,0:T(8,128)S(1)} %copy-done.22), kind=kLoop, calls=%fused_computation.7 | loop fusion | flops 42762240 | bytes 106979328 | tf_op jit(solution)/shard_map/convert_element_type | solution.py:230
  1094.6 11.8 convolution_multiply_fusion
  1121.8 11.8 multiply_convert_fusion.2
  1170.8 18.2 convolution_convert_fusion
  1189.3 18.9 convolution_convert_fusion.1
  1228.2 46.5 %reduce-scatter.11.cloned.1.call-done = bf16[96,2304]{1,0:T(8,128)(2,1)} async-done(((bf16[768,2304]{1,0:T(8,128)(2,1)}), bf16[96,2304]{1,0:T(8,128)(2,1)}) %reduce-scatter.11.cloned.1.call-update) | async-done | bytes 442384 | tf_op jit(solution)/shard_map/reduce_scatter | solution.py:271
  1274.8 315.8 %reduce-scatter.17.cloned.1.call-done = bf16[4,3072,96]{1,2,0:T(8,128)(2,1)} async-done(((bf16[4,3072,768]{1,2,0:T(8,128)(2,1)}), bf16[4,3072,96]{1,2,0:T(8,128)(2,1)}) %reduce-scatter.17.cloned.1.call-update) | async-done | bytes 2359312 | tf_op jit(solution)/shard_map/reduce_scatter | solution.py:283
  1590.5 316.4 %reduce-scatter.15.cloned.1.call-done = bf16[4,96,3072]{2,1,0:T(8,128)(2,1)} async-done(((bf16[4,768,3072]{2,1,0:T(8,128)(2,1)}), bf16[4,96,3072]{2,1,0:T(8,128)(2,1)}) %reduce-scatter.15.cloned.1.call-update) | async-done | bytes 2359312 | tf_op jit(solution)/shard_map/reduce_scatter | solution.py:280
  1909.4 59.6 %reduce-scatter.21.cloned.1.call-done = bf16[96,4]{1,0:T(8,128)(2,1)} async-done(((bf16[768,4]{1,0:T(8,128)(2,1)}), bf16[96,4]{1,0:T(8,128)(2,1)}) %reduce-scatter.21.cloned.1.call-update) | async-done | bytes 784
  1977.6 55.3 %reduce-scatter.19.cloned.1.call-done = bf16[96,4]{1,0:T(8,128)(2,1)} async-done(((bf16[768,4]{1,0:T(8,128)(2,1)}), bf16[96,4]{1,0:T(8,128)(2,1)}) %reduce-scatter.19.cloned.1.call-update) | async-done | bytes 784
  2044.3 96.6 %all-reduce.4.cloned.1.call-done = (bf16[96,2304]{1,0:T(8,128)(2,1)}, bf16[96,768]{1,0:T(8,128)(2,1)}, bf16[4,96,3072]{2,1,0:T(8,128)(2,1)}, bf16[4,3072,96]{1,2,0:T(8,128)(2,1)}) async-done(((bf16[96,2304]{1,0:T(8,128)(2,1)}, bf16[96,768]{1,0:T(8,128)(2,1)}, bf16[4,96,3072]{2,1,0:T(8,128)(2,1)}, bf16[4,3072,96]{1,2,0:T(8,128)(2,1)}), (bf16[96,2304]{1,0:T(8,128)(2,1)}, bf16[96,768]{1,0:T(8,128)(2,1)}, ...) | async-done | bytes 5308432 | tf_op jit(solution)/shard_map/psum | solution.py:289
  2141.0 11.4 multiply_subtract_fusion
  2152.4 10.3 multiply_subtract_fusion.1
  (284 shorter events, 248.8 us)
Async XLA Ops:
  7.2 67.7 %all-gather.7.cloned.1.call-start = ((), (), s32[]{:S(2)}) async-start(), calls=%async_computation.6 | async-start | bytes 3981312 | tf_op jit(solution)/shard_map/all_gather | solution.py:95
  9.2 216.6 %all-gather.9.cloned.1.call-start = ((), (), s32[]{:S(2)}) async-start(), calls=%async_computation.7 | async-start | bytes 1327104 | tf_op jit(solution)/shard_map/all_gather | solution.py:96
  11.0 482.5 %all-gather.11.cloned.1.call-start = ((), (), s32[]{:S(2)}) async-start(), calls=%async_computation.8 | async-start | bytes 21233664 | tf_op jit(solution)/shard_map/all_gather | solution.py:98
  15.1 842.8 %all-gather.13.cloned.1.call-start = ((), (), s32[]{:S(2)}) async-start(), calls=%async_computation.9 | async-start | bytes 21233664 | tf_op jit(solution)/shard_map/all_gather | solution.py:99
  19.4 1208.9 %reduce-scatter.13.cloned.1.call-start = ((), (), s32[]{:S(2)}) async-start(), calls=%async_computation.11 | async-start | bytes 1327104 | tf_op jit(solution)/shard_map/reduce_scatter | solution.py:274
  20.1 205.8 %copy-start.7 = (bf16[768,768]{0,1:T(8,128)(2,1)}, bf16[768,768]{0,1:T(8,128)(2,1)S(1)}, u32[]{:S(2)}) copy-start(bf16[768,768]{0,1:T(8,128)(2,1)S(1)} %copy.155) | copy-start | bytes 3538948
  20.3 60.1 %copy-start.45 = (f32[768]{0:T(1024)}, f32[768]{0:T(1024)S(1)}, u32[]{:S(2)}) copy-start(f32[768]{0:T(1024)S(1)} %broadcast_multiply_fusion.5) | copy-start | bytes 9220
  20.7 59.7 %copy-start.51 = (f32[768]{0:T(1024)}, f32[768]{0:T(1024)S(1)}, u32[]{:S(2)}) copy-start(f32[768]{0:T(1024)S(1)} %add_rsqrt_fusion.1) | copy-start | bytes 9220
  32.3 48.1 %copy-start.49 = (f32[768]{0:T(1024)}, f32[768]{0:T(1024)S(1)}, u32[]{:S(2)}) copy-start(f32[768]{0:T(1024)S(1)} %get-tuple-element.178) | copy-start | bytes 9220
  32.3 48.1 %copy-start.61 = (f32[768]{0:T(1024)}, f32[768]{0:T(1024)S(1)}, u32[]{:S(2)}) copy-start(f32[768]{0:T(1024)S(1)} %get-tuple-element.177) | copy-start | bytes 9220
  32.4 196.7 %copy-start.41 = (f32[768]{0:T(1024)}, f32[768]{0:T(1024)S(1)}, u32[]{:S(2)}) copy-start(f32[768]{0:T(1024)S(1)} %get-tuple-element.175) | copy-start | bytes 9220
  34.6 54.8 %copy-start.55 = (s32[1536]{0:T(1024)}, s32[1536]{0:T(1024)S(1)}, u32[]{:S(2)}) copy-start(s32[1536]{0:T(1024)S(1)} %fusion.59) | copy-start | bytes 18436
  74.9 49.4 %copy-start.24 = (bf16[768,768]{1,0:T(8,128)(2,1)S(1)}, bf16[768,768]{1,0:T(8,128)(2,1)}, u32[]{:S(2)}) copy-start(bf16[768,768]{1,0:T(8,128)(2,1)} %param.27) | copy-start | bytes 3538948
  83.4 58.7 %collective-permute-start = (bf16[196,1536]{1,0:T(8,128)(2,1)}, bf16[196,1536]{1,0:T(8,128)(2,1)}, u32[]{:S(2)}, u32[]{:S(2)}) collective-permute-start(bf16[196,1536]{1,0:T(8,128)(2,1)} %get-tuple-element.214), channel_id=1, source_target_pairs={{0,1},{1,2},{2,3},{3,4},{4,5},{5,6},{6,7},{7,8},{8,9},{9,10},{10,1... | collective-permute-start | bytes 1806344 | tf_op jit(solution)/shard_map/ppermute | solution.py:26
  87.3 54.8 %collective-permute-start.1 = (bf16[196,1536]{1,0:T(8,128)(2,1)}, bf16[196,1536]{1,0:T(8,128)(2,1)}, u32[]{:S(2)}, u32[]{:S(2)}) collective-permute-start(bf16[196,1536]{1,0:T(8,128)(2,1)} %get-tuple-element.213), channel_id=1, source_target_pairs={{1,0},{2,1},{3,2},{4,3},{5,4},{6,5},{7,6},{8,7},{9,8},{10,9},{11,1... | collective-permute-start | bytes 1806344 | tf_op jit(solution)/shard_map/ppermute | solution.py:28
  166.6 23.4 %copy-start.9 = (bf16[1160,768]{0,1:T(8,128)(2,1)}, bf16[1160,768]{0,1:T(8,128)(2,1)S(1)}, u32[]{:S(2)}) copy-start(bf16[1160,768]{0,1:T(8,128)(2,1)S(1)} %copy.159) | copy-start | bytes 5345284
  190.1 16.9 copy-start.30
  190.1 16.9 copy-start.14
  206.9 18.9 copy-start.34
  231.2 262.3 %copy-start.63 = (pred[4,480]{1,0:T(4,128)(4,1)S(1)}, pred[4,480]{1,0:T(4,128)(4,1)}, u32[]{:S(2)}) copy-start(pred[4,480]{1,0:T(4,128)(4,1)} %broadcast_in_dim.117) | copy-start | bytes 5764
  245.4 660.6 %copy-start.56 = (f32[4,480]{1,0:T(4,128)}, f32[4,480]{1,0:T(4,128)S(1)}, u32[]{:S(2)}) copy-start(f32[4,480]{1,0:T(4,128)S(1)} %mul.429) | copy-start | bytes 23044
  857.9 17.5 copy-start.2
  1000.3 18.3 copy-start.15
  1059.4 35.2 %copy-start.11 = (bf16[768,768]{0,1:T(8,128)(2,1)S(1)}, bf16[768,768]{0,1:T(8,128)(2,1)}, u32[]{:S(2)}) copy-start(bf16[768,768]{0,1:T(8,128)(2,1)} %copy.158) | copy-start | bytes 3538948
  1115.4 32.1 %collective-permute-start.2 = (bf16[196,1536]{1,0:T(8,128)(2,1)S(1)}, bf16[196,1536]{1,0:T(8,128)(2,1)}, u32[]{:S(2)}, u32[]{:S(2)}) collective-permute-start(bf16[196,1536]{1,0:T(8,128)(2,1)S(1)} %get-tuple-element.209), channel_id=1, source_target_pairs={{0,1},{1,2},{2,3},{3,4},{4,5},{5,6},{6,7},{7,8},{8,9},{9,10},{10,1... | collective-permute-start | bytes 1806344 | tf_op jit(solution)/shard_map/ppermute | solution.py:26
  1119.6 29.5 %collective-permute-start.3 = (bf16[196,1536]{1,0:T(8,128)(2,1)S(1)}, bf16[196,1536]{1,0:T(8,128)(2,1)}, u32[]{:S(2)}, u32[]{:S(2)}) collective-permute-start(bf16[196,1536]{1,0:T(8,128)(2,1)S(1)} %get-tuple-element.210), channel_id=1, source_target_pairs={{1,0},{2,1},{3,2},{4,3},{5,4},{6,5},{7,6},{8,7},{9,8},{10,9},{11,1... | collective-permute-start | bytes 1806344 | tf_op jit(solution)/shard_map/ppermute | solution.py:28
  1121.6 153.2 %reduce-scatter.11.cloned.1.call-start = ((), (), s32[]{:S(2)}) async-start(), calls=%async_computation.10 | async-start | bytes 3981312 | tf_op jit(solution)/shard_map/reduce_scatter | solution.py:271
  1170.8 419.8 %reduce-scatter.17.cloned.1.call-start = ((), (), s32[]{:S(2)}) async-start(), calls=%async_computation.13 | async-start | bytes 21233664 | tf_op jit(solution)/shard_map/reduce_scatter | solution.py:283
  1189.0 717.9 %reduce-scatter.15.cloned.1.call-start = ((), (), s32[]{:S(2)}) async-start(), calls=%async_computation.12 | async-start | bytes 21233664 | tf_op jit(solution)/shard_map/reduce_scatter | solution.py:280
  1208.2 760.8 %reduce-scatter.21.cloned.1.call-start = ((), (), s32[]{:S(2)}) async-start(), calls=%async_computation.15 | async-start | bytes 221184
  1213.5 819.4 %reduce-scatter.19.cloned.1.call-start = ((), (), s32[]{:S(2)}) async-start(), calls=%async_computation.14 | async-start | bytes 221184
  1228.2 912.8 %all-reduce.4.cloned.1.call-start = ((), (), s32[]{:S(2)}) async-start(), calls=%async_computation.16 | async-start | bytes 10616832 | tf_op jit(solution)/shard_map/psum | solution.py:289
  (49 other events, 361.8 us)
Sparse Core Ops, SparseCore 0:
  10.8 64.0 all-gather.6
  77.6 50.4 all-gather.8
  130.2 363.2 all-gather.10
  495.5 362.4 all-gather.12
  1121.7 68.8 reduce-scatter.12
  1194.6 80.0 reduce-scatter.10
  1278.6 311.8 reduce-scatter.16
  1594.4 312.5 reduce-scatter.14
  1910.8 58.1 reduce-scatter.20
  1972.7 60.1 reduce-scatter.18
  2035.5 105.4 all-reduce.3
where the time goes:
time: 2180 us; the launch traced here: 2170 us
  waiting for transfers between devices  1460 us (67%)
  matrix products  275 us (13%)
  other arithmetic  207 us (9%)
  local copies, waits for them, and re-layouts  163 us (7%)
  blocking collectives  40.6 us (2%)
    reduce_scatter x1, waiting for transfers between devices, per_device(): lax.psum_scatter(inner_grad.astype(jnp.bfloat16), 'group', scatter_dimens...  316 us
    reduce_scatter x1, waiting for transfers between devices, per_device(): lax.psum_scatter(outer_grad.astype(jnp.bfloat16), 'group', scatter_dimens...  316 us
    all_gather x1, waiting for transfers between devices, fetch_all(): lax.all_gather(rounded[5], 'group', axis=2, tiled=True)  283 us
    all_gather x1, waiting for transfers between devices, fetch_all(): lax.all_gather(rounded[4], 'group', axis=1, tiled=True)  247 us
    unnamed x13, waiting for transfers between devices  115 us
    psum x1, waiting for transfers between devices, per_device(): lax.psum(summed[1].astype(jnp.bfloat16), 'replica').astype(jnp.float32)  96.6 us
    convert_element_type x1, other arithmetic, per_device(): activated = gelu_exact(pre_act).astype(jnp.bfloat16)  56.6 us
    reduce_scatter x1, waiting for transfers between devices, per_device(): lax.psum_scatter(qkv_grad.astype(jnp.bfloat16), 'group', scatter_dimensio...  46.5 us
  transfers between devices with their start and end apart: 15, of which 11 were waited for; matrix products, arithmetic and copies ran while one was open for 16% of the time, Pallas kernels for 0%

commit v1 on v0

v1 whole, which is shorter than its diff:
```python
from functools import partial

import jax
import jax.numpy as jnp
from jax import lax
from jax.experimental import pallas as pl
from jax.experimental.pallas import tpu as pltpu
from jax.sharding import PartitionSpec as P

HEADS = 12
IMG = 197
STEP = 10
NORM_EPS = 1e-06
MASKED = -1e30
RATES = (0.5, 0.08, 0.6, 0.06, 0.08, 0.15)
LANES = 128
QB = 128
HALO = 256
SPAN = QB + 2 * HALO
CORE_BIT = 1
CHIP_BIT = 2
F32 = jnp.float32
BF16 = jnp.bfloat16
NT = (((1,), (1,)), ((), ()))


def swap(block, bit):
    count = lax.axis_size("replica")
    return lax.ppermute(block, "replica", [(r, r ^ bit) for r in range(count)])


def spread(block):
    other_chip = swap(block, CHIP_BIT)
    return [block, other_chip, swap(block, CORE_BIT), swap(other_chip, CORE_BIT)]


def quarter_of(replica):
    return (replica & 1) * 2 + ((replica >> 1) & 1)


def pick(blocks, index):
    return lax.dynamic_index_in_dim(jnp.stack(blocks), index, 0, keepdims=False)


def shift(head, tail, axes):
    count = lax.axis_size(axes)
    up = [(i, i + 1) for i in range(count - 1)]
    down = [(i + 1, i) for i in range(count - 1)]
    return lax.ppermute(tail, axes, up), lax.ppermute(head, axes, down)


def standardize(values):
    centre = jnp.mean(values, axis=-1, keepdims=True)
    shifted = values - centre
    row_scale = lax.rsqrt(jnp.mean(shifted * shifted, axis=-1, keepdims=True) + NORM_EPS)
    return (shifted * row_scale, row_scale)


def norm_back(grad_norm, normed, row_scale, gain_row):
    grad_hat = grad_norm * gain_row
    centred = grad_hat - jnp.mean(grad_hat, axis=-1, keepdims=True)
    return row_scale * (centred - normed * jnp.mean(grad_hat * normed, axis=-1, keepdims=True))


def adam_step(weight, moment, squares, gradient, rate_value):
    drift = 0.9 * moment + 0.1 * gradient
    energy = 0.999 * squares + 0.001 * gradient * gradient
    first_hat = drift / (1.0 - 0.9**STEP)
    second_hat = energy / (1.0 - 0.999**STEP)
    after = weight - rate_value * (first_hat / (jnp.sqrt(second_hat) + 1e-08) + 0.1 * weight)
    return (drift, energy, after)


def stacked_heads(rows, factor):
    half = rows.shape[1] // 2
    lane = lax.broadcasted_iota(jnp.int32, rows.shape, 1)
    values = rows.astype(F32) * factor
    first = jnp.where(lane < half, values, 0.0)
    second = jnp.where(lane < half, 0.0, values)
    return jnp.concatenate([first, second], axis=0).astype(BF16)


def unstacked_heads(product, rows):
    half = product.shape[0] // 2
    both = jnp.concatenate([product[:half, :rows], product[half:, rows:]], axis=0)
    return both.T


def key_allowed(first_ref, last_ref, block):
    key = lax.broadcasted_iota(jnp.int32, (SPAN, 2 * QB), 0) + block * QB
    return (key >= first_ref[block : block + 1, :]) & (key < last_ref[block : block + 1, :])


def attend_kernel(scale, q_ref, k_ref, v_ref, first_ref, last_ref, ctx_ref, lse_ref, vt_ref):
    vt_ref[...] = v_ref[...].T
    for block in range(q_ref.shape[0] // QB):
        rows = slice(block * QB, (block + 1) * QB)
        span = slice(block * QB, block * QB + SPAN)
        queries = stacked_heads(q_ref[rows, :], scale)
        scores = lax.dot_general(k_ref[span, :], queries, NT, preferred_element_type=F32)
        scores = jnp.where(key_allowed(first_ref, last_ref, block), scores, MASKED)
        peak = jnp.max(scores, axis=0, keepdims=True)
        expo = jnp.exp(scores - peak)
        total = jnp.sum(expo, axis=0, keepdims=True)
        probs = (expo * (1.0 / total)).astype(BF16)
        mixed = jnp.dot(vt_ref[:, span], probs, preferred_element_type=F32)
        ctx_ref[rows, :] = unstacked_heads(mixed, QB).astype(BF16)
        lse_ref[0, block : block + 1, :] = peak + jnp.log(total)


def attend_back_kernel(
    scale,
    q_ref,
    k_ref,
    v_ref,
    grad_ref,
    first_ref,
    last_ref,
    lse_ref,
    dq_ref,
    dk_ref,
    dv_ref,
    kt_ref,
    dk_sum,
    dv_sum,
):
    kt_ref[...] = k_ref[...].T
    dk_sum[...] = jnp.zeros_like(dk_sum)
    dv_sum[...] = jnp.zeros_like(dv_sum)
    for block in range(q_ref.shape[0] // QB):
        rows = slice(block * QB, (block + 1) * QB)
        span = slice(block * QB, block * QB + SPAN)
        queries = stacked_heads(q_ref[rows, :], scale)
        grads = stacked_heads(grad_ref[rows, :], 1.0)
        scores = lax.dot_general(k_ref[span, :], queries, NT, preferred_element_type=F32)
        scores = jnp.where(key_allowed(first_ref, last_ref, block), scores, MASKED)
        probs = jnp.exp(scores - lse_ref[0, block : block + 1, :])
        prob_grad = lax.dot_general(v_ref[span, :], grads, NT, preferred_element_type=F32)
        mean = jnp.sum(probs * prob_grad, axis=0, keepdims=True)
        score_grad = (probs * (prob_grad - mean)).astype(BF16)
        dv_sum[span, :] += jnp.dot(probs.astype(BF16), grads, preferred_element_type=F32)
        dk_sum[span, :] += jnp.dot(score_grad, queries, preferred_element_type=F32)
        dq = jnp.dot(kt_ref[:, span], score_grad, preferred_element_type=F32)
        dq_ref[rows, :] = (unstacked_heads(dq, QB) * scale).astype(BF16)
    dk_ref[...] = dk_sum[...].astype(BF16)
    dv_ref[...] = dv_sum[...].astype(BF16)


def attend(qkv_rows, kv_window, first_key, last_key, scale):
    rows, width = qkv_rows.shape[0], qkv_rows.shape[1] // 3
    pairs = width // LANES
    window = kv_window.shape[0]
    whole = pl.BlockSpec(first_key.shape, lambda h: (0, 0))
    return pl.pallas_call(
        partial(attend_kernel, scale),
        grid=(pairs,),
        in_specs=[
            pl.BlockSpec((rows, LANES), lambda h: (0, h)),
            pl.BlockSpec((window, LANES), lambda h: (0, h)),
            pl.BlockSpec((window, LANES), lambda h: (0, pairs + h)),
            whole,
            whole,
        ],
        out_specs=[
            pl.BlockSpec((rows, LANES), lambda h: (0, h)),
            pl.BlockSpec((1, 8, 2 * QB), lambda h: (h, 0, 0)),
        ],
        out_shape=[
            jax.ShapeDtypeStruct((rows, width), BF16),
            jax.ShapeDtypeStruct((pairs, 8, 2 * QB), F32),
        ],
        scratch_shapes=[pltpu.VMEM((LANES, window), BF16)],
        compiler_params=pltpu.CompilerParams(vmem_limit_bytes=40 * 2**20),
        cost_estimate=pl.CostEstimate(
            flops=4 * pairs * rows * SPAN * 2 * LANES,
            bytes_accessed=2 * 2 * window * width * 2,
            transcendentals=2 * pairs * rows * SPAN,
        ),
        name="attend",
    )(qkv_rows, kv_window, kv_window, first_key, last_key)


def attend_back(qkv_rows, kv_window, context_grad, first_key, last_key, lse, scale):
    rows, width = context_grad.shape
    pairs = width // LANES
    window = kv_window.shape[0]
    whole = pl.BlockSpec(first_key.shape, lambda h: (0, 0))
    return pl.pallas_call(
        partial(attend_back_kernel, scale),
        grid=(pairs,),
        in_specs=[
            pl.BlockSpec((rows, LANES), lambda h: (0, h)),
            pl.BlockSpec((window, LANES), lambda h: (0, h)),
            pl.BlockSpec((window, LANES), lambda h: (0, pairs + h)),
            pl.BlockSpec((rows, LANES), lambda h: (0, h)),
            whole,
            whole,
            pl.BlockSpec((1, 8, 2 * QB), lambda h: (h, 0, 0)),
        ],
        out_specs=[
            pl.BlockSpec((rows, LANES), lambda h: (0, h)),
            pl.BlockSpec((window, LANES), lambda h: (0, h)),
            pl.BlockSpec((window, LANES), lambda h: (0, h)),
        ],
        out_shape=[
            jax.ShapeDtypeStruct((rows, width), BF16),
            jax.ShapeDtypeStruct((window, width), BF16),
            jax.ShapeDtypeStruct((window, width), BF16),
        ],
        scratch_shapes=[
            pltpu.VMEM((LANES, window), BF16),
            pltpu.VMEM((window, LANES), F32),
            pltpu.VMEM((window, LANES), F32),
        ],
        compiler_params=pltpu.CompilerParams(vmem_limit_bytes=40 * 2**20),
        cost_estimate=pl.CostEstimate(
            flops=10 * pairs * rows * SPAN * 2 * LANES,
            bytes_accessed=4 * 2 * window * width * 2,
            transcendentals=2 * pairs * rows * SPAN,
        ),
        name="attend_back",
    )(qkv_rows, kv_window, kv_window, context_grad, first_key, last_key, lse)


def gelu_both(pre):
    below = 0.5 + 0.5 * lax.erf(pre * (0.5**0.5))
    density = jnp.exp(pre * pre * -0.5) * 0.3989422804014327
    return pre * below, below + pre * density


def expert_kernel(
    rows_ref,
    dy_ref,
    rank_row_ref,
    rank_col_ref,
    gate_row_ref,
    w0_ref,
    w1_ref,
    w2_ref,
    w3_ref,
    y_in_ref,
    s_in_ref,
    y_ref,
    s_ref,
    gate_grad_ref,
    keep_ref,
    give_ref,
    weights,
    arrived,
    x_slots,
    xt_slots,
    g_slots,
    gt_slots,
    dy_slots,
    gate_slots,
    eout,
    xgrad,
):
    step = pl.program_id(0)
    tokens = rows_ref.shape[0]
    slots = x_slots.shape[0]
    sources = (w0_ref, w1_ref, w2_ref, w3_ref)

    def fetch(number):
        return pltpu.make_async_copy(
            sources[number], weights.at[number % 2], arrived.at[number % 2]
        )

    def slot_mask():
        slot = lax.broadcasted_iota(jnp.int32, (slots, tokens), 0)
        return slot == rank_row_ref[...]

    @pl.when(step == 0)
    def _():
        fetch(0).start()
        fetch(1).start()
        mask = slot_mask()
        spots = jnp.where(mask, 1.0, 0.0).astype(BF16)
        x_f32 = jnp.dot(spots, rows_ref[...], preferred_element_type=F32)
        x_slots[...] = x_f32.astype(BF16)
        xt_slots[...] = x_f32.T.astype(BF16)
        dy_f32 = jnp.dot(spots, dy_ref[...], preferred_element_type=F32)
        dy_slots[...] = dy_f32.astype(BF16)
        gate = jnp.sum(jnp.where(mask, gate_row_ref[...], 0.0), axis=1, keepdims=True)
        gate_slots[...] = gate
        g_f32 = dy_f32 * gate
        g_slots[...] = g_f32.astype(BF16)
        gt_slots[...] = g_f32.T.astype(BF16)
        eout[...] = jnp.zeros_like(eout)
        xgrad[...] = jnp.zeros_like(xgrad)

    for number in range(4):

        @pl.when(step == number)
        def _():
            fetch(number).wait()
            if 1 <= number < 3:
                fetch(number + 1).start()

    slot_of = lax.rem(step, 2)
    inner = weights[slot_of, 0]
    outer = weights[slot_of, 1]
    pre = jnp.dot(x_slots[...], inner, preferred_element_type=F32)
    act_grad = jnp.dot(g_slots[...], outer, preferred_element_type=F32)
    act, slope = gelu_both(pre)
    act = act.astype(BF16)
    pre_grad = (act_grad * slope).astype(BF16)
    eout[...] += lax.dot_general(act, outer, NT, preferred_element_type=F32)
    xgrad[...] += lax.dot_general(pre_grad, inner, NT, preferred_element_type=F32)
    inner_grad = jnp.dot(xt_slots[...], pre_grad, preferred_element_type=F32).astype(BF16)
    outer_grad = jnp.dot(gt_slots[...], act, preferred_element_type=F32).astype(BF16)

    @pl.when(step < 2)
    def _():
        keep_ref[0, 0] = inner_grad
        keep_ref[0, 1] = outer_grad

    @pl.when(step >= 2)
    def _():
        give_ref[0, 0] = inner_grad
        give_ref[0, 1] = outer_grad

    @pl.when(step == 3)
    def _():
        out = eout[...]
        slot_grad = jnp.sum(dy_slots[...].astype(F32) * out, axis=1, keepdims=True)
        gate_grad_ref[...] = jnp.sum(jnp.where(slot_mask(), slot_grad, 0.0), axis=0, keepdims=True)
        slot = lax.broadcasted_iota(jnp.int32, (tokens, slots), 1)
        spots = jnp.where(slot == rank_col_ref[...], 1.0, 0.0).astype(BF16)
        scaled = (out * gate_slots[...]).astype(BF16)
        y_ref[...] = y_in_ref[...] + jnp.dot(spots, scaled, preferred_element_type=F32)
        s_ref[...] = s_in_ref[...] + jnp.dot(
            spots, xgrad[...].astype(BF16), preferred_element_type=F32
        )


def expert(rows, dy, rank_row, rank_col, gate_row, quarters, y_sum, s_sum, capacity):
    tokens, width = rows.shape
    hidden = quarters[0].shape[2]
    slots = -(-capacity // LANES) * LANES

    def whole(shape):
        return pl.BlockSpec(shape, lambda i: (0, 0), pipeline_mode=pl.Buffered(1))

    raw = pl.BlockSpec(memory_space=pl.ANY)
    grad_block = (1, 2, width, hidden)
    return pl.pallas_call(
        expert_kernel,
        grid=(4,),
        in_specs=[
            whole((tokens, width)),
            whole((tokens, width)),
            whole((1, tokens)),
            whole((tokens, 1)),
            whole((1, tokens)),
            raw,
            raw,
            raw,
            raw,
            whole((tokens, width)),
            whole((tokens, width)),
        ],
        out_specs=[
            pl.BlockSpec((tokens, width), lambda i: (0, 0)),
            pl.BlockSpec((tokens, width), lambda i: (0, 0)),
            pl.BlockSpec((1, tokens), lambda i: (0, 0)),
            pl.BlockSpec(grad_block, lambda i: (jnp.minimum(i, 1), 0, 0, 0)),
            pl.BlockSpec(grad_block, lambda i: (jnp.maximum(i - 2, 0), 0, 0, 0)),
        ],
        out_shape=[
            jax.ShapeDtypeStruct((tokens, width), F32),
            jax.ShapeDtypeStruct((tokens, width), F32),
            jax.ShapeDtypeStruct((1, tokens), F32),
            jax.ShapeDtypeStruct((2, 2, width, hidden), BF16),
            jax.ShapeDtypeStruct((2, 2, width, hidden), BF16),
        ],
        scratch_shapes=[
            pltpu.VMEM((2, 2, width, hidden), BF16),
            pltpu.SemaphoreType.DMA((2,)),
            pltpu.VMEM((slots, width), BF16),
            pltpu.VMEM((width, slots), BF16),
            pltpu.VMEM((slots, width), BF16),
            pltpu.VMEM((width, slots), BF16),
            pltpu.VMEM((slots, width), BF16),
            pltpu.VMEM((slots, 1), F32),
            pltpu.VMEM((slots, width), F32),
            pltpu.VMEM((slots, width), F32),
        ],
        compiler_params=pltpu.CompilerParams(vmem_limit_bytes=60 * 2**20),
        cost_estimate=pl.CostEstimate(
            flops=6 * 2 * 4 * slots * width * hidden,
            bytes_accessed=16 * 2 * width * hidden * 2,
            transcendentals=4 * 2 * slots * hidden,
        ),
        name="expert",
    )(rows, dy, rank_row, rank_col, gate_row, *quarters, y_sum, s_sum)


def per_device(
    block_input,
    out_grad,
    image_pos,
    routes,
    norm_weight,
    norm_moment,
    norm_squares,
    qkv_weight,
    qkv_moment,
    qkv_squares,
    proj_weight,
    proj_moment,
    proj_squares,
    router_weight,
    router_moment,
    router_squares,
    inner_weight,
    inner_moment,
    inner_squares,
    outer_weight,
    outer_moment,
    outer_squares,
):
    row_count, width = block_input.shape
    capacity = 5 * row_count // 8
    scale = (width // HEADS) ** (-0.5)
    expert_count, _, hidden = inner_weight.shape
    cut = hidden // 4
    replica = lax.axis_index("replica")
    quarter = quarter_of(replica)
    device_pos = lax.axis_index(("replica", "group"))
    all_rows = row_count * lax.axis_size(("replica", "group"))
    first_row = device_pos * row_count

    dense_all = jnp.concatenate([qkv_weight, proj_weight], axis=1)
    dense_cut = lax.dynamic_slice_in_dim(dense_all, quarter * width, width, axis=1)
    small = jnp.concatenate([norm_weight.T, router_weight], axis=1)
    small = jnp.pad(small, ((0, 0), (0, LANES - small.shape[1])))
    dense_piece = jnp.concatenate([dense_cut, small], axis=1).astype(BF16)
    dense_own = lax.all_gather(dense_piece, "group", axis=0, tiled=True)
    outer_turned = outer_weight.transpose(0, 2, 1)
    expert_piece = jnp.stack(
        [
            lax.dynamic_slice_in_dim(inner_weight, quarter * cut, cut, axis=2),
            lax.dynamic_slice_in_dim(outer_turned, quarter * cut, cut, axis=2),
        ],
        axis=1,
    ).astype(BF16)
    expert_quarters = []
    for e in range(expert_count):
        own = lax.all_gather(expert_piece[e], "group", axis=1, tiled=True)
        expert_quarters.append(spread(own))

    dense_blocks = [block[:, :width] for block in spread(dense_own)]
    dense = [pick(dense_blocks, quarter ^ at) for at in range(4)]
    qkv_full = jnp.concatenate(dense[:3], axis=1)
    proj_full = dense[3]
    small_rows = dense_own[:, width : width + 8].T
    norm_full = small_rows[:4].astype(F32)
    router_t = small_rows[4:8]

    x_float = block_input.astype(F32)
    normed_one, scale_one = standardize(x_float)
    first_in = (normed_one * norm_full[0] + norm_full[1]).astype(BF16)
    qkv_rows = jnp.dot(first_in, qkv_full, preferred_element_type=F32).astype(BF16)
    kv_rows = qkv_rows[:, width:]
    below, above = shift(kv_rows[:HALO], kv_rows[row_count - HALO :], ("replica", "group"))
    kv_window = jnp.concatenate([below, kv_rows, above], axis=0)
    row_at = first_row + jnp.arange(row_count, dtype=jnp.int32)
    image_start = row_at - image_pos[:, 0]
    image_end = image_start + image_pos[:, 1]
    first_key = jnp.maximum(image_start, 0) - first_row + HALO
    last_key = jnp.minimum(image_end, all_rows) - first_row + HALO
    first_key = jnp.tile(first_key.reshape(-1, QB), (1, 2))
    last_key = jnp.tile(last_key.reshape(-1, QB), (1, 2))
    context, lse = attend(qkv_rows, kv_window, first_key, last_key, scale)
    residual = x_float + jnp.dot(context, proj_full, preferred_element_type=F32)
    normed_two, scale_two = standardize(residual)
    second_in = (normed_two * norm_full[2] + norm_full[3]).astype(BF16)

    logits = lax.dot_general(router_t, second_in, NT, preferred_element_type=F32)
    logit_expo = jnp.exp(logits - jnp.max(logits, axis=0, keepdims=True))
    gates = logit_expo / jnp.sum(logit_expo, axis=0, keepdims=True)
    names = jnp.arange(expert_count, dtype=jnp.int32)
    named = jnp.any(routes.T[None, :, :] == names[:, None, None], axis=1)
    earlier = jnp.arange(row_count)[:, None] < jnp.arange(row_count)[None, :]
    before = jnp.dot(named.astype(BF16), earlier.astype(BF16), preferred_element_type=F32)
    ranks = jnp.where(named, before.astype(jnp.int32), -1)
    ranks_col = ranks.T

    y_sum, s_sum = residual, jnp.zeros_like(residual)
    gate_grads, expert_owned = [], []
    for e in range(expert_count):
        y_sum, s_sum, gate_grad, keep, give = expert(
            second_in,
            out_grad,
            ranks[e : e + 1],
            ranks_col[:, e : e + 1],
            gates[e : e + 1],
            expert_quarters[e],
            y_sum,
            s_sum,
            capacity,
        )
        gate_grads.append(gate_grad)
        expert_owned.append(reduce_quarter(keep, give, 1))
    block_output = y_sum.astype(BF16)

    prob_grad = jnp.concatenate(gate_grads, axis=0)
    logit_grad = gates * (prob_grad - jnp.sum(gates * prob_grad, axis=0, keepdims=True))
    logit_grad = logit_grad.astype(BF16)
    router_grad = jnp.dot(logit_grad, second_in, preferred_element_type=F32)
    second_grad = s_sum + lax.dot_general(
        logit_grad, router_t, (((0,), (0,)), ((), ())), preferred_element_type=F32
    )
    gain_two_grad = jnp.sum(second_grad * normed_two, axis=0)
    bias_two_grad = jnp.sum(second_grad, axis=0)
    grad_out = out_grad.astype(F32)
    resid_grad = grad_out + norm_back(second_grad, normed_two, scale_two, norm_full[2])
    branch_grad = resid_grad.astype(BF16)
    proj_grad = jnp.dot(context.T, branch_grad, preferred_element_type=F32)
    context_grad = lax.dot_general(branch_grad, proj_full, NT, preferred_element_type=F32)
    context_grad = context_grad.astype(BF16)

    query_grad, key_grad, value_grad = attend_back(
        qkv_rows, kv_window, context_grad, first_key, last_key, lse, scale
    )
    window_grad = jnp.concatenate([key_grad, value_grad], axis=1)
    from_below, from_above = shift(
        window_grad[:HALO], window_grad[HALO + row_count :], ("replica", "group")
    )
    own_grad = window_grad[HALO : HALO + row_count].astype(F32)
    outside = jnp.concatenate(
        [
            from_below,
            jnp.zeros((row_count - 2 * HALO, 2 * width), BF16),
            from_above,
        ],
        axis=0,
    ).astype(F32)
    kv_grad = (own_grad + outside).astype(BF16)
    qkv_grad_rows = jnp.concatenate([query_grad, kv_grad], axis=1)
    qkv_grad = jnp.dot(first_in.T, qkv_grad_rows, preferred_element_type=F32)
    first_grad = lax.dot_general(qkv_grad_rows, qkv_full, NT, preferred_element_type=F32)
    gain_one_grad = jnp.sum(first_grad * normed_one, axis=0)
    bias_one_grad = jnp.sum(first_grad, axis=0)
    input_grad = (resid_grad + norm_back(first_grad, normed_one, scale_one, norm_full[0])).astype(
        BF16
    )

    norm_grad = jnp.stack([gain_one_grad, bias_one_grad, gain_two_grad, bias_two_grad], axis=0)
    small_grad = jnp.concatenate([norm_grad, router_grad], axis=0).T
    small_grad = jnp.pad(small_grad, ((0, 0), (0, LANES - small_grad.shape[1]))).astype(BF16)
    grad_blocks = [qkv_grad[:, i * width : (i + 1) * width].astype(BF16) for i in range(3)]
    grad_blocks.append(proj_grad.astype(BF16))
    grad_stack = jnp.stack(
        [
            jnp.concatenate([block, small_grad if at == 0 else jnp.zeros_like(small_grad)], axis=1)
            for at, block in enumerate(grad_blocks)
        ]
    )
    local = [lax.dynamic_index_in_dim(grad_stack, quarter ^ j, 0) for j in range(4)]
    dense_owned = reduce_quarter(
        jnp.concatenate(local[:2], axis=0), jnp.concatenate(local[2:], axis=0), 0
    )
    dense_parts = spread(dense_owned)
    dense_sum = [pick(dense_parts, quarter ^ at).astype(F32) for at in range(4)]
    expert_parts = spread(jnp.stack(expert_owned))
    expert_sum = jnp.concatenate(
        [pick(expert_parts, quarter ^ at) for at in range(4)], axis=3
    ).astype(F32)

    small_sum = dense_sum[0][:, width : width + 8]
    norm_new = adam_step(norm_weight, norm_moment, norm_squares, small_sum[:, :4].T, RATES[0])
    qkv_sum = jnp.concatenate([part[:, :width] for part in dense_sum[:3]], axis=1)
    qkv_new = adam_step(qkv_weight, qkv_moment, qkv_squares, qkv_sum, RATES[1])
    proj_new = adam_step(
        proj_weight, proj_moment, proj_squares, dense_sum[3][:, :width], RATES[2]
    )
    router_new = adam_step(
        router_weight, router_moment, router_squares, small_sum[:, 4:8], RATES[3]
    )
    inner_new = adam_step(inner_weight, inner_moment, inner_squares, expert_sum[:, 0], RATES[4])
    outer_new = adam_step(
        outer_weight,
        outer_moment,
        outer_squares,
        expert_sum[:, 1].transpose(0, 2, 1),
        RATES[5],
    )
    return (
        block_output,
        input_grad,
        *norm_new,
        *qkv_new,
        *proj_new,
        *router_new,
        *inner_new,
        *outer_new,
    )


def reduce_quarter(keep, give, dim):
    got = swap(give, CORE_BIT)
    mine = (keep[0].astype(F32) + got[0].astype(F32)).astype(BF16)
    theirs = (keep[1].astype(F32) + got[1].astype(F32)).astype(BF16)
    got = swap(theirs, CHIP_BIT)
    mine = (mine.astype(F32) + got.astype(F32)).astype(BF16)
    owned = lax.psum_scatter(mine, "group", scatter_dimension=dim, tiled=True)
    bit = 4
    while bit < lax.axis_size("replica"):
        got = swap(owned, bit)
        owned = (owned.astype(F32) + got.astype(F32)).astype(BF16)
        bit *= 2
    return owned


def solution(mesh):
    tokens = P(("replica", "group"), None)
    columns = P(None, "group")
    rows = P("group", None)
    inner = P(None, "group", None)
    outer = P(None, None, "group")
    weights = (columns,) * 3 + (rows,) * 9 + (inner,) * 3 + (outer,) * 3
    return jax.shard_map(
        per_device,
        mesh=mesh,
        in_specs=(tokens,) * 4 + weights,
        out_specs=(tokens,) * 2 + weights,
        check_vma=False,
    )
```

time: 2180 us -> 980 us (0.45)
  waiting for transfers between devices: 1460 us -> 589 us
  matrix products: 275 us -> 24.3 us
  Pallas kernels: 0 us -> 159 us
  other arithmetic: 207 us -> 85 us
  local copies, waits for them, and re-layouts: 163 us -> 54.9 us
  blocking collectives: 40.6 us -> 0 us
  starting transfers between devices: 12.9 us -> 42.3 us
    reduce_scatter x4, waiting for transfers between devices: 679 us -> 103 us  [reduce_quarter(): owned = lax.psum_scatter(mine, 'group', scatter_dimension=dim, tiled=True)]
    all_gather x4 -> x5, waiting for transfers between devices: 561 us -> 160 us  [the longest x4 123 us: per_device(): own = lax.all_gather(expert_piece[e], 'group', axis=1, tiled=True)]
    ppermute x4 -> x35, waiting for transfers between devices: 7.79 us -> 325 us  [the longest x31 296 us: swap(): return lax.ppermute(block, 'replica', [(r, r ^ bit) for r in range(count)])]
    dot_general x21 -> x10, matrix products: 275 us -> 24.3 us  [the longest x1 5.27 us: per_device(): lax.dot_general(qkv_grad_rows, qkv_full, NT, preferred_element_type=F32)]
    pallas_call x0 -> x6, Pallas kernels: none -> 159 us  [the longest x4 109 us: expert(): pl.pallas_call(expert_kernel, grid=(4,), in_specs=[whole((tokens, width))...]
    unnamed x13 -> x11, waiting for transfers between devices: 115 us -> 1.35 us
    psum x1 -> x0, waiting for transfers between devices: 96.6 us -> none  [per_device(): lax.psum(summed[1].astype(jnp.bfloat16), 'replica').astype(jnp.float32)]
    convert_element_type x10 -> x16, other arithmetic: 108 us -> 41 us  [the longest x5 21.5 us: reduce_quarter(): mine = (mine.astype(F32) + got.astype(F32)).astype(BF16)]
  transfers between devices with their start and end apart: 15 -> 45, of which waited for: 11 -> 18; matrix products, arithmetic and copies ran while one was open for 16% -> 12% of each run, Pallas kernels for 0% -> 11%
where the time goes in v1:
time: 980 us; the launch traced here: 971 us
  waiting for transfers between devices  589 us (60%)
  Pallas kernels  159 us (16%)
  other arithmetic  85 us (9%)
  local copies, waits for them, and re-layouts  54.9 us (6%)
  starting transfers between devices  42.3 us (4%)
  matrix products  24.3 us (2%)
  between operations  15.7 us (2%)
    ppermute x31, waiting for transfers between devices, swap(): return lax.ppermute(block, 'replica', [(r, r ^ bit) for r in range(count)])  296 us
    all_gather x4, waiting for transfers between devices, per_device(): own = lax.all_gather(expert_piece[e], 'group', axis=1, tiled=True)  123 us
    pallas_call x4, Pallas kernels, expert(): pl.pallas_call(expert_kernel, grid=(4,), in_specs=[whole((tokens, width))...  109 us
    reduce_scatter x4, waiting for transfers between devices, reduce_quarter(): owned = lax.psum_scatter(mine, 'group', scatter_dimension=dim, tiled=True)  103 us
    all_gather x1, waiting for transfers between devices, per_device(): dense_own = lax.all_gather(dense_piece, 'group', axis=0, tiled=True)  36.3 us
    ppermute x31, starting transfers between devices, swap(): return lax.ppermute(block, 'replica', [(r, r ^ bit) for r in range(count)])  30 us
    unnamed x162, local copies, waits for them, and re-layouts  29.3 us
    ppermute x4, waiting for transfers between devices, shift(): return (lax.ppermute(tail, axes, up), lax.ppermute(head, axes, down))  29 us
  transfers between devices with their start and end apart: 45, of which 18 were waited for; matrix products, arithmetic and copies ran while one was open for 12% of the time, Pallas kernels for 11%

profile of v1, /device:TPU:23, one launch (start us, length us, event | category | flops | bytes accessed | tf_op | source)
XLA Modules:
  0.0 970.7 jit_solution(3575131928660863235)
XLA Ops:
  15.8 36.3 %all-gather.10.cloned.1.call-done = bf16[768,896]{1,0:T(8,128)(2,1)} async-done(((bf16[96,896]{1,0:T(8,128)(2,1)}), bf16[768,896]{1,0:T(8,128)(2,1)}) %all-gather.10.cloned.1.call-update) | async-done | bytes 1376272 | tf_op jit(solution)/shard_map/all_gather | solution.py:439
  56.7 26.2 %collective-permute-done = bf16[768,896]{1,0:T(8,128)(2,1)} collective-permute-done((bf16[768,896]{1,0:T(8,128)(2,1)}, bf16[768,896]{1,0:T(8,128)(2,1)}, u32[]{:S(2)}, u32[]{:S(2)}) %collective-permute-start) | collective-permute-done | bytes 1376288 | tf_op jit(solution)/shard_map/ppermute | solution.py:29
  90.7 14.7 %all-gather.18.cloned.1.call-done = bf16[1,2,768,768]{3,2,1,0:T(8,128)(2,1)} async-done(((bf16[1,2,96,768]{3,2,1,0:T(8,128)(2,1)}), bf16[1,2,768,768]{3,2,1,0:T(8,128)(2,1)}) %all-gather.18.cloned.1.call-update) | async-done | bytes 2359312 | tf_op jit(solution)/shard_map/all_gather | solution.py:450
  125.4 50.2 %all-gather.16.cloned.1.call-done = bf16[1,2,768,768]{3,2,1,0:T(8,128)(2,1)} async-done(((bf16[1,2,96,768]{3,2,1,0:T(8,128)(2,1)}), bf16[1,2,768,768]{3,2,1,0:T(8,128)(2,1)}) %all-gather.16.cloned.1.call-update) | async-done | bytes 2359312 | tf_op jit(solution)/shard_map/all_gather | solution.py:450
  190.9 39.6 %all-gather.14.cloned.1.call-done = bf16[1,2,768,768]{3,2,1,0:T(8,128)(2,1)} async-done(((bf16[1,2,96,768]{3,2,1,0:T(8,128)(2,1)}), bf16[1,2,768,768]{3,2,1,0:T(8,128)(2,1)}) %all-gather.14.cloned.1.call-update) | async-done | bytes 2359312 | tf_op jit(solution)/shard_map/all_gather | solution.py:450
  234.7 24.9 %attend.1 = (bf16[768,768]{1,0:T(8,128)(2,1)S(1)}, f32[6,8,256]{2,1,0:T(8,128)S(1)}) custom-call(bf16[768,2304]{1,0:T(8,128)(2,1)S(1)} %convolution_convert_fusion.1.q_ref, bf16[1280,1536]{1,0:T(8,128)(2,1)S(1)} %pad_maximum_fusion.3.k_ref.v_ref, bf16[1280,1536]{1,0:T(8,128)(2,1)S(1)} %pad_maximum_fusion.3.k_ref.v_ref, s32[6,256]{1,0:T(8,128)S(1)} %bitcast.168, ...), custom_call_target="tpu_custom_call" | custom-call | flops 3019898880 | bytes 7864320 | tf_op jit(solution)/shard_map/attend/pallas_call | solution.py:154
  265.0 18.9 %all-gather.12.cloned.1.call-done = bf16[1,2,768,768]{3,2,1,0:T(8,128)(2,1)} async-done(((bf16[1,2,96,768]{3,2,1,0:T(8,128)(2,1)}), bf16[1,2,768,768]{3,2,1,0:T(8,128)(2,1)}) %all-gather.12.cloned.1.call-update) | async-done | bytes 2359312 | tf_op jit(solution)/shard_map/all_gather | solution.py:450
  292.0 27.2 %expert.4 = (f32[768,768]{1,0:T(8,128)}, f32[768,768]{1,0:T(8,128)}, f32[1,768]{1,0:T(1,128)}, bf16[2,2,768,768]{3,2,1,0:T(8,128)(2,1)}, bf16[2,2,768,768]{3,2,1,0:T(8,128)(2,1)}) custom-call(bf16[768,768]{1,0:T(8,128)(2,1)} %copy-done.9, bf16[768,768]{1,0:T(8,128)(2,1)} %dy_ref.7, s32[1,768]{1,0:T(1,128)} %copy.243.rank_row_ref, ...), custom_call_target="tpu_custom_call" | custom-call | flops 14495514624 | bytes 37748736 | tf_op jit(solution)/shard_map/expert/pallas_call | solution.py:347
  319.4 16.5 %collective-permute-done.5.w1_ref = bf16[2,768,768]{2,1,0:T(8,128)(2,1)} collective-permute-done((bf16[2,768,768]{2,1,0:T(8,128)(2,1)}, bf16[2,768,768]{2,1,0:T(8,128)(2,1)}, u32[]{:S(2)}, u32[]{:S(2)}) %collective-permute-start.5) | collective-permute-done | bytes 2359328 | tf_op jit(solution)/shard_map/ppermute | solution.py:29
  337.9 27.2 %expert.5 = (f32[768,768]{1,0:T(8,128)}, f32[768,768]{1,0:T(8,128)}, f32[1,768]{1,0:T(1,128)}, bf16[2,2,768,768]{3,2,1,0:T(8,128)(2,1)}, bf16[2,2,768,768]{3,2,1,0:T(8,128)(2,1)}) custom-call(bf16[768,768]{1,0:T(8,128)(2,1)} %copy-done.9, bf16[768,768]{1,0:T(8,128)(2,1)} %dy_ref.7, s32[1,768]{1,0:T(1,128)} %copy.242.rank_row_ref, ...), custom_call_target="tpu_custom_call" | custom-call | flops 14495514624 | bytes 37748736 | tf_op jit(solution)/shard_map/expert/pallas_call | solution.py:347
  365.2 27.5 %expert.6 = (f32[768,768]{1,0:T(8,128)}, f32[768,768]{1,0:T(8,128)}, f32[1,768]{1,0:T(1,128)}, bf16[2,2,768,768]{3,2,1,0:T(8,128)(2,1)}, bf16[2,2,768,768]{3,2,1,0:T(8,128)(2,1)}) custom-call(bf16[768,768]{1,0:T(8,128)(2,1)} %copy-done.9, bf16[768,768]{1,0:T(8,128)(2,1)} %dy_ref.7, s32[1,768]{1,0:T(1,128)} %copy.241.rank_row_ref, ...), custom_call_target="tpu_custom_call" | custom-call | flops 14495514624 | bytes 37748736 | tf_op jit(solution)/shard_map/expert/pallas_call | solution.py:347
  392.7 27.1 %expert.7 = (f32[768,768]{1,0:T(8,128)}, f32[768,768]{1,0:T(8,128)}, f32[1,768]{1,0:T(1,128)}, bf16[2,2,768,768]{3,2,1,0:T(8,128)(2,1)}, bf16[2,2,768,768]{3,2,1,0:T(8,128)(2,1)}) custom-call(bf16[768,768]{1,0:T(8,128)(2,1)} %copy-done.9, bf16[768,768]{1,0:T(8,128)(2,1)} %dy_ref.7, s32[1,768]{1,0:T(1,128)} %copy.240.rank_row_ref, ...), custom_call_target="tpu_custom_call" | custom-call | flops 14495514624 | bytes 37748736 | tf_op jit(solution)/shard_map/expert/pallas_call | solution.py:347
  429.6 25.0 %attend_back.1 = (bf16[768,768]{1,0:T(8,128)(2,1)S(1)}, bf16[1280,768]{1,0:T(8,128)(2,1)S(1)}, bf16[1280,768]{1,0:T(8,128)(2,1)S(1)}) custom-call(bf16[768,2304]{1,0:T(8,128)(2,1)S(1)} %convolution_convert_fusion.1.q_ref, bf16[1280,1536]{1,0:T(8,128)(2,1)S(1)} %copy-done.1, bf16[1280,1536]{1,0:T(8,128)(2,1)S(1)} %copy-done.1, ...), custom_call_target="tpu_custom_call" | custom-call | flops 7549747200 | bytes 15728640 | tf_op jit(solution)/shard_map/attend_back/pallas_call | solution.py:188
  464.3 28.7 %collective-permute-done.17 = bf16[256,1536]{1,0:T(8,128)(2,1)S(1)} collective-permute-done((bf16[256,1536]{1,0:T(8,128)(2,1)S(1)}, bf16[256,1536]{1,0:T(8,128)(2,1)S(1)}, u32[]{:S(2)}, u32[]{:S(2)}) %collective-permute-start.17) | collective-permute-done | bytes 786464 | tf_op jit(solution)/shard_map/ppermute | solution.py:49
  494.0 5.3 fusion.21
  499.3 5.1 convolution_convert_fusion
  509.3 4.7 collective-permute-done.19
  518.8 27.0 %collective-permute-done.20 = bf16[768,896]{1,0:T(8,128)(2,1)S(1)} collective-permute-done((bf16[768,896]{1,0:T(8,128)(2,1)S(1)}, bf16[768,896]{1,0:T(8,128)(2,1)S(1)}, u32[]{:S(2)}, u32[]{:S(2)}) %collective-permute-start.20) | collective-permute-done | bytes 1376288 | tf_op jit(solution)/shard_map/ppermute | solution.py:29
  547.7 48.8 %collective-permute-done.25 = bf16[2,768,768]{2,1,0:T(8,128)(2,1)} collective-permute-done((bf16[2,768,768]{2,1,0:T(8,128)(2,1)S(1)}, bf16[2,768,768]{2,1,0:T(8,128)(2,1)}, u32[]{:S(2)}, u32[]{:S(2)}) %collective-permute-start.25) | collective-permute-done | bytes 2359328 | tf_op jit(solution)/shard_map/ppermute | solution.py:29
  596.5 5.3 fusion.5
  606.4 52.7 %collective-permute-done.27 = bf16[2,768,768]{2,1,0:T(8,128)(2,1)S(1)} collective-permute-done((bf16[2,768,768]{2,1,0:T(8,128)(2,1)S(1)}, bf16[2,768,768]{2,1,0:T(8,128)(2,1)S(1)}, u32[]{:S(2)}, u32[]{:S(2)}) %collective-permute-start.27) | collective-permute-done | bytes 2359328 | tf_op jit(solution)/shard_map/ppermute | solution.py:29
  659.1 4.8 fusion.4
  668.0 52.6 %collective-permute-done.29 = bf16[2,768,768]{2,1,0:T(8,128)(2,1)S(1)} collective-permute-done((bf16[2,768,768]{2,1,0:T(8,128)(2,1)S(1)}, bf16[2,768,768]{2,1,0:T(8,128)(2,1)S(1)}, u32[]{:S(2)}, u32[]{:S(2)}) %collective-permute-start.29) | collective-permute-done | bytes 2359328 | tf_op jit(solution)/shard_map/ppermute | solution.py:29
  720.6 4.8 fusion.3
  728.9 51.7 %collective-permute-done.31 = bf16[2,768,768]{2,1,0:T(8,128)(2,1)S(1)} collective-permute-done((bf16[2,768,768]{2,1,0:T(8,128)(2,1)S(1)}, bf16[2,768,768]{2,1,0:T(8,128)(2,1)S(1)}, u32[]{:S(2)}, u32[]{:S(2)}) %collective-permute-start.31) | collective-permute-done | bytes 2359328 | tf_op jit(solution)/shard_map/ppermute | solution.py:29
  780.6 4.9 fusion.2
  796.7 31.4 %reduce-scatter.12.cloned.1.call-done = bf16[2,96,768]{2,1,0:T(8,128)(2,1)} async-done(((bf16[2,768,768]{2,1,0:T(8,128)(2,1)}), bf16[2,96,768]{2,1,0:T(8,128)(2,1)}) %reduce-scatter.12.cloned.1.call-update) | async-done | bytes 294928 | tf_op jit(solution)/shard_map/reduce_scatter | solution.py:608
  828.0 72.0 %reduce-scatter.14.cloned.1.call-done = bf16[2,96,768]{2,1,0:T(8,128)(2,1)} async-done(((bf16[2,768,768]{2,1,0:T(8,128)(2,1)}), bf16[2,96,768]{2,1,0:T(8,128)(2,1)}) %reduce-scatter.14.cloned.1.call-update) | async-done | bytes 294928 | tf_op jit(solution)/shard_map/reduce_scatter | solution.py:608
  912.1 15.8 %collective-permute-done.32 = bf16[4,2,96,768]{3,2,1,0:T(8,128)(2,1)} collective-permute-done((bf16[4,2,96,768]{3,2,1,0:T(8,128)(2,1)}, bf16[4,2,96,768]{3,2,1,0:T(8,128)(2,1)}, u32[]{:S(2)}, u32[]{:S(2)}) %collective-permute-start.32) | collective-permute-done | bytes 1179680 | tf_op jit(solution)/shard_map/ppermute | solution.py:29
  927.9 3.7 collective-permute-start.34
  946.4 8.4 multiply_subtract_fusion
  954.8 8.9 multiply_subtract_fusion.1
  (342 shorter events, 157.0 us)
Async XLA Ops:
  10.5 94.9 %all-gather.18.cloned.1.call-start = ((), (), s32[]{:S(2)}) async-start(), calls=%async_computation.13 | async-start | bytes 2654208 | tf_op jit(solution)/shard_map/all_gather | solution.py:450
  14.4 161.2 %all-gather.16.cloned.1.call-start = ((), (), s32[]{:S(2)}) async-start(), calls=%async_computation.12 | async-start | bytes 2654208 | tf_op jit(solution)/shard_map/all_gather | solution.py:450
  15.1 215.3 %all-gather.14.cloned.1.call-start = ((), (), s32[]{:S(2)}) async-start(), calls=%async_computation.11 | async-start | bytes 2654208 | tf_op jit(solution)/shard_map/all_gather | solution.py:450
  15.7 268.2 %all-gather.12.cloned.1.call-start = ((), (), s32[]{:S(2)}) async-start(), calls=%async_computation.10 | async-start | bytes 2654208 | tf_op jit(solution)/shard_map/all_gather | solution.py:450
  52.3 742.1 %reduce-scatter.16.cloned.1.call-start = ((), (), s32[]{:S(2)}) async-start(), calls=%async_computation.14 | async-start | bytes 1548288
  105.4 127.8 %collective-permute-start.14 = (bf16[2,768,768]{2,1,0:T(8,128)(2,1)}, bf16[2,768,768]{2,1,0:T(8,128)(2,1)}, u32[]{:S(2)}, u32[]{:S(2)}) collective-permute-start(bf16[2,768,768]{2,1,0:T(8,128)(2,1)} %bitcast.18.w0_ref), channel_id=1, source_target_pairs={{0,16},{8,24},{16,0},{24,8},{1,17},{9,25},{17,1},{25,9},{2,18},{10... | collective-permute-start | bytes 7077896 | tf_op jit(solution)/shard_map/ppermute | solution.py:29
  114.4 75.0 %collective-permute-start.3 = (bf16[256,1536]{1,0:T(8,128)(2,1)}, bf16[256,1536]{1,0:T(8,128)(2,1)}, u32[]{:S(2)}, u32[]{:S(2)}) collective-permute-start(bf16[256,1536]{1,0:T(8,128)(2,1)} %get-tuple-element.257), channel_id=1, source_target_pairs={{0,1},{1,2},{2,3},{3,4},{4,5},{5,6},{6,7},{7,8},{8,9},{9,10},{10,1... | collective-permute-start | bytes 2359304 | tf_op jit(solution)/shard_map/ppermute | solution.py:49
  118.1 112.3 %collective-permute-start.4 = (bf16[256,1536]{1,0:T(8,128)(2,1)}, bf16[256,1536]{1,0:T(8,128)(2,1)}, u32[]{:S(2)}, u32[]{:S(2)}) collective-permute-start(bf16[256,1536]{1,0:T(8,128)(2,1)} %get-tuple-element.258), channel_id=1, source_target_pairs={{1,0},{2,1},{3,2},{4,3},{5,4},{6,5},{7,6},{8,7},{9,8},{10,9},{11,1... | collective-permute-start | bytes 2359304 | tf_op jit(solution)/shard_map/ppermute | solution.py:49
  123.5 160.4 %collective-permute-start.15 = (bf16[2,768,768]{2,1,0:T(8,128)(2,1)}, bf16[2,768,768]{2,1,0:T(8,128)(2,1)}, u32[]{:S(2)}, u32[]{:S(2)}) collective-permute-start(bf16[2,768,768]{2,1,0:T(8,128)(2,1)} %bitcast.18.w0_ref), channel_id=1, source_target_pairs={{0,8},{8,0},{16,24},{24,16},{1,9},{9,1},{17,25},{25,17},{2,10},{10... | collective-permute-start | bytes 7077896 | tf_op jit(solution)/shard_map/ppermute | solution.py:29
  175.6 108.6 %collective-permute-start.11 = (bf16[2,768,768]{2,1,0:T(8,128)(2,1)}, bf16[2,768,768]{2,1,0:T(8,128)(2,1)}, u32[]{:S(2)}, u32[]{:S(2)}) collective-permute-start(bf16[2,768,768]{2,1,0:T(8,128)(2,1)} %bitcast.17.w0_ref), channel_id=1, source_target_pairs={{0,16},{8,24},{16,0},{24,8},{1,17},{9,25},{17,1},{25,9},{2,18},{10... | collective-permute-start | bytes 7077896 | tf_op jit(solution)/shard_map/ppermute | solution.py:29
  189.5 129.8 %collective-permute-start.12 = (bf16[2,768,768]{2,1,0:T(8,128)(2,1)}, bf16[2,768,768]{2,1,0:T(8,128)(2,1)}, u32[]{:S(2)}, u32[]{:S(2)}) collective-permute-start(bf16[2,768,768]{2,1,0:T(8,128)(2,1)} %bitcast.17.w0_ref), channel_id=1, source_target_pairs={{0,8},{8,0},{16,24},{24,16},{1,9},{9,1},{17,25},{25,17},{2,10},{10... | collective-permute-start | bytes 7077896 | tf_op jit(solution)/shard_map/ppermute | solution.py:29
  230.4 59.6 %collective-permute-start.8 = (bf16[2,768,768]{2,1,0:T(8,128)(2,1)}, bf16[2,768,768]{2,1,0:T(8,128)(2,1)}, u32[]{:S(2)}, u32[]{:S(2)}) collective-permute-start(bf16[2,768,768]{2,1,0:T(8,128)(2,1)} %bitcast.16.w0_ref), channel_id=1, source_target_pairs={{0,16},{8,24},{16,0},{24,8},{1,17},{9,25},{17,1},{25,9},{2,18},{10... | collective-permute-start | bytes 7077896 | tf_op jit(solution)/shard_map/ppermute | solution.py:29
  233.2 56.8 %collective-permute-start.16 = (bf16[2,768,768]{2,1,0:T(8,128)(2,1)}, bf16[2,768,768]{2,1,0:T(8,128)(2,1)}, u32[]{:S(2)}, u32[]{:S(2)}) collective-permute-start(bf16[2,768,768]{2,1,0:T(8,128)(2,1)} %collective-permute-done.14.w1_ref), channel_id=1, source_target_pairs={{0,8},{8,0},{16,24},{24,16},{1,9},{9,1},{17,25},{25,17},{2,10},{10... | collective-permute-start | bytes 7077896 | tf_op jit(solution)/shard_map/ppermute | solution.py:29
  283.9 51.9 %collective-permute-start.5 = (bf16[2,768,768]{2,1,0:T(8,128)(2,1)}, bf16[2,768,768]{2,1,0:T(8,128)(2,1)}, u32[]{:S(2)}, u32[]{:S(2)}) collective-permute-start(bf16[2,768,768]{2,1,0:T(8,128)(2,1)} %bitcast.189), channel_id=1, source_target_pairs={{0,16},{8,24},{16,0},{24,8},{1,17},{9,25},{17,1},{25,9},{2,18},{10... | collective-permute-start | bytes 7077896 | tf_op jit(solution)/shard_map/ppermute | solution.py:29
  284.2 53.7 %collective-permute-start.13 = (bf16[2,768,768]{2,1,0:T(8,128)(2,1)}, bf16[2,768,768]{2,1,0:T(8,128)(2,1)}, u32[]{:S(2)}, u32[]{:S(2)}) collective-permute-start(bf16[2,768,768]{2,1,0:T(8,128)(2,1)} %collective-permute-done.11.w1_ref), channel_id=1, source_target_pairs={{0,8},{8,0},{16,24},{24,16},{1,9},{9,1},{17,25},{25,17},{2,10},{10... | collective-permute-start | bytes 7077896 | tf_op jit(solution)/shard_map/ppermute | solution.py:29
  290.0 75.2 %collective-permute-start.9 = (bf16[2,768,768]{2,1,0:T(8,128)(2,1)}, bf16[2,768,768]{2,1,0:T(8,128)(2,1)}, u32[]{:S(2)}, u32[]{:S(2)}) collective-permute-start(bf16[2,768,768]{2,1,0:T(8,128)(2,1)} %bitcast.16.w0_ref), channel_id=1, source_target_pairs={{0,8},{8,0},{16,24},{24,16},{1,9},{9,1},{17,25},{25,17},{2,10},{10... | collective-permute-start | bytes 7077896 | tf_op jit(solution)/shard_map/ppermute | solution.py:29
  290.0 75.2 %collective-permute-start.10 = (bf16[2,768,768]{2,1,0:T(8,128)(2,1)}, bf16[2,768,768]{2,1,0:T(8,128)(2,1)}, u32[]{:S(2)}, u32[]{:S(2)}) collective-permute-start(bf16[2,768,768]{2,1,0:T(8,128)(2,1)} %collective-permute-done.8.w1_ref), channel_id=1, source_target_pairs={{0,8},{8,0},{16,24},{24,16},{1,9},{9,1},{17,25},{25,17},{2,10},{10... | collective-permute-start | bytes 7077896 | tf_op jit(solution)/shard_map/ppermute | solution.py:29
  319.2 73.4 %collective-permute-start.6 = (bf16[2,768,768]{2,1,0:T(8,128)(2,1)}, bf16[2,768,768]{2,1,0:T(8,128)(2,1)}, u32[]{:S(2)}, u32[]{:S(2)}) collective-permute-start(bf16[2,768,768]{2,1,0:T(8,128)(2,1)} %bitcast.190), channel_id=1, source_target_pairs={{0,8},{8,0},{16,24},{24,16},{1,9},{9,1},{17,25},{25,17},{2,10},{10... | collective-permute-start | bytes 7077896 | tf_op jit(solution)/shard_map/ppermute | solution.py:29
  335.8 56.8 %collective-permute-start.7 = (bf16[2,768,768]{2,1,0:T(8,128)(2,1)}, bf16[2,768,768]{2,1,0:T(8,128)(2,1)}, u32[]{:S(2)}, u32[]{:S(2)}) collective-permute-start(bf16[2,768,768]{2,1,0:T(8,128)(2,1)} %collective-permute-done.5.w1_ref), channel_id=1, source_target_pairs={{0,8},{8,0},{16,24},{24,16},{1,9},{9,1},{17,25},{25,17},{2,10},{10... | collective-permute-start | bytes 7077896 | tf_op jit(solution)/shard_map/ppermute | solution.py:29
  461.0 54.3 %collective-permute-start.24 = (bf16[2,2,768,768]{3,2,1,0:T(8,128)(2,1)}, bf16[2,2,768,768]{3,2,1,0:T(8,128)(2,1)}, u32[]{:S(2)}, u32[]{:S(2)}) collective-permute-start(bf16[2,2,768,768]{3,2,1,0:T(8,128)(2,1)} %get-tuple-element.63), channel_id=1, source_target_pairs={{0,8},{8,0},{16,24},{24,16},{1,9},{9,1},{17,25},{25,17},{2,10},{10... | collective-permute-start | bytes 14155784 | tf_op jit(solution)/shard_map/ppermute | solution.py:29
  514.7 88.5 %collective-permute-start.26 = (bf16[2,2,768,768]{3,2,1,0:T(8,128)(2,1)}, bf16[2,2,768,768]{3,2,1,0:T(8,128)(2,1)}, u32[]{:S(2)}, u32[]{:S(2)}) collective-permute-start(bf16[2,2,768,768]{3,2,1,0:T(8,128)(2,1)} %get-tuple-element.65), channel_id=1, source_target_pairs={{0,8},{8,0},{16,24},{24,16},{1,9},{9,1},{17,25},{25,17},{2,10},{10... | collective-permute-start | bytes 14155784 | tf_op jit(solution)/shard_map/ppermute | solution.py:29
  517.6 78.9 %collective-permute-start.25 = (bf16[2,768,768]{2,1,0:T(8,128)(2,1)S(1)}, bf16[2,768,768]{2,1,0:T(8,128)(2,1)}, u32[]{:S(2)}, u32[]{:S(2)}) collective-permute-start(bf16[2,768,768]{2,1,0:T(8,128)(2,1)S(1)} %fusion.24), channel_id=1, source_target_pairs={{0,16},{8,24},{16,0},{24,8},{1,17},{9,25},{17,1},{25,9},{2,18},{10... | collective-permute-start | bytes 7077896 | tf_op jit(solution)/shard_map/ppermute | solution.py:29
  547.4 249.2 %reduce-scatter.8.cloned.1.call-start = ((), (), s32[]{:S(2)}) async-start(), calls=%async_computation.6 | async-start | bytes 2654208 | tf_op jit(solution)/shard_map/reduce_scatter | solution.py:608
  601.8 194.8 %reduce-scatter.10.cloned.1.call-start = ((), (), s32[]{:S(2)}) async-start(), calls=%async_computation.7 | async-start | bytes 2654208 | tf_op jit(solution)/shard_map/reduce_scatter | solution.py:608
  601.9 62.9 %collective-permute-start.28 = (bf16[2,2,768,768]{3,2,1,0:T(8,128)(2,1)}, bf16[2,2,768,768]{3,2,1,0:T(8,128)(2,1)}, u32[]{:S(2)}, u32[]{:S(2)}) collective-permute-start(bf16[2,2,768,768]{3,2,1,0:T(8,128)(2,1)} %get-tuple-element.67), channel_id=1, source_target_pairs={{0,8},{8,0},{16,24},{24,16},{1,9},{9,1},{17,25},{25,17},{2,10},{10... | collective-permute-start | bytes 14155784 | tf_op jit(solution)/shard_map/ppermute | solution.py:29
  606.1 53.0 %collective-permute-start.27 = (bf16[2,768,768]{2,1,0:T(8,128)(2,1)S(1)}, bf16[2,768,768]{2,1,0:T(8,128)(2,1)S(1)}, u32[]{:S(2)}, u32[]{:S(2)}) collective-permute-start(bf16[2,768,768]{2,1,0:T(8,128)(2,1)S(1)} %fusion.26), channel_id=1, source_target_pairs={{0,16},{8,24},{16,0},{24,8},{1,17},{9,25},{17,1},{25,9},{2,18},{10... | collective-permute-start | bytes 7077896 | tf_op jit(solution)/shard_map/ppermute | solution.py:29
  664.0 164.1 %reduce-scatter.12.cloned.1.call-start = ((), (), s32[]{:S(2)}) async-start(), calls=%async_computation.8 | async-start | bytes 2654208 | tf_op jit(solution)/shard_map/reduce_scatter | solution.py:608
  664.0 61.5 %collective-permute-start.30 = (bf16[2,2,768,768]{3,2,1,0:T(8,128)(2,1)}, bf16[2,2,768,768]{3,2,1,0:T(8,128)(2,1)}, u32[]{:S(2)}, u32[]{:S(2)}) collective-permute-start(bf16[2,2,768,768]{3,2,1,0:T(8,128)(2,1)} %get-tuple-element.69), channel_id=1, source_target_pairs={{0,8},{8,0},{16,24},{24,16},{1,9},{9,1},{17,25},{25,17},{2,10},{10... | collective-permute-start | bytes 14155784 | tf_op jit(solution)/shard_map/ppermute | solution.py:29
  667.7 52.9 %collective-permute-start.29 = (bf16[2,768,768]{2,1,0:T(8,128)(2,1)S(1)}, bf16[2,768,768]{2,1,0:T(8,128)(2,1)S(1)}, u32[]{:S(2)}, u32[]{:S(2)}) collective-permute-start(bf16[2,768,768]{2,1,0:T(8,128)(2,1)S(1)} %fusion.28), channel_id=1, source_target_pairs={{0,16},{8,24},{16,0},{24,8},{1,17},{9,25},{17,1},{25,9},{2,18},{10... | collective-permute-start | bytes 7077896 | tf_op jit(solution)/shard_map/ppermute | solution.py:29
  725.5 174.6 %reduce-scatter.14.cloned.1.call-start = ((), (), s32[]{:S(2)}) async-start(), calls=%async_computation.9 | async-start | bytes 2654208 | tf_op jit(solution)/shard_map/reduce_scatter | solution.py:608
  728.5 52.0 %collective-permute-start.31 = (bf16[2,768,768]{2,1,0:T(8,128)(2,1)S(1)}, bf16[2,768,768]{2,1,0:T(8,128)(2,1)S(1)}, u32[]{:S(2)}, u32[]{:S(2)}) collective-permute-start(bf16[2,768,768]{2,1,0:T(8,128)(2,1)S(1)} %fusion.30), channel_id=1, source_target_pairs={{0,16},{8,24},{16,0},{24,8},{1,17},{9,25},{17,1},{25,9},{2,18},{10... | collective-permute-start | bytes 7077896 | tf_op jit(solution)/shard_map/ppermute | solution.py:29
  796.4 110.0 %collective-permute-start.21 = (bf16[96,896]{0,1:T(8,128)(2,1)}, bf16[96,896]{0,1:T(8,128)(2,1)}, u32[]{:S(2)}, u32[]{:S(2)}) collective-permute-start(bf16[96,896]{0,1:T(8,128)(2,1)} %copy.239), channel_id=1, source_target_pairs={{0,16},{8,24},{16,0},{24,8},{1,17},{9,25},{17,1},{25,9},{2,18},{10... | collective-permute-start | bytes 516104 | tf_op jit(solution)/shard_map/ppermute | solution.py:29
  (86 other events, 1317.6 us)
Sparse Core Ops, SparseCore 0:
  10.8 41.1 all-gather.9
  54.8 50.5 all-gather.17
  108.2 67.4 all-gather.15
  178.2 52.1 all-gather.13
  233.0 50.8 all-gather.11
  547.6 64.6 reduce-scatter.15
  615.8 67.7 reduce-scatter.7
  687.6 68.1 reduce-scatter.9
  760.0 68.0 reduce-scatter.11
  832.0 68.0 reduce-scatter.13

commit v2 on v1

--- a/solution.py
+++ b/solution.py
@@ -21,6 +21,9 @@
 CHIP_BIT = 2
 F32 = jnp.float32
 BF16 = jnp.bfloat16
+EXPERT_COST = pl.CostEstimate(flops=45 * 10**9, bytes_accessed=10**5, transcendentals=0)
+ATTEND_COST = pl.CostEstimate(flops=30 * 10**9, bytes_accessed=10**5, transcendentals=0)
+BACK_COST = pl.CostEstimate(flops=15 * 10**9, bytes_accessed=10**5, transcendentals=0)
 NT = (((1,), (1,)), ((), ()))
 
 
@@ -47,6 +50,114 @@
     up = [(i, i + 1) for i in range(count - 1)]
     down = [(i + 1, i) for i in range(count - 1)]
     return lax.ppermute(tail, axes, up), lax.ppermute(head, axes, down)
+
+
+def group_shape():
+    count = lax.axis_size("group")
+    far = min(4, count)
+    return far, count // far
+
+
+def group_swap(block, flip):
+    count = lax.axis_size("group")
+    return lax.ppermute(block, "group", [(g, g ^ flip) for g in range(count)])
+
+
+def gather_far(piece):
+    far, near = group_shape()
+    return [piece] + [group_swap(piece, k * near) for k in range(1, far)]
+
+
+def gather_near(stack):
+    _, near = group_shape()
+    return [stack] + [group_swap(stack, j) for j in range(1, near)]
+
+
+def summed(parts):
+    return sum(part.astype(F32) for part in parts).astype(BF16)
+
+
+def scatter_near(blocks, *after):
+    far, near = group_shape()
+    place = lax.axis_index("group") % near
+    blocks = blocks.reshape(*blocks.shape[:-3], far, near, *blocks.shape[-2:])
+    axis = blocks.ndim - 3
+    parts = [lax.dynamic_index_in_dim(blocks, place ^ j, axis, keepdims=False) for j in range(near)]
+    mine = tie(parts[0], *after) if after else parts[0]
+    return summed([mine] + [group_swap(parts[j], j) for j in range(1, near)])
+
+
+def scatter_far(blocks, *after):
+    far, near = group_shape()
+    place = lax.axis_index("group") // near
+    axis = blocks.ndim - 3
+    parts = [lax.dynamic_index_in_dim(blocks, place ^ k, axis, keepdims=False) for k in range(far)]
+    mine = tie(parts[0], *after) if after else parts[0]
+    return summed([mine] + [group_swap(parts[k], k * near) for k in range(1, far)])
+
+
+def sum_chips(block, bit):
+    while bit < lax.axis_size("replica"):
+        block = summed([block, swap(block, bit)])
+        bit *= 2
+    return block
+
+
+def halves(own, other, core):
+    return jnp.where(core == 0, own, other), jnp.where(core == 0, other, own)
+
+
+def place_kernel(near, far, rows, cut, place_ref, *refs):
+    own, other = refs[:near], refs[near : 2 * near]
+    full_ref, side_ref, sems = refs[-3:]
+    copies = []
+    for j in range(near):
+        for k in range(far):
+            shard = (place_ref[0] ^ k) * near + (place_ref[1] ^ j)
+            core = place_ref[2]
+            for refs_of, half in ((own, core), (other, 1 - core)):
+                columns = pl.ds(pl.multiple_of(half * cut, LANES), cut)
+                copies.append((refs_of[j].at[k, :, pl.ds(0, cut)], full_ref.at[shard, :, columns]))
+            copies.append((own[j].at[k, :, pl.ds(cut, LANES)], side_ref.at[shard]))
+    copies = [
+        pltpu.make_async_copy(source, target, sems.at[at])
+        for at, (source, target) in enumerate(copies)
+    ]
+    for copy in copies:
+        copy.start()
+    for copy in copies:
+        copy.wait()
+
+
+def place_pieces(own, other, place, after=()):
+    near, far = len(own), own[0].shape[0]
+    rows, cut = own[0].shape[1], own[0].shape[2] - LANES
+    raw = pl.BlockSpec(memory_space=pl.ANY)
+    full, side = pl.pallas_call(
+        partial(place_kernel, near, far, rows, cut),
+        in_specs=[pl.BlockSpec(memory_space=pltpu.SMEM)] + [raw] * (2 * near + len(after)),
+        out_specs=[raw, raw],
+        out_shape=[
+            jax.ShapeDtypeStruct((near * far, rows, 2 * cut), BF16),
+            jax.ShapeDtypeStruct((near * far, rows, LANES), BF16),
+        ],
+        scratch_shapes=[pltpu.SemaphoreType.DMA((3 * near * far,))],
+        name="place_pieces",
+    )(place, *own, *other, *after)
+    return full.reshape(-1, 2 * cut), side.reshape(-1, LANES)
+
+
+def tie(value, *others):
+    raw = pl.BlockSpec(memory_space=pl.ANY)
+    return pl.pallas_call(
+        lambda *refs: None,
+        in_specs=[raw] * (1 + len(others)),
+        out_specs=raw,
+        out_shape=jax.ShapeDtypeStruct(value.shape, value.dtype),
+        input_output_aliases={0: 0},
+        compiler_params=pltpu.CompilerParams(vmem_limit_bytes=56 * 2**20),
+        name="tie",
+    )(value, *others)
 
 
 def standardize(values):
@@ -91,7 +202,8 @@
     return (key >= first_ref[block : block + 1, :]) & (key < last_ref[block : block + 1, :])
 
 
-def attend_kernel(scale, q_ref, k_ref, v_ref, first_ref, last_ref, ctx_ref, lse_ref, vt_ref):
+def attend_kernel(scale, q_ref, k_ref, v_ref, first_ref, last_ref, *refs):
+    ctx_ref, lse_ref, vt_ref = refs[-3:]
     vt_ref[...] = v_ref[...].T
     for block in range(q_ref.shape[0] // QB):
         rows = slice(block * QB, (block + 1) * QB)
@@ -117,13 +229,9 @@
     first_ref,
     last_ref,
     lse_ref,
-    dq_ref,
-    dk_ref,
-    dv_ref,
-    kt_ref,
-    dk_sum,
-    dv_sum,
+    *refs,
 ):
+    dq_ref, dk_ref, dv_ref, kt_ref, dk_sum, dv_sum = refs[-6:]
     kt_ref[...] = k_ref[...].T
     dk_sum[...] = jnp.zeros_like(dk_sum)
     dv_sum[...] = jnp.zeros_like(dv_sum)
@@ -146,7 +254,7 @@
     dv_ref[...] = dv_sum[...].astype(BF16)
 
 
-def attend(qkv_rows, kv_window, first_key, last_key, scale):
+def attend(qkv_rows, kv_window, first_key, last_key, scale, after=()):
     rows, width = qkv_rows.shape[0], qkv_rows.shape[1] // 3
     pairs = width // LANES
     window = kv_window.shape[0]
@@ -160,6 +268,7 @@
             pl.BlockSpec((window, LANES), lambda h: (0, pairs + h)),
             whole,
             whole,
+            *[pl.BlockSpec(memory_space=pl.ANY)] * len(after),
         ],
         out_specs=[
             pl.BlockSpec((rows, LANES), lambda h: (0, h)),
@@ -170,32 +279,30 @@
             jax.ShapeDtypeStruct((pairs, 8, 2 * QB), F32),
         ],
         scratch_shapes=[pltpu.VMEM((LANES, window), BF16)],
-        compiler_params=pltpu.CompilerParams(vmem_limit_bytes=40 * 2**20),
-        cost_estimate=pl.CostEstimate(
-            flops=4 * pairs * rows * SPAN * 2 * LANES,
-            bytes_accessed=2 * 2 * window * width * 2,
-            transcendentals=2 * pairs * rows * SPAN,
-        ),
+        compiler_params=pltpu.CompilerParams(vmem_limit_bytes=56 * 2**20),
+        cost_estimate=ATTEND_COST,
         name="attend",
-    )(qkv_rows, kv_window, kv_window, first_key, last_key)
-
-
-def attend_back(qkv_rows, kv_window, context_grad, first_key, last_key, lse, scale):
+    )(qkv_rows, kv_window, kv_window, first_key, last_key, *after)
+
+
+def attend_back(qkv_rows, kv_window, context_grad, first_key, last_key, lse, scale, heads, after=()):
     rows, width = context_grad.shape
     pairs = width // LANES
+    low, count = heads.start, len(heads)
     window = kv_window.shape[0]
     whole = pl.BlockSpec(first_key.shape, lambda h: (0, 0))
     return pl.pallas_call(
         partial(attend_back_kernel, scale),
-        grid=(pairs,),
+        grid=(count,),
         in_specs=[
-            pl.BlockSpec((rows, LANES), lambda h: (0, h)),
-            pl.BlockSpec((window, LANES), lambda h: (0, h)),
-            pl.BlockSpec((window, LANES), lambda h: (0, pairs + h)),
-            pl.BlockSpec((rows, LANES), lambda h: (0, h)),
+            pl.BlockSpec((rows, LANES), lambda h: (0, low + h)),
+            pl.BlockSpec((window, LANES), lambda h: (0, low + h)),
+            pl.BlockSpec((window, LANES), lambda h: (0, pairs + low + h)),
+            pl.BlockSpec((rows, LANES), lambda h: (0, low + h)),
             whole,
             whole,
-            pl.BlockSpec((1, 8, 2 * QB), lambda h: (h, 0, 0)),
+            pl.BlockSpec((1, 8, 2 * QB), lambda h: (low + h, 0, 0)),
+            *[pl.BlockSpec(memory_space=pl.ANY)] * len(after),
         ],
         out_specs=[
             pl.BlockSpec((rows, LANES), lambda h: (0, h)),
@@ -203,23 +310,19 @@
             pl.BlockSpec((window, LANES), lambda h: (0, h)),
         ],
         out_shape=[
-            jax.ShapeDtypeStruct((rows, width), BF16),
-            jax.ShapeDtypeStruct((window, width), BF16),
-            jax.ShapeDtypeStruct((window, width), BF16),
+            jax.ShapeDtypeStruct((rows, count * LANES), BF16),
+            jax.ShapeDtypeStruct((window, count * LANES), BF16),
+            jax.ShapeDtypeStruct((window, count * LANES), BF16),
         ],
         scratch_shapes=[
             pltpu.VMEM((LANES, window), BF16),
             pltpu.VMEM((window, LANES), F32),
             pltpu.VMEM((window, LANES), F32),
         ],
-        compiler_params=pltpu.CompilerParams(vmem_limit_bytes=40 * 2**20),
-        cost_estimate=pl.CostEstimate(
-            flops=10 * pairs * rows * SPAN * 2 * LANES,
-            bytes_accessed=4 * 2 * window * width * 2,
-            transcendentals=2 * pairs * rows * SPAN,
-        ),
+        compiler_params=pltpu.CompilerParams(vmem_limit_bytes=56 * 2**20),
+        cost_estimate=BACK_COST,
         name="attend_back",
-    )(qkv_rows, kv_window, kv_window, context_grad, first_key, last_key, lse)
+    )(qkv_rows, kv_window, kv_window, context_grad, first_key, last_key, lse, *after)
 
 
 def gelu_both(pre):
@@ -228,43 +331,37 @@
     return pre * below, below + pre * density
 
 
-def expert_kernel(
-    rows_ref,
-    dy_ref,
-    rank_row_ref,
-    rank_col_ref,
-    gate_row_ref,
-    w0_ref,
-    w1_ref,
-    w2_ref,
-    w3_ref,
-    y_in_ref,
-    s_in_ref,
-    y_ref,
-    s_ref,
-    gate_grad_ref,
-    keep_ref,
-    give_ref,
-    weights,
-    arrived,
-    x_slots,
-    xt_slots,
-    g_slots,
-    gt_slots,
-    dy_slots,
-    gate_slots,
-    eout,
-    xgrad,
-):
+def expert_kernel(lists, near, waits, *refs):
+    place_ref, rows_ref, dy_ref, rank_row_ref, rank_col_ref, gate_row_ref, y_in_ref, s_in_ref = refs[:8]
+    source_refs = refs[8 : 8 + lists]
+    outs = refs[8 + lists + waits :]
+    y_ref, s_ref, gate_grad_ref, keep_ref, give_ref, weights, arrived = outs[:7]
+    x_slots, xt_slots, g_slots, gt_slots, dy_slots, gate_slots, eout, xgrad = outs[7:]
     step = pl.program_id(0)
-    tokens = rows_ref.shape[0]
+    tokens, width = rows_ref.shape
     slots = x_slots.shape[0]
-    sources = (w0_ref, w1_ref, w2_ref, w3_ref)
+    hidden = weights.shape[-1]
 
     def fetch(number):
-        return pltpu.make_async_copy(
-            sources[number], weights.at[number % 2], arrived.at[number % 2]
-        )
+        slot = number % 2
+        if near == 0:
+            return [
+                pltpu.make_async_copy(source_refs[number], weights.at[slot], arrived.at[slot, 0])
+            ]
+        copies = []
+        columns = pl.ds(number % 2 * hidden, hidden)
+        for j in range(near):
+            source = source_refs[number // 2 * near + j]
+            for k in range(source.shape[0]):
+                shard = (place_ref[0] ^ k) * near + (place_ref[1] ^ j)
+                copies.append(
+                    pltpu.make_async_copy(
+                        source.at[k, :, :, columns],
+                        weights.at[slot, :, shard],
+                        arrived.at[slot, len(copies)],
+                    )
+                )
+        return copies
 
     def slot_mask():
         slot = lax.broadcasted_iota(jnp.int32, (slots, tokens), 0)
@@ -272,8 +369,8 @@
 
     @pl.when(step == 0)
     def _():
-        fetch(0).start()
-        fetch(1).start()
+        for copy in fetch(0) + fetch(1):
+            copy.start()
         mask = slot_mask()
         spots = jnp.where(mask, 1.0, 0.0).astype(BF16)
         x_f32 = jnp.dot(spots, rows_ref[...], preferred_element_type=F32)
@@ -293,13 +390,15 @@
 
         @pl.when(step == number)
         def _():
-            fetch(number).wait()
+            for copy in fetch(number):
+                copy.wait()
             if 1 <= number < 3:
-                fetch(number + 1).start()
+                for copy in fetch(number + 1):
+                    copy.start()
 
     slot_of = lax.rem(step, 2)
-    inner = weights[slot_of, 0]
-    outer = weights[slot_of, 1]
+    inner = weights[slot_of, 0].reshape(width, hidden)
+    outer = weights[slot_of, 1].reshape(width, hidden)
     pre = jnp.dot(x_slots[...], inner, preferred_element_type=F32)
     act_grad = jnp.dot(g_slots[...], outer, preferred_element_type=F32)
     act, slope = gelu_both(pre)
@@ -334,10 +433,11 @@
         )
 
 
-def expert(rows, dy, rank_row, rank_col, gate_row, quarters, y_sum, s_sum, capacity):
+def expert(place, rows, dy, rank_row, rank_col, gate_row, sources, near, y_sum, s_sum, after=()):
     tokens, width = rows.shape
-    hidden = quarters[0].shape[2]
-    slots = -(-capacity // LANES) * LANES
+    group = lax.axis_size("group")
+    hidden = sources[0].shape[-1] // (2 if near else 1)
+    slots = -(-(5 * tokens // 8) // LANES) * LANES
 
     def whole(shape):
         return pl.BlockSpec(shape, lambda i: (0, 0), pipeline_mode=pl.Buffered(1))
@@ -345,20 +445,18 @@
     raw = pl.BlockSpec(memory_space=pl.ANY)
     grad_block = (1, 2, width, hidden)
     return pl.pallas_call(
-        expert_kernel,
+        partial(expert_kernel, len(sources), near, len(after)),
         grid=(4,),
         in_specs=[
+            pl.BlockSpec(memory_space=pltpu.SMEM),
             whole((tokens, width)),
             whole((tokens, width)),
             whole((1, tokens)),
             whole((tokens, 1)),
             whole((1, tokens)),
-            raw,
-            raw,
-            raw,
-            raw,
             whole((tokens, width)),
             whole((tokens, width)),
+            *[raw] * (len(sources) + len(after)),
         ],
         out_specs=[
             pl.BlockSpec((tokens, width), lambda i: (0, 0)),
@@ -375,8 +473,8 @@
             jax.ShapeDtypeStruct((2, 2, width, hidden), BF16),
         ],
         scratch_shapes=[
-            pltpu.VMEM((2, 2, width, hidden), BF16),
-            pltpu.SemaphoreType.DMA((2,)),
+            pltpu.VMEM((2, 2, group, width // group, hidden), BF16),
+            pltpu.SemaphoreType.DMA((2, group)),
             pltpu.VMEM((slots, width), BF16),
             pltpu.VMEM((width, slots), BF16),
             pltpu.VMEM((slots, width), BF16),
@@ -387,13 +485,9 @@
             pltpu.VMEM((slots, width), F32),
         ],
         compiler_params=pltpu.CompilerParams(vmem_limit_bytes=60 * 2**20),
-        cost_estimate=pl.CostEstimate(
-            flops=6 * 2 * 4 * slots * width * hidden,
-            bytes_accessed=16 * 2 * width * hidden * 2,
-            transcendentals=4 * 2 * slots * hidden,
-        ),
+        cost_estimate=EXPERT_COST,
         name="expert",
-    )(rows, dy, rank_row, rank_col, gate_row, *quarters, y_sum, s_sum)
+    )(place, rows, dy, rank_row, rank_col, gate_row, y_sum, s_sum, *sources, *after)
 
 
 def per_device(
@@ -421,7 +515,6 @@
     outer_squares,
 ):
     row_count, width = block_input.shape
-    capacity = 5 * row_count // 8
     scale = (width // HEADS) ** (-0.5)
     expert_count, _, hidden = inner_weight.shape
     cut = hidden // 4
@@ -431,32 +524,51 @@
     all_rows = row_count * lax.axis_size(("replica", "group"))
     first_row = device_pos * row_count
 
-    dense_all = jnp.concatenate([qkv_weight, proj_weight], axis=1)
-    dense_cut = lax.dynamic_slice_in_dim(dense_all, quarter * width, width, axis=1)
+    far, near = group_shape()
+    core = replica & 1
+    group_at = lax.axis_index("group")
+    place = jnp.stack([group_at // near, group_at % near, core, core]).astype(jnp.int32)
+
+    def dense_gather(matrix, side):
+        cut_to = matrix.shape[1] // 2
+        half = lax.dynamic_slice_in_dim(matrix, core * cut_to, cut_to, axis=1)
+        return gather_far(jnp.concatenate([half, side], axis=1).astype(BF16))
+
+    def dense_place(pieces, after=()):
+        own = gather_near(jnp.stack(pieces))
+        return place_pieces(own, [swap(block, CORE_BIT) for block in own], place, after)
+
     small = jnp.concatenate([norm_weight.T, router_weight], axis=1)
     small = jnp.pad(small, ((0, 0), (0, LANES - small.shape[1])))
-    dense_piece = jnp.concatenate([dense_cut, small], axis=1).astype(BF16)
-    dense_own = lax.all_gather(dense_piece, "group", axis=0, tiled=True)
+    qkv_far = dense_gather(qkv_weight, small)
+    proj_far = dense_gather(proj_weight, jnp.zeros_like(small))
+
     outer_turned = outer_weight.transpose(0, 2, 1)
-    expert_piece = jnp.stack(
-        [
-            lax.dynamic_slice_in_dim(inner_weight, quarter * cut, cut, axis=2),
-            lax.dynamic_slice_in_dim(outer_turned, quarter * cut, cut, axis=2),
-        ],
-        axis=1,
-    ).astype(BF16)
-    expert_quarters = []
-    for e in range(expert_count):
-        own = lax.all_gather(expert_piece[e], "group", axis=1, tiled=True)
-        expert_quarters.append(spread(own))
-
-    dense_blocks = [block[:, :width] for block in spread(dense_own)]
-    dense = [pick(dense_blocks, quarter ^ at) for at in range(4)]
-    qkv_full = jnp.concatenate(dense[:3], axis=1)
-    proj_full = dense[3]
-    small_rows = dense_own[:, width : width + 8].T
+
+    def expert_cut(e, part, count):
+        size = hidden // count
+        return jnp.stack(
+            [
+                lax.dynamic_slice_in_dim(matrix[e], part * size, size, axis=1)
+                for matrix in (inner_weight, outer_turned)
+            ]
+        ).astype(BF16)
+
+    expert_sources, owns = {}, {}
+    group = far * near
+    for e in range(0, expert_count, 2):
+        own = lax.all_gather(expert_cut(e, quarter, 4), "group", axis=1, tiled=True)
+        owns[e] = own
+
+    far_pieces = {}
+    first_far = gather_far(tie(expert_cut(1, core, 2), qkv_far[-1]))
+    qkv_full, small_full = dense_place(qkv_far, (first_far[1], *proj_far[1:]))
+    proj_full, _ = dense_place(proj_far)
+    small_rows = small_full[:, :8].T
     norm_full = small_rows[:4].astype(F32)
     router_t = small_rows[4:8]
+    far_pieces[1] = first_far
+    far_pieces[3] = gather_far(tie(expert_cut(3, core, 2), first_far[-1]))
 
     x_float = block_input.astype(F32)
     normed_one, scale_one = standardize(x_float)
@@ -473,6 +585,15 @@
     first_key = jnp.tile(first_key.reshape(-1, QB), (1, 2))
     last_key = jnp.tile(last_key.reshape(-1, QB), (1, 2))
     context, lse = attend(qkv_rows, kv_window, first_key, last_key, scale)
+    owns[2] = tie(owns[2], context)
+    for e in range(0, expert_count, 2):
+        blocks = spread(owns[e])
+        expert_sources[e] = [block.reshape(2, group, width // group, cut) for block in blocks]
+    far_stacks = {}
+    for e in range(1, expert_count, 2):
+        far_stacks[e] = jnp.stack([tie(far_pieces[e][0], context), *far_pieces[e][1:]])
+        own = gather_near(far_stacks[e])
+        expert_sources[e] = own + [swap(block, CORE_BIT) for block in own]
     residual = x_float + jnp.dot(context, proj_full, preferred_element_type=F32)
     normed_two, scale_two = standardize(residual)
     second_in = (normed_two * norm_full[2] + norm_full[3]).astype(BF16)
@@ -488,21 +609,42 @@
     ranks_col = ranks.T
 
     y_sum, s_sum = residual, jnp.zeros_like(residual)
-    gate_grads, expert_owned = [], []
+    gate_grads, kept, partial_sums = [], [], {}
     for e in range(expert_count):
+        after = ()
+        if e == 0:
+            after = (far_stacks[3], owns[2])
+        if e == 1:
+            sources = expert_sources[1]
+            late = tie(sources[near - 1], y_sum)
+            expert_sources[1] = [
+                *sources[: near - 1],
+                late,
+                *sources[near : 2 * near - 1],
+                swap(late, CORE_BIT),
+            ]
+            after = (expert_sources[2][1],)
+        if e == 2:
+            after = (expert_sources[3][near - 1],)
+        if e >= 2:
+            half = add_core(*kept[e - 2])
+            partial_sums[e - 2] = half
+            after += (half[0],)
         y_sum, s_sum, gate_grad, keep, give = expert(
+            place,
             second_in,
             out_grad,
             ranks[e : e + 1],
             ranks_col[:, e : e + 1],
             gates[e : e + 1],
-            expert_quarters[e],
+            expert_sources[e],
+            0 if e % 2 == 0 else near,
             y_sum,
             s_sum,
-            capacity,
+            after,
         )
         gate_grads.append(gate_grad)
-        expert_owned.append(reduce_quarter(keep, give, 1))
+        kept.append((keep, swap(give, CORE_BIT)))
     block_output = y_sum.astype(BF16)
 
     prob_grad = jnp.concatenate(gate_grads, axis=0)
@@ -521,9 +663,41 @@
     context_grad = lax.dot_general(branch_grad, proj_full, NT, preferred_element_type=F32)
     context_grad = context_grad.astype(BF16)
 
-    query_grad, key_grad, value_grad = attend_back(
-        qkv_rows, kv_window, context_grad, first_key, last_key, lse, scale
-    )
+    owned = {}
+    for e in (2, 3):
+        partial_sums[e] = add_core(*kept[e])
+    quarter_sums = {0: add_chip(tie(partial_sums[0][0], y_sum), partial_sums[0][1])}
+    near_sums = {}
+    pairs = width // LANES
+    first_half = attend_back(
+        qkv_rows,
+        kv_window,
+        context_grad,
+        first_key,
+        last_key,
+        lse,
+        scale,
+        range(0, pairs // 2),
+        (quarter_sums[0], partial_sums[2][0]),
+    )
+    shares = {
+        0: [lax.psum_scatter(quarter_sums[0][at], "group", tiled=True) for at in range(2)],
+    }
+    second_half = attend_back(
+        qkv_rows,
+        kv_window,
+        context_grad,
+        first_key,
+        last_key,
+        lse,
+        scale,
+        range(pairs // 2, pairs),
+        (partial_sums[3][0], shares[0][0]),
+    )
+    near_sums[1] = add_near(partial_sums[1], second_half[0])
+    query_grad, key_grad, value_grad = [
+        jnp.concatenate(both, axis=1) for both in zip(first_half, second_half)
+    ]
     window_grad = jnp.concatenate([key_grad, value_grad], axis=1)
     from_below, from_above = shift(
         window_grad[:HALO], window_grad[HALO + row_count :], ("replica", "group")
@@ -550,32 +724,52 @@
     norm_grad = jnp.stack([gain_one_grad, bias_one_grad, gain_two_grad, bias_two_grad], axis=0)
     small_grad = jnp.concatenate([norm_grad, router_grad], axis=0).T
     small_grad = jnp.pad(small_grad, ((0, 0), (0, LANES - small_grad.shape[1]))).astype(BF16)
-    grad_blocks = [qkv_grad[:, i * width : (i + 1) * width].astype(BF16) for i in range(3)]
-    grad_blocks.append(proj_grad.astype(BF16))
-    grad_stack = jnp.stack(
+    columns = 3 * width // 2
+    qkv_grad, proj_grad = qkv_grad.astype(BF16), proj_grad.astype(BF16)
+    dense_grads = jnp.stack(
         [
-            jnp.concatenate([block, small_grad if at == 0 else jnp.zeros_like(small_grad)], axis=1)
-            for at, block in enumerate(grad_blocks)
+            jnp.concatenate([qkv_grad[:, :columns], proj_grad[:, : width // 2], small_grad], axis=1),
+            jnp.concatenate(
+                [qkv_grad[:, columns:], proj_grad[:, width // 2 :], jnp.zeros_like(small_grad)],
+                axis=1,
+            ),
         ]
     )
-    local = [lax.dynamic_index_in_dim(grad_stack, quarter ^ j, 0) for j in range(4)]
-    dense_owned = reduce_quarter(
-        jnp.concatenate(local[:2], axis=0), jnp.concatenate(local[2:], axis=0), 0
-    )
-    dense_parts = spread(dense_owned)
-    dense_sum = [pick(dense_parts, quarter ^ at).astype(F32) for at in range(4)]
-    expert_parts = spread(jnp.stack(expert_owned))
-    expert_sum = jnp.concatenate(
-        [pick(expert_parts, quarter ^ at) for at in range(4)], axis=3
-    ).astype(F32)
-
-    small_sum = dense_sum[0][:, width : width + 8]
+    got = swap(lax.dynamic_index_in_dim(dense_grads, 1 - core, 0, keepdims=False), CORE_BIT)
+    dense_half = summed([lax.dynamic_index_in_dim(dense_grads, core, 0, keepdims=False), got])
+    dense_near = scatter_near(dense_half.reshape(group, width // group, -1))
+    quarter_sums[2] = add_chip(tie(partial_sums[2][0], dense_near), partial_sums[2][1])
+    near_sums[3] = add_near(partial_sums[3], dense_near)
+    shares[2] = [
+        lax.psum_scatter(quarter_sums[2], "group", scatter_dimension=1, tiled=True),
+    ]
+    shares[0][1] = tie(shares[0][1], dense_near)
+    owned[0] = sum_chips(jnp.stack(shares[0]), 4)
+    owned[2] = sum_chips(tie(shares[2][0], dense_near), 4)
+    for e in (1, 3):
+        owned[e] = sum_chips(scatter_far(near_sums[e], dense_near), CHIP_BIT)
+    dense_half = sum_chips(scatter_far(dense_near), CHIP_BIT)
+    low, high = [part.astype(F32) for part in halves(dense_half, swap(dense_half, CORE_BIT), core)]
+
+    expert_sums = []
+    for e in range(expert_count):
+        if e % 2 == 0:
+            parts = spread(owned[e])
+            blocks = [pick(parts, quarter ^ at) for at in range(4)]
+        else:
+            both = halves(owned[e], swap(owned[e], CORE_BIT), core)
+            blocks = [block[at] for block in both for at in range(2)]
+        expert_sums.append(jnp.concatenate(blocks, axis=2))
+    expert_sum = jnp.stack(expert_sums).astype(F32)
+
+    small_sum = low[:, columns + width // 2 :][:, :8]
+    qkv_sum = jnp.concatenate([low[:, :columns], high[:, :columns]], axis=1)
+    proj_sum = jnp.concatenate(
+        [part[:, columns : columns + width // 2] for part in (low, high)], axis=1
+    )
     norm_new = adam_step(norm_weight, norm_moment, norm_squares, small_sum[:, :4].T, RATES[0])
-    qkv_sum = jnp.concatenate([part[:, :width] for part in dense_sum[:3]], axis=1)
     qkv_new = adam_step(qkv_weight, qkv_moment, qkv_squares, qkv_sum, RATES[1])
-    proj_new = adam_step(
-        proj_weight, proj_moment, proj_squares, dense_sum[3][:, :width], RATES[2]
-    )
+    proj_new = adam_step(proj_weight, proj_moment, proj_squares, proj_sum, RATES[2])
     router_new = adam_step(
         router_weight, router_moment, router_squares, small_sum[:, 4:8], RATES[3]
     )
@@ -599,19 +793,18 @@
     )
 
 
-def reduce_quarter(keep, give, dim):
-    got = swap(give, CORE_BIT)
-    mine = (keep[0].astype(F32) + got[0].astype(F32)).astype(BF16)
-    theirs = (keep[1].astype(F32) + got[1].astype(F32)).astype(BF16)
-    got = swap(theirs, CHIP_BIT)
-    mine = (mine.astype(F32) + got.astype(F32)).astype(BF16)
-    owned = lax.psum_scatter(mine, "group", scatter_dimension=dim, tiled=True)
-    bit = 4
-    while bit < lax.axis_size("replica"):
-        got = swap(owned, bit)
-        owned = (owned.astype(F32) + got.astype(F32)).astype(BF16)
-        bit *= 2
-    return owned
+def add_core(keep, got):
+    return [summed([keep[at], got[at]]) for at in range(2)]
+
+
+def add_chip(mine, theirs):
+    return summed([mine, swap(theirs, CHIP_BIT)])
+
+
+def add_near(half, *after):
+    group = lax.axis_size("group")
+    blocks = jnp.stack(half)
+    return scatter_near(blocks.reshape(2, 2, group, -1, blocks.shape[-1]), *after)
 
 
 def solution(mesh):

time: 980 us -> 994 us (1.014)
  waiting for transfers between devices: 589 us -> 341 us
  Pallas kernels: 159 us -> 322 us
  starting transfers between devices: 42.3 us -> 108 us
  other arithmetic: 85 us -> 114 us
    ppermute x31 -> x33, waiting for transfers between devices: 296 us -> 36.8 us  [swap(): return lax.ppermute(block, 'replica', [(r, r ^ bit) for r in range(count)])]
    ppermute x0 -> x28, waiting for transfers between devices: none -> 192 us  [group_swap(): return lax.ppermute(block, 'group', [(g, g ^ flip) for g in range(count)])]
    pallas_call x5 -> x22, Pallas kernels: 134 us -> 296 us  [the longest x2 159 us: place_pieces(): pl.pallas_call(partial(place_kernel, near, far, rows, cut), in_specs=[pl....]
    all_gather x5 -> x2, waiting for transfers between devices: 160 us -> 0.01 us  [per_device(): own = lax.all_gather(expert_cut(e, quarter, 4), 'group', axis=1, tiled=True)]
    ppermute x31 -> x33, starting transfers between devices: 30 us -> 72.7 us  [swap(): return lax.ppermute(block, 'replica', [(r, r ^ bit) for r in range(count)])]
    ppermute x0 -> x28, starting transfers between devices: none -> 21.5 us  [group_swap(): return lax.ppermute(block, 'group', [(g, g ^ flip) for g in range(count)])]
    reduce_scatter x4 -> x3, waiting for transfers between devices: 103 us -> 83.2 us  [the longest x2 83.2 us: per_device(): lax.psum_scatter(quarter_sums[0][at], 'group', tiled=True)]
    another operation x5 -> x15, other arithmetic: 3.72 us -> 15.7 us  [the longest x2 5.96 us: per_device(): jnp.stack([tie(far_pieces[e][0], context), *far_pieces[e][1:]])]
  transfers between devices with their start and end apart: 45 -> 70, of which waited for: 18 -> 22; matrix products, arithmetic and copies ran while one was open for 12% -> 16% of each run, Pallas kernels for 11% -> 33%
where the time goes in v2:
time: 994 us; the launch traced here: 985 us
  waiting for transfers between devices  341 us (34%)
  Pallas kernels  322 us (32%)
  other arithmetic  114 us (11%)
  starting transfers between devices  108 us (11%)
  local copies, waits for them, and re-layouts  64.3 us (6%)
  matrix products  19.7 us (2%)
  between operations  15.8 us (2%)
    ppermute x28, waiting for transfers between devices, group_swap(): return lax.ppermute(block, 'group', [(g, g ^ flip) for g in range(count)])  192 us
    pallas_call x2, Pallas kernels, place_pieces(): pl.pallas_call(partial(place_kernel, near, far, rows, cut), in_specs=[pl....  159 us
    pallas_call x4, Pallas kernels, expert(): pl.pallas_call(partial(expert_kernel, len(sources), near, len(after)), gr...  110 us
    reduce_scatter x2, waiting for transfers between devices, per_device(): lax.psum_scatter(quarter_sums[0][at], 'group', tiled=True)  83.2 us
    ppermute x33, starting transfers between devices, swap(): return lax.ppermute(block, 'replica', [(r, r ^ bit) for r in range(count)])  72.7 us
    convert_element_type x16, other arithmetic, summed(): return sum((part.astype(F32) for part in parts)).astype(BF16)  43.8 us
    ppermute x33, waiting for transfers between devices, swap(): return lax.ppermute(block, 'replica', [(r, r ^ bit) for r in range(count)])  36.8 us
    unnamed x235, local copies, waits for them, and re-layouts  32 us
  transfers between devices with their start and end apart: 70, of which 22 were waited for; matrix products, arithmetic and copies ran while one was open for 16% of the time, Pallas kernels for 33%

profile of v2, /device:TPU:23, one launch (start us, length us, event | category | flops | bytes accessed | tf_op | source)
XLA Modules:
  0.0 985.2 jit_solution(6082050962290073798)
XLA Ops:
  24.0 6.1 collective-permute-done.2.refs_1_
  30.1 17.8 %collective-permute-done.1 = bf16[96,1280]{1,0:T(8,128)(2,1)} collective-permute-done((bf16[96,1280]{1,0:T(8,128)(2,1)}, bf16[96,1280]{1,0:T(8,128)(2,1)}, u32[]{:S(2)}, u32[]{:S(2)}) %collective-permute-start.1) | collective-permute-done | bytes 245792 | tf_op jit(solution)/shard_map/ppermute | solution.py:63
  55.2 28.4 %collective-permute-done.3.refs_1_ = bf16[4,96,1280]{2,1,0:T(8,128)(2,1)} collective-permute-done((bf16[4,96,1280]{2,1,0:T(8,128)(2,1)S(1)}, bf16[4,96,1280]{2,1,0:T(8,128)(2,1)}, u32[]{:S(2)}, u32[]{:S(2)}) %collective-permute-start.3) | collective-permute-done | bytes 983072 | tf_op jit(solution)/shard_map/ppermute | solution.py:63
  97.6 13.9 %collective-permute-done.6.refs_4_ = bf16[2,96,1536]{2,1,0:T(8,128)(2,1)S(1)} collective-permute-done((bf16[2,96,1536]{2,1,0:T(8,128)(2,1)}, bf16[2,96,1536]{2,1,0:T(8,128)(2,1)S(1)}, u32[]{:S(2)}, u32[]{:S(2)}) %collective-permute-start.6) | collective-permute-done | bytes 589856 | tf_op jit(solution)/shard_map/ppermute | solution.py:63
  112.3 115.1 %place_pieces.2 = (bf16[8,96,2304]{2,1,0:T(8,128)(2,1)}, bf16[8,96,128]{2,1,0:T(8,128)(2,1)}) custom-call(s32[4]{0:T(128)} %pad_add_fusion.place_ref.refs_0_, bf16[4,96,1280]{2,1,0:T(8,128)(2,1)} %copy-done.29, bf16[4,96,1280]{2,1,0:T(8,128)(2,1)} %collective-permute-done.3.refs_1_, bf16[4,96,1280]{2,1,0:T(8,128)(2,1)} %collective-permute-done.4.refs_2_, ...), custom_call_target="tpu_custom_call" | custom-call | tf_op jit(solution)/shard_map/place_pieces/pallas_call | solution.py:136
  248.4 30.0 %collective-permute-done.18.refs_1_ = bf16[2,96,1536]{2,1,0:T(8,128)(2,1)S(1)} collective-permute-done((bf16[2,96,1536]{2,1,0:T(8,128)(2,1)S(1)}, bf16[2,96,1536]{2,1,0:T(8,128)(2,1)S(1)}, u32[]{:S(2)}, u32[]{:S(2)}) %collective-permute-start.18) | collective-permute-done | bytes 589856 | tf_op jit(solution)/shard_map/ppermute | solution.py:63
  281.1 43.7 %place_pieces.3 = (bf16[8,96,768]{2,1,0:T(8,128)(2,1)}, bf16[8,96,128]{2,1,0:T(8,128)(2,1)}) custom-call(s32[4]{0:T(128)} %pad_add_fusion.place_ref.refs_0_, bf16[4,96,512]{2,1,0:T(8,128)(2,1)} %pad_maximum_fusion.12.refs_0_, bf16[4,96,512]{2,1,0:T(8,128)(2,1)} %collective-permute-done.12.refs_1_, bf16[4,96,512]{2,1,0:T(8,128)(2,1)} %collective-permute-done.13.refs_2_, ...), custom_call_target="tpu_custom_call" | custom-call | tf_op jit(solution)/shard_map/place_pieces/pallas_call | solution.py:136
  329.8 9.2 collective-permute-start.15
  339.0 25.9 %attend.1 = (bf16[768,768]{1,0:T(8,128)(2,1)}, f32[6,8,256]{2,1,0:T(8,128)}) custom-call(bf16[768,2304]{1,0:T(8,128)(2,1)} %copy-done.25, bf16[1280,1536]{1,0:T(8,128)(2,1)} %pad_maximum_fusion.k_ref.v_ref, bf16[1280,1536]{1,0:T(8,128)(2,1)} %pad_maximum_fusion.k_ref.v_ref, s32[6,256]{1,0:T(8,128)} %bitcast.273, s32[6,256]{1,0:T(8,128)} %bitcast.270), custom_call_target="tpu_custom_call" | custom-call | flops 30000001024 | bytes 100000 | tf_op jit(solution)/shard_map/attend/pallas_call | solution.py:262
  369.2 10.4 %collective-permute-start.24 = (bf16[4,2,96,1536]{3,2,1,0:T(8,128)(2,1)}, bf16[4,2,96,1536]{3,2,1,0:T(8,128)(2,1)}, u32[]{:S(2)}, u32[]{:S(2)}) collective-permute-start(bf16[4,2,96,1536]{3,2,1,0:T(8,128)(2,1)} %pad_maximum_fusion.3.refs_8_), channel_id=1, source_target_pairs={{0,8},{8,0},{16,24},{24,16},{1,9},{9,1},{17,25},{25,17},{2,10},{10... | collective-permute-start | bytes 7077896 | tf_op jit(solution)/shard_map/ppermute | solution.py:32
  379.7 7.0 collective-permute-done.15
  402.4 27.2 %expert.4 = (f32[768,768]{1,0:T(8,128)}, f32[768,768]{1,0:T(8,128)}, f32[1,768]{1,0:T(1,128)}, bf16[2,2,768,768]{3,2,1,0:T(8,128)(2,1)}, bf16[2,2,768,768]{3,2,1,0:T(8,128)(2,1)}) custom-call(s32[4]{0:T(128)} %pad_add_fusion.place_ref.refs_0_, bf16[768,768]{1,0:T(8,128)(2,1)} %copy-done.6, bf16[768,768]{1,0:T(8,128)(2,1)} %refs_2_.7, ...), custom_call_target="tpu_custom_call" | custom-call | flops 44999999488 | bytes 100000 | tf_op jit(solution)/shard_map/expert/pallas_call | solution.py:447
  431.7 20.9 %collective-permute-done.26 = bf16[2,768,768]{2,1,0:T(8,128)(2,1)} collective-permute-done((bf16[2,768,768]{2,1,0:T(8,128)(2,1)}, bf16[2,768,768]{2,1,0:T(8,128)(2,1)}, u32[]{:S(2)}, u32[]{:S(2)}) %collective-permute-start.26) | collective-permute-done | bytes 2359328 | tf_op jit(solution)/shard_map/ppermute | solution.py:32
  454.7 27.8 %expert.5 = (f32[768,768]{1,0:T(8,128)}, f32[768,768]{1,0:T(8,128)}, f32[1,768]{1,0:T(1,128)}, bf16[2,2,768,768]{3,2,1,0:T(8,128)(2,1)}, bf16[2,2,768,768]{3,2,1,0:T(8,128)(2,1)}) custom-call(s32[4]{0:T(128)} %pad_add_fusion.place_ref.refs_0_, bf16[768,768]{1,0:T(8,128)(2,1)} %copy-done.6, bf16[768,768]{1,0:T(8,128)(2,1)} %refs_2_.7, ...), custom_call_target="tpu_custom_call" | custom-call | flops 44999999488 | bytes 100000 | tf_op jit(solution)/shard_map/expert/pallas_call | solution.py:447
  492.6 27.5 %expert.6 = (f32[768,768]{1,0:T(8,128)}, f32[768,768]{1,0:T(8,128)}, f32[1,768]{1,0:T(1,128)}, bf16[2,2,768,768]{3,2,1,0:T(8,128)(2,1)}, bf16[2,2,768,768]{3,2,1,0:T(8,128)(2,1)}) custom-call(s32[4]{0:T(128)} %pad_add_fusion.place_ref.refs_0_, bf16[768,768]{1,0:T(8,128)(2,1)} %copy-done.6, bf16[768,768]{1,0:T(8,128)(2,1)} %refs_2_.7, ...), custom_call_target="tpu_custom_call" | custom-call | flops 44999999488 | bytes 100000 | tf_op jit(solution)/shard_map/expert/pallas_call | solution.py:447
  520.9 5.8 add_convert_fusion.5
  526.7 27.7 %expert.7 = (f32[768,768]{1,0:T(8,128)}, f32[768,768]{1,0:T(8,128)}, f32[1,768]{1,0:T(1,128)}, bf16[2,2,768,768]{3,2,1,0:T(8,128)(2,1)}, bf16[2,2,768,768]{3,2,1,0:T(8,128)(2,1)}) custom-call(s32[4]{0:T(128)} %pad_add_fusion.place_ref.refs_0_, bf16[768,768]{1,0:T(8,128)(2,1)} %copy-done.6, bf16[768,768]{1,0:T(8,128)(2,1)} %refs_2_.7, ...), custom_call_target="tpu_custom_call" | custom-call | flops 44999999488 | bytes 100000 | tf_op jit(solution)/shard_map/expert/pallas_call | solution.py:447
  576.1 13.7 %attend_back.2 = (bf16[768,384]{1,0:T(8,128)(2,1)}, bf16[1280,384]{1,0:T(8,128)(2,1)}, bf16[1280,384]{1,0:T(8,128)(2,1)}) custom-call(bf16[768,2304]{1,0:T(8,128)(2,1)} %copy-done.25, bf16[1280,1536]{1,0:T(8,128)(2,1)} %pad_maximum_fusion.k_ref.v_ref, bf16[1280,1536]{1,0:T(8,128)(2,1)} %pad_maximum_fusion.k_ref.v_ref, ...), custom_call_target="tpu_custom_call" | custom-call | flops 15000000512 | bytes 100000 | tf_op jit(solution)/shard_map/attend_back/pallas_call | solution.py:294
  596.4 29.1 %reduce-scatter.4.cloned.1.call-done.refs_1_ = bf16[96,768]{1,0:T(8,128)(2,1)} async-done(((bf16[768,768]{1,0:T(8,128)(2,1)}), bf16[96,768]{1,0:T(8,128)(2,1)}) %reduce-scatter.4.cloned.1.call-update) | async-done | bytes 147472 | tf_op jit(solution)/shard_map/reduce_scatter | solution.py:684
  625.5 13.7 %attend_back.3 = (bf16[768,384]{1,0:T(8,128)(2,1)}, bf16[1280,384]{1,0:T(8,128)(2,1)}, bf16[1280,384]{1,0:T(8,128)(2,1)}) custom-call(bf16[768,2304]{1,0:T(8,128)(2,1)} %copy-done.25, bf16[1280,1536]{1,0:T(8,128)(2,1)} %pad_maximum_fusion.k_ref.v_ref, bf16[1280,1536]{1,0:T(8,128)(2,1)} %pad_maximum_fusion.k_ref.v_ref, ...), custom_call_target="tpu_custom_call" | custom-call | flops 15000000512 | bytes 100000 | tf_op jit(solution)/shard_map/attend_back/pallas_call | solution.py:294
  650.2 27.7 %collective-permute-done.37 = bf16[256,1536]{1,0:T(8,128)(2,1)S(1)} collective-permute-done((bf16[256,1536]{1,0:T(8,128)(2,1)S(1)}, bf16[256,1536]{1,0:T(8,128)(2,1)S(1)}, u32[]{:S(2)}, u32[]{:S(2)}) %collective-permute-start.37) | collective-permute-done | bytes 786464 | tf_op jit(solution)/shard_map/ppermute | solution.py:52
  721.7 21.5 %collective-permute-done.40 = bf16[4,96,1664]{2,1,0:T(8,128)(2,1)S(1)} collective-permute-done((bf16[4,96,1664]{2,1,0:T(8,128)(2,1)S(1)}, bf16[4,96,1664]{2,1,0:T(8,128)(2,1)S(1)}, u32[]{:S(2)}, u32[]{:S(2)}) %collective-permute-start.40) | collective-permute-done | bytes 1277984 | tf_op jit(solution)/shard_map/ppermute | solution.py:63
  744.7 54.1 %reduce-scatter.6.cloned.1.call-done.refs_0_ = bf16[96,768]{1,0:T(8,128)(2,1)} async-done(((bf16[768,768]{1,0:T(8,128)(2,1)}), bf16[96,768]{1,0:T(8,128)(2,1)}) %reduce-scatter.6.cloned.1.call-update) | async-done | bytes 147472 | tf_op jit(solution)/shard_map/reduce_scatter | solution.py:684
  815.8 7.1 collective-permute-done.41
  826.2 23.7 %collective-permute-done.43 = bf16[96,1664]{1,0:T(8,128)(2,1)S(1)} collective-permute-done((bf16[96,1664]{1,0:T(8,128)(2,1)S(1)}, bf16[96,1664]{1,0:T(8,128)(2,1)S(1)}, u32[]{:S(2)}, u32[]{:S(2)}) %collective-permute-start.43) | collective-permute-done | bytes 319520 | tf_op jit(solution)/shard_map/ppermute | solution.py:63
  851.1 14.9 %collective-permute-start.47 = (bf16[2,96,768]{2,1,0:T(8,128)(2,1)}, bf16[2,96,768]{2,1,0:T(8,128)(2,1)S(1)}, u32[]{:S(2)}, u32[]{:S(2)}) collective-permute-start(bf16[2,96,768]{2,1,0:T(8,128)(2,1)} %get-tuple-element.293), channel_id=1, source_target_pairs={{0,8},{8,0},{16,24},{24,16},{1,9},{9,1},{17,25},{25,17},{2,10},{10... | collective-permute-start | bytes 884744 | tf_op jit(solution)/shard_map/ppermute | solution.py:32
  867.6 31.7 %collective-permute-done.61 = bf16[2,2,96,768]{3,2,1,0:T(8,128)(2,1)S(1)} collective-permute-done((bf16[2,2,96,768]{3,2,1,0:T(8,128)(2,1)S(1)}, bf16[2,2,96,768]{3,2,1,0:T(8,128)(2,1)S(1)}, u32[]{:S(2)}, u32[]{:S(2)}) %collective-permute-start.61) | collective-permute-done | bytes 589856 | tf_op jit(solution)/shard_map/ppermute | solution.py:63
  899.3 9.6 collective-permute-start.54
  908.9 7.7 collective-permute-done.62
  949.7 6.4 collective-permute-done.56
  961.0 9.2 multiply_subtract_fusion
  970.2 8.2 multiply_subtract_fusion.1
  (529 shorter events, 246.8 us)
Async XLA Ops:
  7.2 322.6 %all-gather.3.cloned.1.call-start = ((), (), s32[]{:S(2)}) async-start(), calls=%async_computation.3 | async-start | bytes 2654208 | tf_op jit(solution)/shard_map/all_gather | solution.py:560
  14.2 385.1 %all-gather.5.cloned.1.call-start = ((), (), s32[]{:S(2)}) async-start(), calls=%async_computation.4 | async-start | bytes 2654208 | tf_op jit(solution)/shard_map/all_gather | solution.py:560
  20.1 71.1 %collective-permute-start.7 = (bf16[96,512]{1,0:T(8,128)(2,1)}, bf16[96,512]{1,0:T(8,128)(2,1)}, u32[]{:S(2)}, u32[]{:S(2)}) collective-permute-start(bf16[96,512]{1,0:T(8,128)(2,1)} %get-tuple-element.295), channel_id=1, source_target_pairs={{0,2},{1,3},{2,0},{3,1},{4,6},{5,7},{6,4},{7,5},{8,10},{9,11},{10,... | collective-permute-start | bytes 294920 | tf_op jit(solution)/shard_map/ppermute | solution.py:63
  21.6 70.3 %collective-permute-start.8 = (bf16[96,512]{1,0:T(8,128)(2,1)}, bf16[96,512]{1,0:T(8,128)(2,1)}, u32[]{:S(2)}, u32[]{:S(2)}) collective-permute-start(bf16[96,512]{1,0:T(8,128)(2,1)} %get-tuple-element.295), channel_id=1, source_target_pairs={{0,4},{1,5},{2,6},{3,7},{4,0},{5,1},{6,2},{7,3},{8,12},{9,13},{10,... | collective-permute-start | bytes 294920 | tf_op jit(solution)/shard_map/ppermute | solution.py:63
  22.4 603.1 %reduce-scatter.4.cloned.1.call-start = ((), (), s32[]{:S(2)}) async-start(), calls=%async_computation.5 | async-start | bytes 1327104 | tf_op jit(solution)/shard_map/reduce_scatter | solution.py:684
  52.6 58.9 %collective-permute-start.4 = (bf16[4,96,1280]{2,1,0:T(8,128)(2,1)S(1)}, bf16[4,96,1280]{2,1,0:T(8,128)(2,1)}, u32[]{:S(2)}, u32[]{:S(2)}) collective-permute-start(bf16[4,96,1280]{2,1,0:T(8,128)(2,1)S(1)} %pad_maximum_fusion.8.refs_0_), channel_id=1, source_target_pairs={{0,8},{8,0},{16,24},{24,16},{1,9},{9,1},{17,25},{25,17},{2,10},{10... | collective-permute-start | bytes 2949128 | tf_op jit(solution)/shard_map/ppermute | solution.py:32
  97.4 147.5 %collective-permute-start.12 = (bf16[4,96,512]{2,1,0:T(8,128)(2,1)}, bf16[4,96,512]{2,1,0:T(8,128)(2,1)}, u32[]{:S(2)}, u32[]{:S(2)}) collective-permute-start(bf16[4,96,512]{2,1,0:T(8,128)(2,1)} %pad_maximum_fusion.12.refs_0_), channel_id=1, source_target_pairs={{0,1},{1,0},{2,3},{3,2},{4,5},{5,4},{6,7},{7,6},{8,9},{9,8},{10,11... | collective-permute-start | bytes 1179656 | tf_op jit(solution)/shard_map/ppermute | solution.py:63
  235.9 88.9 %collective-permute-start.10 = (bf16[256,1536]{1,0:T(8,128)(2,1)}, bf16[256,1536]{1,0:T(8,128)(2,1)}, u32[]{:S(2)}, u32[]{:S(2)}) collective-permute-start(bf16[256,1536]{1,0:T(8,128)(2,1)} %get-tuple-element.241), channel_id=1, source_target_pairs={{0,1},{1,2},{2,3},{3,4},{4,5},{5,6},{6,7},{7,8},{8,9},{9,10},{10,1... | collective-permute-start | bytes 2359304 | tf_op jit(solution)/shard_map/ppermute | solution.py:52
  241.1 85.5 %collective-permute-start.11 = (bf16[256,1536]{1,0:T(8,128)(2,1)}, bf16[256,1536]{1,0:T(8,128)(2,1)}, u32[]{:S(2)}, u32[]{:S(2)}) collective-permute-start(bf16[256,1536]{1,0:T(8,128)(2,1)} %get-tuple-element.242), channel_id=1, source_target_pairs={{1,0},{2,1},{3,2},{4,3},{5,4},{6,5},{7,6},{8,7},{9,8},{10,9},{11,1... | collective-permute-start | bytes 2359304 | tf_op jit(solution)/shard_map/ppermute | solution.py:52
  278.4 86.5 %collective-permute-start.22 = (bf16[2,96,1536]{2,1,0:T(8,128)(2,1)S(1)}, bf16[2,96,1536]{2,1,0:T(8,128)(2,1)}, u32[]{:S(2)}, u32[]{:S(2)}) collective-permute-start(bf16[2,96,1536]{2,1,0:T(8,128)(2,1)S(1)} %copy-done.24), channel_id=1, source_target_pairs={{0,4},{1,5},{2,6},{3,7},{4,0},{5,1},{6,2},{7,3},{8,12},{9,13},{10,... | collective-permute-start | bytes 1769480 | tf_op jit(solution)/shard_map/ppermute | solution.py:63
  279.2 90.0 %collective-permute-start.19 = (bf16[2,96,1536]{2,1,0:T(8,128)(2,1)}, bf16[2,96,1536]{2,1,0:T(8,128)(2,1)S(1)}, u32[]{:S(2)}, u32[]{:S(2)}) collective-permute-start(bf16[2,96,1536]{2,1,0:T(8,128)(2,1)} %tie.15.refs_0_), channel_id=1, source_target_pairs={{0,2},{1,3},{2,0},{3,1},{4,6},{5,7},{6,4},{7,5},{8,10},{9,11},{10,... | collective-permute-start | bytes 1769480 | tf_op jit(solution)/shard_map/ppermute | solution.py:63
  280.3 99.3 %collective-permute-start.20 = (bf16[2,96,1536]{2,1,0:T(8,128)(2,1)}, bf16[2,96,1536]{2,1,0:T(8,128)(2,1)}, u32[]{:S(2)}, u32[]{:S(2)}) collective-permute-start(bf16[2,96,1536]{2,1,0:T(8,128)(2,1)} %tie.15.refs_0_), channel_id=1, source_target_pairs={{0,4},{1,5},{2,6},{3,7},{4,0},{5,1},{6,2},{7,3},{8,12},{9,13},{10,... | collective-permute-start | bytes 1769480 | tf_op jit(solution)/shard_map/ppermute | solution.py:63
  325.8 53.8 %collective-permute-start.21 = (bf16[2,96,1536]{2,1,0:T(8,128)(2,1)S(1)}, bf16[2,96,1536]{2,1,0:T(8,128)(2,1)}, u32[]{:S(2)}, u32[]{:S(2)}) collective-permute-start(bf16[2,96,1536]{2,1,0:T(8,128)(2,1)S(1)} %copy-done.22), channel_id=1, source_target_pairs={{0,6},{1,7},{2,4},{3,5},{4,2},{5,3},{6,0},{7,1},{8,14},{9,15},{10,... | collective-permute-start | bytes 1769480 | tf_op jit(solution)/shard_map/ppermute | solution.py:63
  329.8 56.8 %collective-permute-start.15 = (bf16[2,768,768]{2,1,0:T(8,128)(2,1)}, bf16[2,768,768]{2,1,0:T(8,128)(2,1)}, u32[]{:S(2)}, u32[]{:S(2)}) collective-permute-start(bf16[2,768,768]{2,1,0:T(8,128)(2,1)} %all-gather.3.cloned.1.call-done), channel_id=1, source_target_pairs={{0,16},{8,24},{16,0},{24,8},{1,17},{9,25},{17,1},{25,9},{2,18},{10... | collective-permute-start | bytes 7077896 | tf_op jit(solution)/shard_map/ppermute | solution.py:32
  369.2 60.5 %collective-permute-start.23 = (bf16[4,2,96,1536]{3,2,1,0:T(8,128)(2,1)}, bf16[4,2,96,1536]{3,2,1,0:T(8,128)(2,1)}, u32[]{:S(2)}, u32[]{:S(2)}) collective-permute-start(bf16[4,2,96,1536]{3,2,1,0:T(8,128)(2,1)} %pad_maximum_fusion.3.refs_8_), channel_id=1, source_target_pairs={{0,1},{1,0},{2,3},{3,2},{4,5},{5,4},{6,7},{7,6},{8,9},{9,8},{10,11... | collective-permute-start | bytes 7077896 | tf_op jit(solution)/shard_map/ppermute | solution.py:63
  369.2 62.2 %collective-permute-start.24 = (bf16[4,2,96,1536]{3,2,1,0:T(8,128)(2,1)}, bf16[4,2,96,1536]{3,2,1,0:T(8,128)(2,1)}, u32[]{:S(2)}, u32[]{:S(2)}) collective-permute-start(bf16[4,2,96,1536]{3,2,1,0:T(8,128)(2,1)} %pad_maximum_fusion.3.refs_8_), channel_id=1, source_target_pairs={{0,8},{8,0},{16,24},{24,16},{1,9},{9,1},{17,25},{25,17},{2,10},{10... | collective-permute-start | bytes 7077896 | tf_op jit(solution)/shard_map/ppermute | solution.py:32
  430.0 55.8 %collective-permute-start.30 = (bf16[2,2,768,768]{3,2,1,0:T(8,128)(2,1)}, bf16[2,2,768,768]{3,2,1,0:T(8,128)(2,1)}, u32[]{:S(2)}, u32[]{:S(2)}) collective-permute-start(bf16[2,2,768,768]{3,2,1,0:T(8,128)(2,1)} %get-tuple-element.60), channel_id=1, source_target_pairs={{0,8},{8,0},{16,24},{24,16},{1,9},{9,1},{17,25},{25,17},{2,10},{10... | collective-permute-start | bytes 14155784 | tf_op jit(solution)/shard_map/ppermute | solution.py:32
  431.4 53.9 %collective-permute-start.29 = (bf16[4,2,96,1536]{3,2,1,0:T(8,128)(2,1)}, bf16[4,2,96,1536]{3,2,1,0:T(8,128)(2,1)}, u32[]{:S(2)}, u32[]{:S(2)}) collective-permute-start(bf16[4,2,96,1536]{3,2,1,0:T(8,128)(2,1)} %pad_maximum_fusion.2.refs_12_.refs_8_), channel_id=1, source_target_pairs={{0,1},{1,0},{2,3},{3,2},{4,5},{5,4},{6,7},{7,6},{8,9},{9,8},{10,11... | collective-permute-start | bytes 7077896 | tf_op jit(solution)/shard_map/ppermute | solution.py:63
  431.4 59.8 %collective-permute-start.27 = (bf16[2,768,768]{2,1,0:T(8,128)(2,1)}, bf16[2,768,768]{2,1,0:T(8,128)(2,1)}, u32[]{:S(2)}, u32[]{:S(2)}) collective-permute-start(bf16[2,768,768]{2,1,0:T(8,128)(2,1)} %tie.17.refs_13_), channel_id=1, source_target_pairs={{0,8},{8,0},{16,24},{24,16},{1,9},{9,1},{17,25},{25,17},{2,10},{10... | collective-permute-start | bytes 7077896 | tf_op jit(solution)/shard_map/ppermute | solution.py:32
  491.1 63.4 %collective-permute-start.34 = (bf16[2,768,768]{2,1,0:T(8,128)(2,1)S(1)}, bf16[2,768,768]{2,1,0:T(8,128)(2,1)}, u32[]{:S(2)}, u32[]{:S(2)}) collective-permute-start(bf16[2,768,768]{2,1,0:T(8,128)(2,1)S(1)} %get-tuple-element.223), channel_id=1, source_target_pairs={{0,16},{8,24},{16,0},{24,8},{1,17},{9,25},{17,1},{25,9},{2,18},{10... | collective-permute-start | bytes 7077896 | tf_op jit(solution)/shard_map/ppermute | solution.py:32
  560.5 238.4 %reduce-scatter.6.cloned.1.call-start = ((), (), s32[]{:S(2)}) async-start(), calls=%async_computation.6 | async-start | bytes 1327104 | tf_op jit(solution)/shard_map/reduce_scatter | solution.py:684
  567.9 135.5 %collective-permute-start.49 = (bf16[2,2,4,96,768]{4,3,2,1,0:T(8,128)(2,1)}, bf16[2,2,4,96,768]{4,3,2,1,0:T(8,128)(2,1)}, u32[]{:S(2)}, u32[]{:S(2)}) collective-permute-start(bf16[2,2,4,96,768]{4,3,2,1,0:T(8,128)(2,1)} %get-tuple-element.226), channel_id=1, source_target_pairs={{0,1},{1,0},{2,3},{3,2},{4,5},{5,4},{6,7},{7,6},{8,9},{9,8},{10,11... | collective-permute-start | bytes 7077896 | tf_op jit(solution)/shard_map/ppermute | solution.py:63
  703.0 244.6 %reduce-scatter.8.cloned.1.call-start = ((), (), s32[]{:S(2)}) async-start(), calls=%async_computation.7 | async-start | bytes 2654208 | tf_op jit(solution)/shard_map/reduce_scatter | solution.py:744
  703.1 100.9 %collective-permute-start.55 = (bf16[2,768,768]{2,1,0:T(8,128)(2,1)}, bf16[2,768,768]{2,1,0:T(8,128)(2,1)}, u32[]{:S(2)}, u32[]{:S(2)}) collective-permute-start(bf16[2,768,768]{2,1,0:T(8,128)(2,1)} %get-tuple-element.219), channel_id=1, source_target_pairs={{0,16},{8,24},{16,0},{24,8},{1,17},{9,25},{17,1},{25,9},{2,18},{10... | collective-permute-start | bytes 7077896 | tf_op jit(solution)/shard_map/ppermute | solution.py:32
  712.8 87.7 %collective-permute-start.50 = (bf16[2,2,96,768]{3,2,1,0:T(8,128)(2,1)}, bf16[2,2,96,768]{3,2,1,0:T(8,128)(2,1)}, u32[]{:S(2)}, u32[]{:S(2)}) collective-permute-start(bf16[2,2,96,768]{3,2,1,0:T(8,128)(2,1)} %get-tuple-element.248), channel_id=1, source_target_pairs={{0,2},{1,3},{2,0},{3,1},{4,6},{5,7},{6,4},{7,5},{8,10},{9,11},{10,... | collective-permute-start | bytes 1769480 | tf_op jit(solution)/shard_map/ppermute | solution.py:63
  714.0 86.8 %collective-permute-start.51 = (bf16[2,2,96,768]{3,2,1,0:T(8,128)(2,1)}, bf16[2,2,96,768]{3,2,1,0:T(8,128)(2,1)}, u32[]{:S(2)}, u32[]{:S(2)}) collective-permute-start(bf16[2,2,96,768]{3,2,1,0:T(8,128)(2,1)} %get-tuple-element.247), channel_id=1, source_target_pairs={{0,4},{1,5},{2,6},{3,7},{4,0},{5,1},{6,2},{7,3},{8,12},{9,13},{10,... | collective-permute-start | bytes 1769480 | tf_op jit(solution)/shard_map/ppermute | solution.py:63
  718.3 92.4 %collective-permute-start.59 = (bf16[2,2,4,96,768]{4,3,2,1,0:T(8,128)(2,1)}, bf16[2,2,4,96,768]{4,3,2,1,0:T(8,128)(2,1)}, u32[]{:S(2)}, u32[]{:S(2)}) collective-permute-start(bf16[2,2,4,96,768]{4,3,2,1,0:T(8,128)(2,1)} %get-tuple-element.228), channel_id=1, source_target_pairs={{0,1},{1,0},{2,3},{3,2},{4,5},{5,4},{6,7},{7,6},{8,9},{9,8},{10,11... | collective-permute-start | bytes 7077896 | tf_op jit(solution)/shard_map/ppermute | solution.py:63
  743.2 57.6 %collective-permute-start.52 = (bf16[2,2,96,768]{3,2,1,0:T(8,128)(2,1)S(1)}, bf16[2,2,96,768]{3,2,1,0:T(8,128)(2,1)}, u32[]{:S(2)}, u32[]{:S(2)}) collective-permute-start(bf16[2,2,96,768]{3,2,1,0:T(8,128)(2,1)S(1)} %get-tuple-element.246), channel_id=1, source_target_pairs={{0,6},{1,7},{2,4},{3,5},{4,2},{5,3},{6,0},{7,1},{8,14},{9,15},{10,... | collective-permute-start | bytes 1769480 | tf_op jit(solution)/shard_map/ppermute | solution.py:63
  802.7 63.3 %collective-permute-start.53 = (bf16[2,2,96,768]{3,2,1,0:T(8,128)(2,1)S(1)}, bf16[2,2,96,768]{3,2,1,0:T(8,128)(2,1)}, u32[]{:S(2)}, u32[]{:S(2)}) collective-permute-start(bf16[2,2,96,768]{3,2,1,0:T(8,128)(2,1)S(1)} %add_convert_fusion.17), channel_id=1, source_target_pairs={{0,16},{8,24},{16,0},{24,8},{1,17},{9,25},{17,1},{25,9},{2,18},{10... | collective-permute-start | bytes 1769480 | tf_op jit(solution)/shard_map/ppermute | solution.py:32
  826.2 73.1 %collective-permute-start.61 = (bf16[2,2,96,768]{3,2,1,0:T(8,128)(2,1)S(1)}, bf16[2,2,96,768]{3,2,1,0:T(8,128)(2,1)S(1)}, u32[]{:S(2)}, u32[]{:S(2)}) collective-permute-start(bf16[2,2,96,768]{3,2,1,0:T(8,128)(2,1)S(1)} %get-tuple-element.251), channel_id=1, source_target_pairs={{0,4},{1,5},{2,6},{3,7},{4,0},{5,1},{6,2},{7,3},{8,12},{9,13},{10,... | collective-permute-start | bytes 1769480 | tf_op jit(solution)/shard_map/ppermute | solution.py:63
  849.9 66.7 %collective-permute-start.62 = (bf16[2,2,96,768]{3,2,1,0:T(8,128)(2,1)S(1)}, bf16[2,2,96,768]{3,2,1,0:T(8,128)(2,1)S(1)}, u32[]{:S(2)}, u32[]{:S(2)}) collective-permute-start(bf16[2,2,96,768]{3,2,1,0:T(8,128)(2,1)S(1)} %get-tuple-element.250), channel_id=1, source_target_pairs={{0,6},{1,7},{2,4},{3,5},{4,2},{5,3},{6,0},{7,1},{8,14},{9,15},{10,... | collective-permute-start | bytes 1769480 | tf_op jit(solution)/shard_map/ppermute | solution.py:63
  851.1 66.9 %collective-permute-start.47 = (bf16[2,96,768]{2,1,0:T(8,128)(2,1)}, bf16[2,96,768]{2,1,0:T(8,128)(2,1)S(1)}, u32[]{:S(2)}, u32[]{:S(2)}) collective-permute-start(bf16[2,96,768]{2,1,0:T(8,128)(2,1)} %get-tuple-element.293), channel_id=1, source_target_pairs={{0,8},{8,0},{16,24},{24,16},{1,9},{9,1},{17,25},{25,17},{2,10},{10... | collective-permute-start | bytes 884744 | tf_op jit(solution)/shard_map/ppermute | solution.py:32
  (147 other events, 2711.4 us)
Sparse Core Ops, SparseCore 0:
  14.3 72.7 all-gather.2
  89.9 55.6 all-gather.4
  560.6 64.8 reduce-scatter.3
  703.1 95.6 reduce-scatter.5
  807.7 95.7 reduce-scatter.7

commit v3 on v2

--- a/solution.py
+++ b/solution.py
@@ -17,11 +17,13 @@
 QB = 128
 HALO = 256
 SPAN = QB + 2 * HALO
+TAIL = 16
+HALVES = 2
 CORE_BIT = 1
 CHIP_BIT = 2
 F32 = jnp.float32
 BF16 = jnp.bfloat16
-EXPERT_COST = pl.CostEstimate(flops=45 * 10**9, bytes_accessed=10**5, transcendentals=0)
+EXPERT_COST = pl.CostEstimate(flops=52 * 10**9, bytes_accessed=10**5, transcendentals=0)
 ATTEND_COST = pl.CostEstimate(flops=30 * 10**9, bytes_accessed=10**5, transcendentals=0)
 BACK_COST = pl.CostEstimate(flops=15 * 10**9, bytes_accessed=10**5, transcendentals=0)
 NT = (((1,), (1,)), ((), ()))
@@ -30,15 +32,6 @@
 def swap(block, bit):
     count = lax.axis_size("replica")
     return lax.ppermute(block, "replica", [(r, r ^ bit) for r in range(count)])
-
-
-def spread(block):
-    other_chip = swap(block, CHIP_BIT)
-    return [block, other_chip, swap(block, CORE_BIT), swap(other_chip, CORE_BIT)]
-
-
-def quarter_of(replica):
-    return (replica & 1) * 2 + ((replica >> 1) & 1)
 
 
 def pick(blocks, index):
@@ -87,13 +80,12 @@
     return summed([mine] + [group_swap(parts[j], j) for j in range(1, near)])
 
 
-def scatter_far(blocks, *after):
+def far_parts(blocks):
     far, near = group_shape()
     place = lax.axis_index("group") // near
     axis = blocks.ndim - 3
     parts = [lax.dynamic_index_in_dim(blocks, place ^ k, axis, keepdims=False) for k in range(far)]
-    mine = tie(parts[0], *after) if after else parts[0]
-    return summed([mine] + [group_swap(parts[k], k * near) for k in range(1, far)])
+    return [parts[0]] + [group_swap(parts[k], k * near) for k in range(1, far)]
 
 
 def sum_chips(block, bit):
@@ -107,41 +99,43 @@
     return jnp.where(core == 0, own, other), jnp.where(core == 0, other, own)
 
 
-def place_kernel(near, far, rows, cut, place_ref, *refs):
+def place_kernel(near, far, cut, place_ref, *refs):
     own, other = refs[:near], refs[near : 2 * near]
-    full_ref, side_ref, sems = refs[-3:]
-    copies = []
+    full_ref, side_ref = refs[-2:]
+    core = place_ref[2]
     for j in range(near):
         for k in range(far):
             shard = (place_ref[0] ^ k) * near + (place_ref[1] ^ j)
-            core = place_ref[2]
-            for refs_of, half in ((own, core), (other, 1 - core)):
-                columns = pl.ds(pl.multiple_of(half * cut, LANES), cut)
-                copies.append((refs_of[j].at[k, :, pl.ds(0, cut)], full_ref.at[shard, :, columns]))
-            copies.append((own[j].at[k, :, pl.ds(cut, LANES)], side_ref.at[shard]))
-    copies = [
-        pltpu.make_async_copy(source, target, sems.at[at])
-        for at, (source, target) in enumerate(copies)
-    ]
-    for copy in copies:
-        copy.start()
-    for copy in copies:
-        copy.wait()
+
+            @pl.when(core == 0)
+            def _():
+                full_ref[shard, :, :cut] = own[j][k, :, :cut]
+                full_ref[shard, :, cut:] = other[j][k, :, :cut]
+
+            @pl.when(core != 0)
+            def _():
+                full_ref[shard, :, :cut] = other[j][k, :, :cut]
+                full_ref[shard, :, cut:] = own[j][k, :, :cut]
+
+            side_ref[shard] = own[j][k, :, cut:]
 
 
 def place_pieces(own, other, place, after=()):
     near, far = len(own), own[0].shape[0]
     rows, cut = own[0].shape[1], own[0].shape[2] - LANES
     raw = pl.BlockSpec(memory_space=pl.ANY)
+    near_by = pl.BlockSpec(memory_space=pltpu.VMEM)
     full, side = pl.pallas_call(
-        partial(place_kernel, near, far, rows, cut),
-        in_specs=[pl.BlockSpec(memory_space=pltpu.SMEM)] + [raw] * (2 * near + len(after)),
-        out_specs=[raw, raw],
+        partial(place_kernel, near, far, cut),
+        in_specs=[pl.BlockSpec(memory_space=pltpu.SMEM)]
+        + [near_by] * (2 * near)
+        + [raw] * len(after),
+        out_specs=[near_by, near_by],
         out_shape=[
             jax.ShapeDtypeStruct((near * far, rows, 2 * cut), BF16),
             jax.ShapeDtypeStruct((near * far, rows, LANES), BF16),
         ],
-        scratch_shapes=[pltpu.SemaphoreType.DMA((3 * near * far,))],
+        compiler_params=pltpu.CompilerParams(vmem_limit_bytes=56 * 2**20),
         name="place_pieces",
     )(place, *own, *other, *after)
     return full.reshape(-1, 2 * cut), side.reshape(-1, LANES)
@@ -331,163 +325,257 @@
     return pre * below, below + pre * density
 
 
-def expert_kernel(lists, near, waits, *refs):
-    place_ref, rows_ref, dy_ref, rank_row_ref, rank_col_ref, gate_row_ref, y_in_ref, s_in_ref = refs[:8]
-    source_refs = refs[8 : 8 + lists]
-    outs = refs[8 + lists + waits :]
-    y_ref, s_ref, gate_grad_ref, keep_ref, give_ref, weights, arrived = outs[:7]
-    x_slots, xt_slots, g_slots, gt_slots, dy_slots, gate_slots, eout, xgrad = outs[7:]
+def pack_kernel(rows_ref, rank_ref, *refs):
+    out_ref = refs[-1]
+    slots, tokens = out_ref.shape[1], rows_ref.shape[0]
+    slot = lax.broadcasted_iota(jnp.int32, (slots, tokens), 0)
+    spots = jnp.where(slot == rank_ref[0], 1.0, 0.0).astype(BF16)
+    out_ref[0] = jnp.dot(spots, rows_ref[...], preferred_element_type=F32).astype(BF16)
+
+
+def pack(rows, ranks, slots):
+    tokens, width = rows.shape
+    count = ranks.shape[0]
+    return pl.pallas_call(
+        pack_kernel,
+        grid=(count,),
+        in_specs=[
+            pl.BlockSpec((tokens, width), lambda e: (0, 0)),
+            pl.BlockSpec((1, 1, tokens), lambda e: (e, 0, 0)),
+        ],
+        out_specs=pl.BlockSpec((1, slots, width), lambda e: (e, 0, 0)),
+        out_shape=jax.ShapeDtypeStruct((count, slots, width), BF16),
+        compiler_params=pltpu.CompilerParams(vmem_limit_bytes=56 * 2**20),
+        name="pack",
+    )(rows, ranks.reshape(count, 1, tokens))
+
+
+def token_spots(rank_col, slots):
+    slot = lax.broadcasted_iota(jnp.int32, (rank_col.shape[0], slots), 1)
+    return slot == rank_col
+
+
+def unpack_grad_kernel(count, *refs):
+    parts, rank_refs = refs[:count], refs[count : 2 * count]
+    sum_ref, gate_grad_ref = refs[-2:]
+    tokens = sum_ref.shape[0]
+    slots = parts[0].shape[0] - TAIL
+    total = jnp.zeros(sum_ref.shape, F32)
+    gate_grads = jnp.zeros((tokens, LANES), F32)
+    lane = lax.broadcasted_iota(jnp.int32, (tokens, LANES), 1)
+    for j in range(count):
+        mask = token_spots(rank_refs[j][...], slots)
+        spots = jnp.where(mask, 1.0, 0.0).astype(BF16)
+        total += jnp.dot(spots, parts[j][:slots, :], preferred_element_type=F32)
+        tail = parts[j][slots:, :].astype(F32)
+        slot_grad = tail[0:1, :slots] + tail[1:2, :slots]
+        gate_grad = jnp.sum(jnp.where(mask, slot_grad, 0.0), axis=1, keepdims=True)
+        gate_grads = jnp.where(lane == j, gate_grad, gate_grads)
+    sum_ref[...] = total
+    gate_grad_ref[...] = gate_grads
+
+
+def unpack_grad(parts, rank_cols, after=()):
+    tokens, width = rank_cols[0].shape[0], parts[0].shape[1]
+    count = len(parts)
+    near_by = pl.BlockSpec(memory_space=pltpu.VMEM)
+    return pl.pallas_call(
+        partial(unpack_grad_kernel, count),
+        in_specs=[near_by] * (2 * count) + [pl.BlockSpec(memory_space=pl.ANY)] * len(after),
+        out_specs=[near_by, near_by],
+        out_shape=[
+            jax.ShapeDtypeStruct((tokens, width), F32),
+            jax.ShapeDtypeStruct((tokens, LANES), F32),
+        ],
+        compiler_params=pltpu.CompilerParams(vmem_limit_bytes=56 * 2**20),
+        name="unpack_grad",
+    )(*parts, *rank_cols, *after)
+
+
+def unpack_out_kernel(count, residual_ref, *refs):
+    parts, rank_refs = refs[:count], refs[count : 2 * count]
+    gate_refs, out_ref = refs[2 * count : 3 * count], refs[-1]
+    total = residual_ref[...]
+    for j in range(count):
+        mask = token_spots(rank_refs[j][...], parts[j].shape[0])
+        spots = jnp.where(mask, 1.0, 0.0).astype(BF16)
+        total += gate_refs[j][...] * jnp.dot(spots, parts[j][...], preferred_element_type=F32)
+    out_ref[...] = total.astype(BF16)
+
+
+def unpack_out(residual, parts, rank_cols, gate_cols, after=()):
+    near_by = pl.BlockSpec(memory_space=pltpu.VMEM)
+    return pl.pallas_call(
+        partial(unpack_out_kernel, len(parts)),
+        in_specs=[near_by] * (1 + 3 * len(parts)) + [pl.BlockSpec(memory_space=pl.ANY)] * len(after),
+        out_specs=near_by,
+        out_shape=jax.ShapeDtypeStruct(residual.shape, BF16),
+        compiler_params=pltpu.CompilerParams(vmem_limit_bytes=56 * 2**20),
+        name="unpack_out",
+    )(residual, *parts, *rank_cols, *gate_cols, *after)
+
+
+def expert_kernel(count, near, first, expert_count, place_ref, router_ref, *refs):
+    x_parts, dy_parts = refs[:count], refs[count : 2 * count]
+    sources = refs[2 * count : 2 * count + near]
+    refs = refs[2 * count + near :]
+    before, refs = (None, refs) if first else (refs[:2], refs[2:])
+    out_ref, xgrad_ref, grad_ref = refs[-15:-12]
+    weights, arrived, part_sems, x_rows, xt_rows, g_rows, gt_rows, dy_rows = refs[-12:-4]
+    act_rows, pg_rows, eout, xgrad = refs[-4:]
     step = pl.program_id(0)
-    tokens, width = rows_ref.shape
-    slots = x_slots.shape[0]
+    steps = pl.num_programs(0)
+    slots, width = x_parts[0].shape
     hidden = weights.shape[-1]
 
-    def fetch(number):
-        slot = number % 2
-        if near == 0:
-            return [
-                pltpu.make_async_copy(source_refs[number], weights.at[slot], arrived.at[slot, 0])
-            ]
+    def fetch(number, slot):
+        columns = pl.ds(pl.multiple_of(number * hidden, LANES), hidden)
         copies = []
-        columns = pl.ds(number % 2 * hidden, hidden)
         for j in range(near):
-            source = source_refs[number // 2 * near + j]
-            for k in range(source.shape[0]):
+            for k in range(sources[j].shape[0]):
                 shard = (place_ref[0] ^ k) * near + (place_ref[1] ^ j)
                 copies.append(
                     pltpu.make_async_copy(
-                        source.at[k, :, :, columns],
+                        sources[j].at[k, :, :, columns],
                         weights.at[slot, :, shard],
                         arrived.at[slot, len(copies)],
                     )
                 )
         return copies
 
-    def slot_mask():
-        slot = lax.broadcasted_iota(jnp.int32, (slots, tokens), 0)
-        return slot == rank_row_ref[...]
+    slot_of = lax.rem(step, 2)
 
     @pl.when(step == 0)
     def _():
-        for copy in fetch(0) + fetch(1):
+        copies = []
+        for part in range(count):
+            rows = pl.ds(part * slots, slots)
+            copies.append((x_parts[part], x_rows.at[rows]))
+            copies.append((dy_parts[part], dy_rows.at[rows]))
+        if before is not None:
+            copies += [(before[0], eout), (before[1], xgrad)]
+        copies = [
+            pltpu.make_async_copy(source, target, part_sems.at[at])
+            for at, (source, target) in enumerate(copies)
+        ]
+        for copy in copies + fetch(0, 0):
             copy.start()
-        mask = slot_mask()
-        spots = jnp.where(mask, 1.0, 0.0).astype(BF16)
-        x_f32 = jnp.dot(spots, rows_ref[...], preferred_element_type=F32)
-        x_slots[...] = x_f32.astype(BF16)
-        xt_slots[...] = x_f32.T.astype(BF16)
-        dy_f32 = jnp.dot(spots, dy_ref[...], preferred_element_type=F32)
-        dy_slots[...] = dy_f32.astype(BF16)
-        gate = jnp.sum(jnp.where(mask, gate_row_ref[...], 0.0), axis=1, keepdims=True)
-        gate_slots[...] = gate
-        g_f32 = dy_f32 * gate
-        g_slots[...] = g_f32.astype(BF16)
-        gt_slots[...] = g_f32.T.astype(BF16)
-        eout[...] = jnp.zeros_like(eout)
-        xgrad[...] = jnp.zeros_like(xgrad)
-
-    for number in range(4):
-
-        @pl.when(step == number)
-        def _():
-            for copy in fetch(number):
-                copy.wait()
-            if 1 <= number < 3:
-                for copy in fetch(number + 1):
-                    copy.start()
-
-    slot_of = lax.rem(step, 2)
+        for copy in copies:
+            copy.wait()
+        if before is None:
+            eout[...] = jnp.zeros_like(eout)
+            xgrad[...] = jnp.zeros_like(xgrad)
+
+        def scale_part(part, carry):
+            rows = pl.ds(pl.multiple_of(part * slots, 16), slots)
+            logits = jnp.dot(x_rows[rows, :], router_ref[...], preferred_element_type=F32)
+            lane = lax.broadcasted_iota(jnp.int32, logits.shape, 1)
+            logits = jnp.where(lane < expert_count, logits, MASKED)
+            expo = jnp.exp(logits - jnp.max(logits, axis=1, keepdims=True))
+            mine = jnp.sum(jnp.where(lane == place_ref[3], expo, 0.0), axis=1, keepdims=True)
+            gate = mine / jnp.sum(expo, axis=1, keepdims=True)
+            g_rows[rows, :] = (dy_rows[rows, :].astype(F32) * gate).astype(BF16)
+            return carry
+
+        lax.fori_loop(0, count, scale_part, 0)
+        xt_rows[...] = x_rows[...].T
+        gt_rows[...] = g_rows[...].T
+
+    @pl.when(step + 1 < steps)
+    def _():
+        for copy in fetch(step + 1, 1 - slot_of):
+            copy.start()
+
+    for copy in fetch(step, slot_of):
+        copy.wait()
     inner = weights[slot_of, 0].reshape(width, hidden)
     outer = weights[slot_of, 1].reshape(width, hidden)
-    pre = jnp.dot(x_slots[...], inner, preferred_element_type=F32)
-    act_grad = jnp.dot(g_slots[...], outer, preferred_element_type=F32)
-    act, slope = gelu_both(pre)
-    act = act.astype(BF16)
-    pre_grad = (act_grad * slope).astype(BF16)
-    eout[...] += lax.dot_general(act, outer, NT, preferred_element_type=F32)
-    xgrad[...] += lax.dot_general(pre_grad, inner, NT, preferred_element_type=F32)
-    inner_grad = jnp.dot(xt_slots[...], pre_grad, preferred_element_type=F32).astype(BF16)
-    outer_grad = jnp.dot(gt_slots[...], act, preferred_element_type=F32).astype(BF16)
-
-    @pl.when(step < 2)
+
+    def part_step(part, carry):
+        rows = pl.ds(pl.multiple_of(part * slots, 16), slots)
+        pre = jnp.dot(x_rows[rows, :], inner, preferred_element_type=F32)
+        act_grad = jnp.dot(g_rows[rows, :], outer, preferred_element_type=F32)
+        act, slope = gelu_both(pre)
+        act = act.astype(BF16)
+        pre_grad = (act_grad * slope).astype(BF16)
+        act_rows[rows, :] = act
+        pg_rows[rows, :] = pre_grad
+        eout[rows, :] += lax.dot_general(act, outer, NT, preferred_element_type=F32)
+        xgrad[rows, :] += lax.dot_general(pre_grad, inner, NT, preferred_element_type=F32)
+        return carry
+
+    lax.fori_loop(0, count, part_step, 0)
+    grad_ref[0] = jnp.dot(xt_rows[...], pg_rows[...], preferred_element_type=F32).astype(BF16)
+    grad_ref[1] = jnp.dot(gt_rows[...], act_rows[...], preferred_element_type=F32).astype(BF16)
+
+    @pl.when(step == steps - 1)
     def _():
-        keep_ref[0, 0] = inner_grad
-        keep_ref[0, 1] = outer_grad
-
-    @pl.when(step >= 2)
-    def _():
-        give_ref[0, 0] = inner_grad
-        give_ref[0, 1] = outer_grad
-
-    @pl.when(step == 3)
-    def _():
-        out = eout[...]
-        slot_grad = jnp.sum(dy_slots[...].astype(F32) * out, axis=1, keepdims=True)
-        gate_grad_ref[...] = jnp.sum(jnp.where(slot_mask(), slot_grad, 0.0), axis=0, keepdims=True)
-        slot = lax.broadcasted_iota(jnp.int32, (tokens, slots), 1)
-        spots = jnp.where(slot == rank_col_ref[...], 1.0, 0.0).astype(BF16)
-        scaled = (out * gate_slots[...]).astype(BF16)
-        y_ref[...] = y_in_ref[...] + jnp.dot(spots, scaled, preferred_element_type=F32)
-        s_ref[...] = s_in_ref[...] + jnp.dot(
-            spots, xgrad[...].astype(BF16), preferred_element_type=F32
-        )
-
-
-def expert(place, rows, dy, rank_row, rank_col, gate_row, sources, near, y_sum, s_sum, after=()):
-    tokens, width = rows.shape
+        if first:
+            out_ref[...] = eout[...]
+            xgrad_ref[...] = xgrad[...]
+            return
+        for part in range(count):
+            rows = slice(part * slots, (part + 1) * slots)
+            out = eout[rows, :]
+            out_ref[part] = out.astype(BF16)
+            xgrad_ref[part, :slots, :] = xgrad[rows, :].astype(BF16)
+            slot_grad = jnp.sum(dy_rows[rows, :].astype(F32) * out, axis=1, keepdims=True)
+            row = jnp.broadcast_to(slot_grad, (slots, LANES)).T[0:1, :]
+            row = jnp.concatenate([row, jnp.zeros((1, width - slots), F32)], axis=1)
+            high = row.astype(BF16).astype(F32)
+            at = lax.broadcasted_iota(jnp.int32, (TAIL, width), 0)
+            tail = jnp.where(at == 0, high, jnp.where(at == 1, row - high, 0.0))
+            xgrad_ref[part, slots:, :] = tail.astype(BF16)
+
+
+def expert(place, router, x_parts, dy_parts, sources, expert_count, before=(), after=()):
+    count, near = len(x_parts), len(sources)
+    slots, width = x_parts[0].shape
     group = lax.axis_size("group")
-    hidden = sources[0].shape[-1] // (2 if near else 1)
-    slots = -(-(5 * tokens // 8) // LANES) * LANES
-
-    def whole(shape):
-        return pl.BlockSpec(shape, lambda i: (0, 0), pipeline_mode=pl.Buffered(1))
-
+    columns = sources[0].shape[-1]
+    hidden = 512 if columns % 512 == 0 else columns
     raw = pl.BlockSpec(memory_space=pl.ANY)
-    grad_block = (1, 2, width, hidden)
+    first = len(before) == 0
+    if first:
+        shapes = [jax.ShapeDtypeStruct((count * slots, width), F32)] * 2
+    else:
+        shapes = [
+            jax.ShapeDtypeStruct((count, slots, width), BF16),
+            jax.ShapeDtypeStruct((count, slots + TAIL, width), BF16),
+        ]
+    rows = count * slots
     return pl.pallas_call(
-        partial(expert_kernel, len(sources), near, len(after)),
-        grid=(4,),
+        partial(expert_kernel, count, near, first, expert_count),
+        grid=(columns // hidden,),
         in_specs=[
             pl.BlockSpec(memory_space=pltpu.SMEM),
-            whole((tokens, width)),
-            whole((tokens, width)),
-            whole((1, tokens)),
-            whole((tokens, 1)),
-            whole((1, tokens)),
-            whole((tokens, width)),
-            whole((tokens, width)),
-            *[raw] * (len(sources) + len(after)),
+            pl.BlockSpec(router.shape, lambda i: (0, 0), pipeline_mode=pl.Buffered(1)),
+            *[raw] * (2 * count + near + len(before) + len(after)),
         ],
         out_specs=[
-            pl.BlockSpec((tokens, width), lambda i: (0, 0)),
-            pl.BlockSpec((tokens, width), lambda i: (0, 0)),
-            pl.BlockSpec((1, tokens), lambda i: (0, 0)),
-            pl.BlockSpec(grad_block, lambda i: (jnp.minimum(i, 1), 0, 0, 0)),
-            pl.BlockSpec(grad_block, lambda i: (jnp.maximum(i - 2, 0), 0, 0, 0)),
-        ],
-        out_shape=[
-            jax.ShapeDtypeStruct((tokens, width), F32),
-            jax.ShapeDtypeStruct((tokens, width), F32),
-            jax.ShapeDtypeStruct((1, tokens), F32),
-            jax.ShapeDtypeStruct((2, 2, width, hidden), BF16),
-            jax.ShapeDtypeStruct((2, 2, width, hidden), BF16),
-        ],
+            pl.BlockSpec(shapes[0].shape, lambda i: (0,) * len(shapes[0].shape)),
+            pl.BlockSpec(shapes[1].shape, lambda i: (0,) * len(shapes[1].shape)),
+            pl.BlockSpec((2, width, hidden), lambda i: (0, 0, i)),
+        ],
+        out_shape=[*shapes, jax.ShapeDtypeStruct((2, width, columns), BF16)],
         scratch_shapes=[
             pltpu.VMEM((2, 2, group, width // group, hidden), BF16),
             pltpu.SemaphoreType.DMA((2, group)),
-            pltpu.VMEM((slots, width), BF16),
-            pltpu.VMEM((width, slots), BF16),
-            pltpu.VMEM((slots, width), BF16),
-            pltpu.VMEM((width, slots), BF16),
-            pltpu.VMEM((slots, width), BF16),
-            pltpu.VMEM((slots, 1), F32),
-            pltpu.VMEM((slots, width), F32),
-            pltpu.VMEM((slots, width), F32),
-        ],
-        compiler_params=pltpu.CompilerParams(vmem_limit_bytes=60 * 2**20),
+            pltpu.SemaphoreType.DMA((2 * count + 2,)),
+            pltpu.VMEM((rows, width), BF16),
+            pltpu.VMEM((width, rows), BF16),
+            pltpu.VMEM((rows, width), BF16),
+            pltpu.VMEM((width, rows), BF16),
+            pltpu.VMEM((rows, width), BF16),
+            pltpu.VMEM((rows, hidden), BF16),
+            pltpu.VMEM((rows, hidden), BF16),
+            pltpu.VMEM((rows, width), F32),
+            pltpu.VMEM((rows, width), F32),
+        ],
+        compiler_params=pltpu.CompilerParams(vmem_limit_bytes=62 * 2**20),
         cost_estimate=EXPERT_COST,
         name="expert",
-    )(place, rows, dy, rank_row, rank_col, gate_row, y_sum, s_sum, *sources, *after)
+    )(place, router, *x_parts, *dy_parts, *sources, *before, *after)
 
 
 def per_device(
@@ -517,9 +605,8 @@
     row_count, width = block_input.shape
     scale = (width // HEADS) ** (-0.5)
     expert_count, _, hidden = inner_weight.shape
-    cut = hidden // 4
     replica = lax.axis_index("replica")
-    quarter = quarter_of(replica)
+    mine = replica & (expert_count - 1)
     device_pos = lax.axis_index(("replica", "group"))
     all_rows = row_count * lax.axis_size(("replica", "group"))
     first_row = device_pos * row_count
@@ -527,7 +614,7 @@
     far, near = group_shape()
     core = replica & 1
     group_at = lax.axis_index("group")
-    place = jnp.stack([group_at // near, group_at % near, core, core]).astype(jnp.int32)
+    place = jnp.stack([group_at // near, group_at % near, core, mine]).astype(jnp.int32)
 
     def dense_gather(matrix, side):
         cut_to = matrix.shape[1] // 2
@@ -543,32 +630,38 @@
     qkv_far = dense_gather(qkv_weight, small)
     proj_far = dense_gather(proj_weight, jnp.zeros_like(small))
 
-    outer_turned = outer_weight.transpose(0, 2, 1)
-
-    def expert_cut(e, part, count):
-        size = hidden // count
+    capacity = 5 * row_count // 8
+    names = jnp.arange(expert_count, dtype=jnp.int32)
+    named = jnp.any(routes.T[None, :, :] == (mine ^ names)[:, None, None], axis=1)
+    earlier = jnp.arange(row_count)[:, None] < jnp.arange(row_count)[None, :]
+    before = jnp.dot(named.astype(BF16), earlier.astype(BF16), preferred_element_type=F32)
+    ranks = jnp.where(named, before.astype(jnp.int32), -1)
+    rank_cols = [ranks[j][:, None] for j in range(expert_count)]
+
+    def exchange(packed):
+        return [packed[0]] + [swap(packed[j], j) for j in range(expert_count - 1, 0, -1)][::-1]
+
+    def expert_cut(part):
+        size = hidden // HALVES
         return jnp.stack(
             [
-                lax.dynamic_slice_in_dim(matrix[e], part * size, size, axis=1)
-                for matrix in (inner_weight, outer_turned)
+                lax.dynamic_index_in_dim(matrix, mine, 0, keepdims=False)[
+                    :, part * size : (part + 1) * size
+                ]
+                for matrix in (inner_weight, outer_weight.transpose(0, 2, 1))
             ]
         ).astype(BF16)
 
-    expert_sources, owns = {}, {}
     group = far * near
-    for e in range(0, expert_count, 2):
-        own = lax.all_gather(expert_cut(e, quarter, 4), "group", axis=1, tiled=True)
-        owns[e] = own
-
-    far_pieces = {}
-    first_far = gather_far(tie(expert_cut(1, core, 2), qkv_far[-1]))
-    qkv_full, small_full = dense_place(qkv_far, (first_far[1], *proj_far[1:]))
+    far_pieces = [gather_far(tie(expert_cut(0), qkv_far[-1]))]
+    far_pieces.append(gather_far(tie(expert_cut(1), far_pieces[0][-1])))
+    dy_parts = exchange(pack(out_grad, ranks, capacity))
+    qkv_full, small_full = dense_place(qkv_far, (far_pieces[0][1], *proj_far[1:]))
     proj_full, _ = dense_place(proj_far)
     small_rows = small_full[:, :8].T
     norm_full = small_rows[:4].astype(F32)
     router_t = small_rows[4:8]
-    far_pieces[1] = first_far
-    far_pieces[3] = gather_far(tie(expert_cut(3, core, 2), first_far[-1]))
+    router_pad = jnp.pad(small_full[:, 4:8], ((0, 0), (0, LANES - 4)))
 
     x_float = block_input.astype(F32)
     normed_one, scale_one = standardize(x_float)
@@ -585,15 +678,10 @@
     first_key = jnp.tile(first_key.reshape(-1, QB), (1, 2))
     last_key = jnp.tile(last_key.reshape(-1, QB), (1, 2))
     context, lse = attend(qkv_rows, kv_window, first_key, last_key, scale)
-    owns[2] = tie(owns[2], context)
-    for e in range(0, expert_count, 2):
-        blocks = spread(owns[e])
-        expert_sources[e] = [block.reshape(2, group, width // group, cut) for block in blocks]
-    far_stacks = {}
-    for e in range(1, expert_count, 2):
-        far_stacks[e] = jnp.stack([tie(far_pieces[e][0], context), *far_pieces[e][1:]])
-        own = gather_near(far_stacks[e])
-        expert_sources[e] = own + [swap(block, CORE_BIT) for block in own]
+    sources, stacks = [], []
+    for pieces in far_pieces:
+        stacks.append(jnp.stack([tie(pieces[0], context), *pieces[1:]]))
+        sources.append(gather_near(stacks[-1]))
     residual = x_float + jnp.dot(context, proj_full, preferred_element_type=F32)
     normed_two, scale_two = standardize(residual)
     second_in = (normed_two * norm_full[2] + norm_full[3]).astype(BF16)
@@ -601,53 +689,26 @@
     logits = lax.dot_general(router_t, second_in, NT, preferred_element_type=F32)
     logit_expo = jnp.exp(logits - jnp.max(logits, axis=0, keepdims=True))
     gates = logit_expo / jnp.sum(logit_expo, axis=0, keepdims=True)
-    names = jnp.arange(expert_count, dtype=jnp.int32)
-    named = jnp.any(routes.T[None, :, :] == names[:, None, None], axis=1)
-    earlier = jnp.arange(row_count)[:, None] < jnp.arange(row_count)[None, :]
-    before = jnp.dot(named.astype(BF16), earlier.astype(BF16), preferred_element_type=F32)
-    ranks = jnp.where(named, before.astype(jnp.int32), -1)
-    ranks_col = ranks.T
-
-    y_sum, s_sum = residual, jnp.zeros_like(residual)
-    gate_grads, kept, partial_sums = [], [], {}
-    for e in range(expert_count):
-        after = ()
-        if e == 0:
-            after = (far_stacks[3], owns[2])
-        if e == 1:
-            sources = expert_sources[1]
-            late = tie(sources[near - 1], y_sum)
-            expert_sources[1] = [
-                *sources[: near - 1],
-                late,
-                *sources[near : 2 * near - 1],
-                swap(late, CORE_BIT),
-            ]
-            after = (expert_sources[2][1],)
-        if e == 2:
-            after = (expert_sources[3][near - 1],)
-        if e >= 2:
-            half = add_core(*kept[e - 2])
-            partial_sums[e - 2] = half
-            after += (half[0],)
-        y_sum, s_sum, gate_grad, keep, give = expert(
-            place,
-            second_in,
-            out_grad,
-            ranks[e : e + 1],
-            ranks_col[:, e : e + 1],
-            gates[e : e + 1],
-            expert_sources[e],
-            0 if e % 2 == 0 else near,
-            y_sum,
-            s_sum,
-            after,
-        )
-        gate_grads.append(gate_grad)
-        kept.append((keep, swap(give, CORE_BIT)))
-    block_output = y_sum.astype(BF16)
-
-    prob_grad = jnp.concatenate(gate_grads, axis=0)
+    gate_cols = [
+        lax.dynamic_index_in_dim(gates, mine ^ j, 0, keepdims=False)[:, None]
+        for j in range(expert_count)
+    ]
+
+    x_parts = exchange(pack(second_in, ranks, capacity))
+    *sums, low_grad = expert(
+        place, router_pad, x_parts, dy_parts, sources[0], expert_count, (), (stacks[1],)
+    )
+    out_slots, grad_slots, high_grad = expert(
+        place, router_pad, x_parts, dy_parts, sources[1], expert_count, sums
+    )
+    near_sums = {0: add_near(low_grad)}
+    s_sum, gate_grads = unpack_grad(exchange(grad_slots), rank_cols, (near_sums[0],))
+    out_parts = exchange(tie(out_slots, s_sum))
+
+    gate_grads = gate_grads[:, :expert_count].T
+    prob_grad = jnp.concatenate(
+        [lax.dynamic_index_in_dim(gate_grads, mine ^ e, 0) for e in range(expert_count)], axis=0
+    )
     logit_grad = gates * (prob_grad - jnp.sum(gates * prob_grad, axis=0, keepdims=True))
     logit_grad = logit_grad.astype(BF16)
     router_grad = jnp.dot(logit_grad, second_in, preferred_element_type=F32)
@@ -663,12 +724,8 @@
     context_grad = lax.dot_general(branch_grad, proj_full, NT, preferred_element_type=F32)
     context_grad = context_grad.astype(BF16)
 
-    owned = {}
-    for e in (2, 3):
-        partial_sums[e] = add_core(*kept[e])
-    quarter_sums = {0: add_chip(tie(partial_sums[0][0], y_sum), partial_sums[0][1])}
-    near_sums = {}
     pairs = width // LANES
+    low_parts = far_parts(near_sums[0])
     first_half = attend_back(
         qkv_rows,
         kv_window,
@@ -678,11 +735,9 @@
         lse,
         scale,
         range(0, pairs // 2),
-        (quarter_sums[0], partial_sums[2][0]),
-    )
-    shares = {
-        0: [lax.psum_scatter(quarter_sums[0][at], "group", tiled=True) for at in range(2)],
-    }
+        (low_parts[1],),
+    )
+    near_sums[1] = add_near(high_grad, first_half[0])
     second_half = attend_back(
         qkv_rows,
         kv_window,
@@ -692,9 +747,9 @@
         lse,
         scale,
         range(pairs // 2, pairs),
-        (partial_sums[3][0], shares[0][0]),
-    )
-    near_sums[1] = add_near(partial_sums[1], second_half[0])
+        (near_sums[1], low_parts[2]),
+    )
+    block_output = unpack_out(residual, out_parts, rank_cols, gate_cols, (second_half[0],))
     query_grad, key_grad, value_grad = [
         jnp.concatenate(both, axis=1) for both in zip(first_half, second_half)
     ]
@@ -738,29 +793,20 @@
     got = swap(lax.dynamic_index_in_dim(dense_grads, 1 - core, 0, keepdims=False), CORE_BIT)
     dense_half = summed([lax.dynamic_index_in_dim(dense_grads, core, 0, keepdims=False), got])
     dense_near = scatter_near(dense_half.reshape(group, width // group, -1))
-    quarter_sums[2] = add_chip(tie(partial_sums[2][0], dense_near), partial_sums[2][1])
-    near_sums[3] = add_near(partial_sums[3], dense_near)
-    shares[2] = [
-        lax.psum_scatter(quarter_sums[2], "group", scatter_dimension=1, tiled=True),
-    ]
-    shares[0][1] = tie(shares[0][1], dense_near)
-    owned[0] = sum_chips(jnp.stack(shares[0]), 4)
-    owned[2] = sum_chips(tie(shares[2][0], dense_near), 4)
-    for e in (1, 3):
-        owned[e] = sum_chips(scatter_far(near_sums[e], dense_near), CHIP_BIT)
-    dense_half = sum_chips(scatter_far(dense_near), CHIP_BIT)
+    owned = jnp.concatenate(
+        [
+            summed([tie(parts[0], dense_near), *parts[1:]])
+            for parts in (low_parts, far_parts(near_sums[1]))
+        ],
+        axis=2,
+    )
+    owned = sum_chips(owned, expert_count)
+    dense_half = sum_chips(summed(far_parts(dense_near)), CHIP_BIT)
     low, high = [part.astype(F32) for part in halves(dense_half, swap(dense_half, CORE_BIT), core)]
 
-    expert_sums = []
-    for e in range(expert_count):
-        if e % 2 == 0:
-            parts = spread(owned[e])
-            blocks = [pick(parts, quarter ^ at) for at in range(4)]
-        else:
-            both = halves(owned[e], swap(owned[e], CORE_BIT), core)
-            blocks = [block[at] for block in both for at in range(2)]
-        expert_sums.append(jnp.concatenate(blocks, axis=2))
-    expert_sum = jnp.stack(expert_sums).astype(F32)
+    other_chip = swap(owned, CHIP_BIT)
+    parts = [owned, swap(owned, CORE_BIT), other_chip, swap(other_chip, CORE_BIT)]
+    expert_sum = jnp.stack([pick(parts, mine ^ e) for e in range(expert_count)]).astype(F32)
 
     small_sum = low[:, columns + width // 2 :][:, :8]
     qkv_sum = jnp.concatenate([low[:, :columns], high[:, :columns]], axis=1)
@@ -793,18 +839,9 @@
     )
 
 
-def add_core(keep, got):
-    return [summed([keep[at], got[at]]) for at in range(2)]
-
-
-def add_chip(mine, theirs):
-    return summed([mine, swap(theirs, CHIP_BIT)])
-
-
-def add_near(half, *after):
+def add_near(grads, *after):
     group = lax.axis_size("group")
-    blocks = jnp.stack(half)
-    return scatter_near(blocks.reshape(2, 2, group, -1, blocks.shape[-1]), *after)
+    return scatter_near(grads.reshape(2, group, -1, grads.shape[-1]), *after)
 
 
 def solution(mesh):

time: 994 us -> 727 us (0.73)
  Pallas kernels: 322 us -> 180 us
  waiting for transfers between devices: 341 us -> 285 us
  other arithmetic: 114 us -> 71.9 us
  starting transfers between devices: 108 us -> 75.9 us
  local copies, waits for them, and re-layouts: 64.3 us -> 80.7 us
  between operations: 15.8 us -> 2.35 us
    pallas_call x6 -> x8, Pallas kernels: 269 us -> 126 us  [the longest x2 93.8 us: expert(): pl.pallas_call(partial(expert_kernel, count, near, first, expert_count),...]
    reduce_scatter x3 -> x0, waiting for transfers between devices: 83.2 us -> none  [the longest x2 83.2 us: per_device(): lax.psum_scatter(quarter_sums[0][at], 'group', tiled=True)]
    ppermute x33 -> x22, waiting for transfers between devices: 36.8 us -> 88.8 us  [swap(): return lax.ppermute(block, 'replica', [(r, r ^ bit) for r in range(count)])]
    ppermute x33 -> x22, starting transfers between devices: 72.7 us -> 29.2 us  [swap(): return lax.ppermute(block, 'replica', [(r, r ^ bit) for r in range(count)])]
    convert_element_type x16 -> x8, other arithmetic: 43.8 us -> 17.1 us  [summed(): return sum((part.astype(F32) for part in parts)).astype(BF16)]
    ppermute x28, waiting for transfers between devices: 192 us -> 168 us  [group_swap(): return lax.ppermute(block, 'group', [(g, g ^ flip) for g in range(count)])]
    squeeze x10 -> x7, local copies, waits for them, and re-layouts: 4.22 us -> 16.2 us  [the longest x4 13.4 us: exchange(): packed[j]]
    unnamed x235 -> x212, local copies, waits for them, and re-layouts: 32 us -> 24.3 us
  transfers between devices with their start and end apart: 70 -> 54, of which waited for: 22 -> 21; matrix products, arithmetic and copies ran while one was open for 16% -> 17% of each run, Pallas kernels for 33% -> 23%
where the time goes in v3:
time: 727 us; the launch traced here: 719 us
  waiting for transfers between devices  285 us (39%)
  Pallas kernels  180 us (25%)
  local copies, waits for them, and re-layouts  80.7 us (11%)
  starting transfers between devices  75.9 us (10%)
  other arithmetic  71.9 us (10%)
  matrix products  22.9 us (3%)
    ppermute x28, waiting for transfers between devices, group_swap(): return lax.ppermute(block, 'group', [(g, g ^ flip) for g in range(count)])  168 us
    pallas_call x2, Pallas kernels, expert(): pl.pallas_call(partial(expert_kernel, count, near, first, expert_count),...  93.8 us
    ppermute x22, waiting for transfers between devices, swap(): return lax.ppermute(block, 'replica', [(r, r ^ bit) for r in range(count)])  88.8 us
    ppermute x28, starting transfers between devices, group_swap(): return lax.ppermute(block, 'group', [(g, g ^ flip) for g in range(count)])  30.9 us
    ppermute x22, starting transfers between devices, swap(): return lax.ppermute(block, 'replica', [(r, r ^ bit) for r in range(count)])  29.2 us
    ppermute x4, waiting for transfers between devices, shift(): return (lax.ppermute(tail, axes, up), lax.ppermute(head, axes, down))  28.7 us
    pallas_call x2, Pallas kernels, attend_back(): pl.pallas_call(partial(attend_back_kernel, scale), grid=(count,), in_spec...  27.6 us
    pallas_call x1, Pallas kernels, attend(): pl.pallas_call(partial(attend_kernel, scale), grid=(pairs,), in_specs=[pl...  25.9 us
  transfers between devices with their start and end apart: 54, of which 21 were waited for; matrix products, arithmetic and copies ran while one was open for 17% of the time, Pallas kernels for 23%

profile of v3, /device:TPU:23, one launch (start us, length us, event | category | flops | bytes accessed | tf_op | source)
XLA Modules:
  0.0 718.9 jit_solution(13035215565244136520)
XLA Ops:
  14.9 10.8 %collective-permute-done.1 = bf16[96,1280]{1,0:T(8,128)(2,1)} collective-permute-done((bf16[96,1280]{1,0:T(8,128)(2,1)S(1)}, bf16[96,1280]{1,0:T(8,128)(2,1)}, u32[]{:S(2)}, u32[]{:S(2)}) %collective-permute-start.1) | collective-permute-done | bytes 245792 | tf_op jit(solution)/shard_map/ppermute | solution.py:56
  32.1 15.9 %collective-permute-done.3.refs_1_ = bf16[4,96,1280]{2,1,0:T(8,128)(2,1)} collective-permute-done((bf16[4,96,1280]{2,1,0:T(8,128)(2,1)S(1)}, bf16[4,96,1280]{2,1,0:T(8,128)(2,1)}, u32[]{:S(2)}, u32[]{:S(2)}) %collective-permute-start.3) | collective-permute-done | bytes 983072 | tf_op jit(solution)/shard_map/ppermute | solution.py:56
  61.5 7.7 %collective-permute-done.6.refs_4_ = bf16[2,96,1536]{2,1,0:T(8,128)(2,1)S(1)} collective-permute-done((bf16[2,96,1536]{2,1,0:T(8,128)(2,1)}, bf16[2,96,1536]{2,1,0:T(8,128)(2,1)S(1)}, u32[]{:S(2)}, u32[]{:S(2)}) %collective-permute-start.6) | collective-permute-done | bytes 589856 | tf_op jit(solution)/shard_map/ppermute | solution.py:56
  76.1 5.5 convolution_convert_fusion.1.q_ref
  82.7 7.5 %collective-permute-start.10 = (bf16[256,1536]{1,0:T(8,128)(2,1)}, bf16[256,1536]{1,0:T(8,128)(2,1)}, u32[]{:S(2)}, u32[]{:S(2)}) collective-permute-start(bf16[256,1536]{1,0:T(8,128)(2,1)} %get-tuple-element.208), channel_id=1, source_target_pairs={{0,1},{1,2},{2,3},{3,4},{4,5},{5,6},{6,7},{7,8},{8,9},{9,10},{10,1... | collective-permute-start | bytes 2359304 | tf_op jit(solution)/shard_map/ppermute | solution.py:45
  95.8 5.3 pack.3
  104.6 23.8 %collective-permute-done.21.refs_1_ = bf16[2,96,1536]{2,1,0:T(8,128)(2,1)S(1)} collective-permute-done((bf16[2,96,1536]{2,1,0:T(8,128)(2,1)S(1)}, bf16[2,96,1536]{2,1,0:T(8,128)(2,1)S(1)}, u32[]{:S(2)}, u32[]{:S(2)}) %collective-permute-start.21) | collective-permute-done | bytes 589856 | tf_op jit(solution)/shard_map/ppermute | solution.py:56
  130.0 5.6 collective-permute-start.19
  147.3 25.9 %attend.1 = (bf16[768,768]{1,0:T(8,128)(2,1)}, f32[6,8,256]{2,1,0:T(8,128)}) custom-call(bf16[768,2304]{1,0:T(8,128)(2,1)} %copy-done.24, bf16[1280,1536]{1,0:T(8,128)(2,1)} %pad_maximum_fusion.1.k_ref.v_ref, bf16[1280,1536]{1,0:T(8,128)(2,1)} %pad_maximum_fusion.1.k_ref.v_ref, s32[6,256]{1,0:T(8,128)} %bitcast.253, s32[6,256]{1,0:T(8,128)} %bitcast.250), custom_call_target="tpu_custom_call" | custom-call | flops 30000001024 | bytes 100000 | tf_op jit(solution)/shard_map/attend/pallas_call | solution.py:256
  182.4 5.3 pack.2
  198.5 16.2 %collective-permute-done.24 = bf16[2,96,1536]{2,1,0:T(8,128)(2,1)S(1)} collective-permute-done((bf16[2,96,1536]{2,1,0:T(8,128)(2,1)S(1)}, bf16[2,96,1536]{2,1,0:T(8,128)(2,1)S(1)}, u32[]{:S(2)}, u32[]{:S(2)}) %collective-permute-start.24) | collective-permute-done | bytes 589856 | tf_op jit(solution)/shard_map/ppermute | solution.py:56
  226.8 16.1 %collective-permute-done.17.refs_3_ = bf16[480,768]{1,0:T(8,128)(2,1)} collective-permute-done((bf16[480,768]{1,0:T(8,128)(2,1)S(1)}, bf16[480,768]{1,0:T(8,128)(2,1)}, u32[]{:S(2)}, u32[]{:S(2)}) %collective-permute-start.17) | collective-permute-done | bytes 737312 | tf_op jit(solution)/shard_map/ppermute | solution.py:34
  242.9 46.1 %expert.2 = (f32[1920,768]{1,0:T(8,128)}, f32[1920,768]{1,0:T(8,128)}, bf16[2,768,1536]{2,1,0:T(8,128)(2,1)}) custom-call(s32[4]{0:T(128)} %pad_add_fusion.place_ref, bf16[768,128]{1,0:T(8,128)(2,1)} %pad.16.router_ref, bf16[480,768]{1,0:T(8,128)(2,1)} %get-tuple-element.225.refs_0_, bf16[480,768]{1,0:T(8,128)(2,1)} %collective-permute-done.15.refs_1_, ...), custom_call_target="tpu_custom_call" | custom-call | flops 51999997952 | bytes 100000 | tf_op jit(solution)/shard_map/expert/pallas_call | solution.py:547
  292.3 47.7 %expert.3 = (bf16[4,480,768]{2,1,0:T(8,128)(2,1)}, bf16[4,496,768]{2,1,0:T(8,128)(2,1)}, bf16[2,768,1536]{2,1,0:T(8,128)(2,1)}) custom-call(s32[4]{0:T(128)} %pad_add_fusion.place_ref, bf16[768,128]{1,0:T(8,128)(2,1)} %pad.16.router_ref, bf16[480,768]{1,0:T(8,128)(2,1)} %get-tuple-element.225.refs_0_, bf16[480,768]{1,0:T(8,128)(2,1)} %collective-permute-done.15.refs_1_, ...), custom_call_target="tpu_custom_call" | custom-call | flops 51999997952 | bytes 100000 | tf_op jit(solution)/shard_map/expert/pallas_call | solution.py:547
  352.3 10.2 %collective-permute-done.29.refs_2_ = bf16[496,768]{1,0:T(8,128)(2,1)S(1)} collective-permute-done((bf16[496,768]{1,0:T(8,128)(2,1)S(1)}, bf16[496,768]{1,0:T(8,128)(2,1)S(1)}, u32[]{:S(2)}, u32[]{:S(2)}) %collective-permute-start.29) | collective-permute-done | bytes 761888 | tf_op jit(solution)/shard_map/ppermute | solution.py:34
  362.5 16.7 %collective-permute-done.30.refs_3_ = bf16[496,768]{1,0:T(8,128)(2,1)S(1)} collective-permute-done((bf16[496,768]{1,0:T(8,128)(2,1)S(1)}, bf16[496,768]{1,0:T(8,128)(2,1)S(1)}, u32[]{:S(2)}, u32[]{:S(2)}) %collective-permute-start.30) | collective-permute-done | bytes 761888 | tf_op jit(solution)/shard_map/ppermute | solution.py:34
  380.1 7.1 unpack_grad.1
  401.1 20.7 %collective-permute-done.35.refs_0_ = bf16[2,96,1536]{2,1,0:T(8,128)(2,1)S(1)} collective-permute-done((bf16[2,96,1536]{2,1,0:T(8,128)(2,1)S(1)}, bf16[2,96,1536]{2,1,0:T(8,128)(2,1)S(1)}, u32[]{:S(2)}, u32[]{:S(2)}) %collective-permute-start.35) | collective-permute-done | bytes 589856 | tf_op jit(solution)/shard_map/ppermute | solution.py:56
  422.6 14.0 %attend_back.2 = (bf16[768,384]{1,0:T(8,128)(2,1)}, bf16[1280,384]{1,0:T(8,128)(2,1)}, bf16[1280,384]{1,0:T(8,128)(2,1)}) custom-call(bf16[768,2304]{1,0:T(8,128)(2,1)} %copy-done.24, bf16[1280,1536]{1,0:T(8,128)(2,1)} %pad_maximum_fusion.1.k_ref.v_ref, bf16[1280,1536]{1,0:T(8,128)(2,1)} %pad_maximum_fusion.1.k_ref.v_ref, ...), custom_call_target="tpu_custom_call" | custom-call | flops 15000000512 | bytes 100000 | tf_op jit(solution)/shard_map/attend_back/pallas_call | solution.py:288
  438.9 4.5 add_convert_fusion.1.refs_0_
  444.2 13.6 %attend_back.3 = (bf16[768,384]{1,0:T(8,128)(2,1)}, bf16[1280,384]{1,0:T(8,128)(2,1)}, bf16[1280,384]{1,0:T(8,128)(2,1)}) custom-call(bf16[768,2304]{1,0:T(8,128)(2,1)} %copy-done.24, bf16[1280,1536]{1,0:T(8,128)(2,1)} %pad_maximum_fusion.1.k_ref.v_ref, bf16[1280,1536]{1,0:T(8,128)(2,1)} %pad_maximum_fusion.1.k_ref.v_ref, ...), custom_call_target="tpu_custom_call" | custom-call | flops 15000000512 | bytes 100000 | tf_op jit(solution)/shard_map/attend_back/pallas_call | solution.py:288
  472.6 28.4 %collective-permute-done.38 = bf16[256,1536]{1,0:T(8,128)(2,1)S(1)} collective-permute-done((bf16[256,1536]{1,0:T(8,128)(2,1)S(1)}, bf16[256,1536]{1,0:T(8,128)(2,1)S(1)}, u32[]{:S(2)}, u32[]{:S(2)}) %collective-permute-start.38) | collective-permute-done | bytes 786464 | tf_op jit(solution)/shard_map/ppermute | solution.py:45
  505.4 5.4 fusion.25
  544.4 13.2 %collective-permute-done.34.refs_3_ = bf16[480,768]{1,0:T(8,128)(2,1)} collective-permute-done((bf16[480,768]{1,0:T(8,128)(2,1)}, bf16[480,768]{1,0:T(8,128)(2,1)}, u32[]{:S(2)}, u32[]{:S(2)}) %collective-permute-start.34) | collective-permute-done | bytes 737312 | tf_op jit(solution)/shard_map/ppermute | solution.py:34
  558.1 7.3 %unpack_out.1 = bf16[768,768]{1,0:T(8,128)(2,1)} custom-call(f32[768,768]{1,0:T(8,128)} %copy-done, bf16[480,768]{1,0:T(8,128)(2,1)} %get-tuple-element.217.refs_0_, bf16[480,768]{1,0:T(8,128)(2,1)} %copy-done.46, bf16[480,768]{1,0:T(8,128)(2,1)} %collective-permute-done.33.refs_2_, bf16[480,768]{1,0:T(8,128)(2,1)} %collective-permute-done.34.refs_3_, ...), custom_call_target="tpu_custom_call" | custom-call | tf_op jit(solution)/shard_map/unpack_out/pallas_call | solution.py:408
  573.9 24.5 %collective-permute-done.42 = bf16[96,1664]{1,0:T(8,128)(2,1)S(1)} collective-permute-done((bf16[96,1664]{1,0:T(8,128)(2,1)S(1)}, bf16[96,1664]{1,0:T(8,128)(2,1)S(1)}, u32[]{:S(2)}, u32[]{:S(2)}) %collective-permute-start.42) | collective-permute-done | bytes 319520 | tf_op jit(solution)/shard_map/ppermute | solution.py:56
  599.9 31.3 %collective-permute-done.43 = bf16[96,1664]{1,0:T(8,128)(2,1)S(1)} collective-permute-done((bf16[96,1664]{1,0:T(8,128)(2,1)S(1)}, bf16[96,1664]{1,0:T(8,128)(2,1)S(1)}, u32[]{:S(2)}, u32[]{:S(2)}) %collective-permute-start.43) | collective-permute-done | bytes 319520 | tf_op jit(solution)/shard_map/ppermute | solution.py:56
  631.2 8.0 %collective-permute-done.44 = bf16[96,1664]{1,0:T(8,128)(2,1)S(1)} collective-permute-done((bf16[96,1664]{1,0:T(8,128)(2,1)S(1)}, bf16[96,1664]{1,0:T(8,128)(2,1)S(1)}, u32[]{:S(2)}, u32[]{:S(2)}) %collective-permute-start.44) | collective-permute-done | bytes 319520 | tf_op jit(solution)/shard_map/ppermute | solution.py:56
  642.8 5.8 collective-permute-done.45
  654.9 24.8 %collective-permute-done.52 = bf16[2,96,3072]{2,1,0:T(8,128)(2,1)} collective-permute-done((bf16[2,96,3072]{2,1,0:T(8,128)(2,1)}, bf16[2,96,3072]{2,1,0:T(8,128)(2,1)}, u32[]{:S(2)}, u32[]{:S(2)}) %collective-permute-start.52) | collective-permute-done | bytes 1179680 | tf_op jit(solution)/shard_map/ppermute | solution.py:34
  701.4 8.4 %multiply_subtract_fusion = (f32[4,3072,96]{1,2,0:T(8,128)}, f32[4,3072,96]{1,2,0:T(8,128)}, f32[4,3072,96]{1,2,0:T(8,128)}) fusion(f32[4,3072,96]{1,2,0:T(8,128)S(1)} %bitcast.226, f32[4,2,96,3072]{3,2,1,0:T(8,128)S(1)} %maximum_convert_fusion, f32[4,3072,96]{1,2,0:T(8,128)S(1)} %bitcast.235, f32[4,3072,96]{1,2,0:T(8,128)} %param.42), kind=kLoop, calls=%fused_computation.20 | loop fusion | flops 17694720 | bytes 33030144 | tf_op jit(solution)/shard_map/sub | solution.py:175
  709.8 8.9 %multiply_subtract_fusion.1 = (f32[4,96,3072]{2,1,0:T(8,128)}, f32[4,96,3072]{2,1,0:T(8,128)}, f32[4,96,3072]{2,1,0:T(8,128)}) fusion(f32[4,96,3072]{2,1,0:T(8,128)S(1)} %bitcast.228, f32[4,2,96,3072]{3,2,1,0:T(8,128)S(1)} %maximum_convert_fusion, f32[4,96,3072]{2,1,0:T(8,128)} %param.40, f32[4,96,3072]{2,1,0:T(8,128)} %param.39), kind=kLoop, calls=%fused_computation.22 | loop fusion | flops 17694720 | bytes 33030144 | tf_op jit(solution)/shard_map/sub | solution.py:175
  (453 shorter events, 224.5 us)
Async XLA Ops:
  7.7 48.1 %collective-permute-start.7 = (bf16[96,512]{1,0:T(8,128)(2,1)}, bf16[96,512]{1,0:T(8,128)(2,1)S(1)}, u32[]{:S(2)}, u32[]{:S(2)}) collective-permute-start(bf16[96,512]{1,0:T(8,128)(2,1)} %get-tuple-element.252), channel_id=1, source_target_pairs={{0,2},{1,3},{2,0},{3,1},{4,6},{5,7},{6,4},{7,5},{8,10},{9,11},{10,... | collective-permute-start | bytes 294920 | tf_op jit(solution)/shard_map/ppermute | solution.py:56
  9.2 47.7 %collective-permute-start.8 = (bf16[96,512]{1,0:T(8,128)(2,1)}, bf16[96,512]{1,0:T(8,128)(2,1)}, u32[]{:S(2)}, u32[]{:S(2)}) collective-permute-start(bf16[96,512]{1,0:T(8,128)(2,1)} %get-tuple-element.252), channel_id=1, source_target_pairs={{0,4},{1,5},{2,6},{3,7},{4,0},{5,1},{6,2},{7,3},{8,12},{9,13},{10,... | collective-permute-start | bytes 294920 | tf_op jit(solution)/shard_map/ppermute | solution.py:56
  29.5 39.7 %collective-permute-start.4 = (bf16[4,96,1280]{2,1,0:T(8,128)(2,1)S(1)}, bf16[4,96,1280]{2,1,0:T(8,128)(2,1)}, u32[]{:S(2)}, u32[]{:S(2)}) collective-permute-start(bf16[4,96,1280]{2,1,0:T(8,128)(2,1)S(1)} %pad_maximum_fusion.8.refs_0_), channel_id=1, source_target_pairs={{0,8},{8,0},{16,24},{24,16},{1,9},{9,1},{17,25},{25,17},{2,10},{10... | collective-permute-start | bytes 2949128 | tf_op jit(solution)/shard_map/ppermute | solution.py:34
  82.7 58.0 %collective-permute-start.10 = (bf16[256,1536]{1,0:T(8,128)(2,1)}, bf16[256,1536]{1,0:T(8,128)(2,1)}, u32[]{:S(2)}, u32[]{:S(2)}) collective-permute-start(bf16[256,1536]{1,0:T(8,128)(2,1)} %get-tuple-element.208), channel_id=1, source_target_pairs={{0,1},{1,2},{2,3},{3,4},{4,5},{5,6},{6,7},{7,8},{8,9},{9,10},{10,1... | collective-permute-start | bytes 2359304 | tf_op jit(solution)/shard_map/ppermute | solution.py:45
  90.2 53.9 %collective-permute-start.11 = (bf16[256,1536]{1,0:T(8,128)(2,1)S(1)}, bf16[256,1536]{1,0:T(8,128)(2,1)}, u32[]{:S(2)}, u32[]{:S(2)}) collective-permute-start(bf16[256,1536]{1,0:T(8,128)(2,1)S(1)} %get-tuple-element.209), channel_id=1, source_target_pairs={{1,0},{2,1},{3,2},{4,3},{5,4},{6,5},{7,6},{8,7},{9,8},{10,9},{11,1... | collective-permute-start | bytes 2359304 | tf_op jit(solution)/shard_map/ppermute | solution.py:45
  92.1 36.2 %collective-permute-start.21 = (bf16[2,96,1536]{2,1,0:T(8,128)(2,1)S(1)}, bf16[2,96,1536]{2,1,0:T(8,128)(2,1)S(1)}, u32[]{:S(2)}, u32[]{:S(2)}) collective-permute-start(bf16[2,96,1536]{2,1,0:T(8,128)(2,1)S(1)} %copy-done.17), channel_id=1, source_target_pairs={{0,6},{1,7},{2,4},{3,5},{4,2},{5,3},{6,0},{7,1},{8,14},{9,15},{10,... | collective-permute-start | bytes 1769480 | tf_op jit(solution)/shard_map/ppermute | solution.py:56
  92.3 37.7 %collective-permute-start.13 = (bf16[4,96,512]{2,1,0:T(8,128)(2,1)S(1)}, bf16[4,96,512]{2,1,0:T(8,128)(2,1)S(1)}, u32[]{:S(2)}, u32[]{:S(2)}) collective-permute-start(bf16[4,96,512]{2,1,0:T(8,128)(2,1)S(1)} %pad_maximum_fusion.12.refs_0_), channel_id=1, source_target_pairs={{0,8},{8,0},{16,24},{24,16},{1,9},{9,1},{17,25},{25,17},{2,10},{10... | collective-permute-start | bytes 1179656 | tf_op jit(solution)/shard_map/ppermute | solution.py:34
  93.7 41.9 %collective-permute-start.14 = (bf16[4,96,512]{2,1,0:T(8,128)(2,1)S(1)}, bf16[4,96,512]{2,1,0:T(8,128)(2,1)}, u32[]{:S(2)}, u32[]{:S(2)}) collective-permute-start(bf16[4,96,512]{2,1,0:T(8,128)(2,1)S(1)} %collective-permute-done.12.refs_1_), channel_id=1, source_target_pairs={{0,8},{8,0},{16,24},{24,16},{1,9},{9,1},{17,25},{25,17},{2,10},{10... | collective-permute-start | bytes 1179656 | tf_op jit(solution)/shard_map/ppermute | solution.py:34
  128.3 51.6 %collective-permute-start.18 = (bf16[480,768]{1,0:T(8,128)(2,1)}, bf16[480,768]{1,0:T(8,128)(2,1)}, u32[]{:S(2)}, u32[]{:S(2)}) collective-permute-start(bf16[480,768]{1,0:T(8,128)(2,1)} %get-tuple-element.220), channel_id=1, source_target_pairs={{0,8},{8,0},{16,24},{24,16},{1,9},{9,1},{17,25},{25,17},{2,10},{10... | collective-permute-start | bytes 2211848 | tf_op jit(solution)/shard_map/ppermute | solution.py:34
  130.0 60.9 %collective-permute-start.19 = (bf16[480,768]{1,0:T(8,128)(2,1)}, bf16[480,768]{1,0:T(8,128)(2,1)}, u32[]{:S(2)}, u32[]{:S(2)}) collective-permute-start(bf16[480,768]{1,0:T(8,128)(2,1)} %get-tuple-element.219), channel_id=1, source_target_pairs={{0,16},{8,24},{16,0},{24,8},{1,17},{9,25},{17,1},{25,9},{2,18},{10... | collective-permute-start | bytes 2211848 | tf_op jit(solution)/shard_map/ppermute | solution.py:34
  135.6 37.6 %collective-permute-start.26 = (bf16[2,96,1536]{2,1,0:T(8,128)(2,1)S(1)}, bf16[2,96,1536]{2,1,0:T(8,128)(2,1)S(1)}, u32[]{:S(2)}, u32[]{:S(2)}) collective-permute-start(bf16[2,96,1536]{2,1,0:T(8,128)(2,1)S(1)} %copy-done.17), channel_id=1, source_target_pairs={{0,4},{1,5},{2,6},{3,7},{4,0},{5,1},{6,2},{7,3},{8,12},{9,13},{10,... | collective-permute-start | bytes 1769480 | tf_op jit(solution)/shard_map/ppermute | solution.py:56
  140.6 53.5 %collective-permute-start.22 = (bf16[2,96,1536]{2,1,0:T(8,128)(2,1)S(1)}, bf16[2,96,1536]{2,1,0:T(8,128)(2,1)S(1)}, u32[]{:S(2)}, u32[]{:S(2)}) collective-permute-start(bf16[2,96,1536]{2,1,0:T(8,128)(2,1)S(1)} %copy-done.16), channel_id=1, source_target_pairs={{0,2},{1,3},{2,0},{3,1},{4,6},{5,7},{6,4},{7,5},{8,10},{9,11},{10,... | collective-permute-start | bytes 1769480 | tf_op jit(solution)/shard_map/ppermute | solution.py:56
  144.1 54.0 %collective-permute-start.23 = (bf16[2,96,1536]{2,1,0:T(8,128)(2,1)S(1)}, bf16[2,96,1536]{2,1,0:T(8,128)(2,1)S(1)}, u32[]{:S(2)}, u32[]{:S(2)}) collective-permute-start(bf16[2,96,1536]{2,1,0:T(8,128)(2,1)S(1)} %copy-done.16), channel_id=1, source_target_pairs={{0,4},{1,5},{2,6},{3,7},{4,0},{5,1},{6,2},{7,3},{8,12},{9,13},{10,... | collective-permute-start | bytes 1769480 | tf_op jit(solution)/shard_map/ppermute | solution.py:56
  177.3 65.6 %collective-permute-start.27 = (bf16[4,2,96,1536]{3,2,1,0:T(8,128)(2,1)}, bf16[4,2,96,1536]{3,2,1,0:T(8,128)(2,1)}, u32[]{:S(2)}, u32[]{:S(2)}) collective-permute-start(bf16[4,2,96,1536]{3,2,1,0:T(8,128)(2,1)} %pad_maximum_fusion.4.refs_8_), channel_id=1, source_target_pairs={{0,1},{1,0},{2,3},{3,2},{4,5},{5,4},{6,7},{7,6},{8,9},{9,8},{10,11... | collective-permute-start | bytes 7077896 | tf_op jit(solution)/shard_map/ppermute | solution.py:56
  179.9 34.8 %collective-permute-start.24 = (bf16[2,96,1536]{2,1,0:T(8,128)(2,1)S(1)}, bf16[2,96,1536]{2,1,0:T(8,128)(2,1)S(1)}, u32[]{:S(2)}, u32[]{:S(2)}) collective-permute-start(bf16[2,96,1536]{2,1,0:T(8,128)(2,1)S(1)} %copy-done.16), channel_id=1, source_target_pairs={{0,6},{1,7},{2,4},{3,5},{4,2},{5,3},{6,0},{7,1},{8,14},{9,15},{10,... | collective-permute-start | bytes 1769480 | tf_op jit(solution)/shard_map/ppermute | solution.py:56
  190.9 34.0 %collective-permute-start.20 = (bf16[480,768]{1,0:T(8,128)(2,1)S(1)}, bf16[480,768]{1,0:T(8,128)(2,1)}, u32[]{:S(2)}, u32[]{:S(2)}) collective-permute-start(bf16[480,768]{1,0:T(8,128)(2,1)S(1)} %copy-done.45), channel_id=1, source_target_pairs={{0,24},{8,16},{16,8},{24,0},{1,25},{9,17},{17,9},{25,1},{2,26},{10... | collective-permute-start | bytes 2211848 | tf_op jit(solution)/shard_map/ppermute | solution.py:34
  224.9 67.4 %collective-permute-start.25 = (bf16[4,2,96,1536]{3,2,1,0:T(8,128)(2,1)}, bf16[4,2,96,1536]{3,2,1,0:T(8,128)(2,1)}, u32[]{:S(2)}, u32[]{:S(2)}) collective-permute-start(bf16[4,2,96,1536]{3,2,1,0:T(8,128)(2,1)} %pad_maximum_fusion.3.refs_10_.refs_8_), channel_id=1, source_target_pairs={{0,1},{1,0},{2,3},{3,2},{4,5},{5,4},{6,7},{7,6},{8,9},{9,8},{10,11... | collective-permute-start | bytes 7077896 | tf_op jit(solution)/shard_map/ppermute | solution.py:56
  292.3 56.3 %collective-permute-start.31 = (bf16[2,4,96,1536]{3,2,1,0:T(8,128)(2,1)}, bf16[2,4,96,1536]{3,2,1,0:T(8,128)(2,1)}, u32[]{:S(2)}, u32[]{:S(2)}) collective-permute-start(bf16[2,4,96,1536]{3,2,1,0:T(8,128)(2,1)} %dynamic-slice_bitcast_fusion.2), channel_id=1, source_target_pairs={{0,1},{1,0},{2,3},{3,2},{4,5},{5,4},{6,7},{7,6},{8,9},{9,8},{10,11... | collective-permute-start | bytes 7077896 | tf_op jit(solution)/shard_map/ppermute | solution.py:56
  344.6 34.6 %collective-permute-start.30 = (bf16[496,768]{1,0:T(8,128)(2,1)S(1)}, bf16[496,768]{1,0:T(8,128)(2,1)S(1)}, u32[]{:S(2)}, u32[]{:S(2)}) collective-permute-start(bf16[496,768]{1,0:T(8,128)(2,1)S(1)} %get-tuple-element.210), channel_id=1, source_target_pairs={{0,24},{8,16},{16,8},{24,0},{1,25},{9,17},{17,9},{25,1},{2,26},{10... | collective-permute-start | bytes 2285576 | tf_op jit(solution)/shard_map/ppermute | solution.py:34
  347.2 91.6 %collective-permute-start.36 = (bf16[2,4,96,1536]{3,2,1,0:T(8,128)(2,1)S(1)}, bf16[2,4,96,1536]{3,2,1,0:T(8,128)(2,1)}, u32[]{:S(2)}, u32[]{:S(2)}) collective-permute-start(bf16[2,4,96,1536]{3,2,1,0:T(8,128)(2,1)S(1)} %get-tuple-element.203), channel_id=1, source_target_pairs={{0,1},{1,0},{2,3},{3,2},{4,5},{5,4},{6,7},{7,6},{8,9},{9,8},{10,11... | collective-permute-start | bytes 7077896 | tf_op jit(solution)/shard_map/ppermute | solution.py:56
  396.9 46.5 %collective-permute-start.37 = (bf16[2,96,1536]{2,1,0:T(8,128)(2,1)}, bf16[2,96,1536]{2,1,0:T(8,128)(2,1)S(1)}, u32[]{:S(2)}, u32[]{:S(2)}) collective-permute-start(bf16[2,96,1536]{2,1,0:T(8,128)(2,1)} %get-tuple-element.228), channel_id=1, source_target_pairs={{0,4},{1,5},{2,6},{3,7},{4,0},{5,1},{6,2},{7,3},{8,12},{9,13},{10,... | collective-permute-start | bytes 1769480 | tf_op jit(solution)/shard_map/ppermute | solution.py:56
  463.8 37.2 %collective-permute-start.38 = (bf16[256,1536]{1,0:T(8,128)(2,1)S(1)}, bf16[256,1536]{1,0:T(8,128)(2,1)S(1)}, u32[]{:S(2)}, u32[]{:S(2)}) collective-permute-start(bf16[256,1536]{1,0:T(8,128)(2,1)S(1)} %get-tuple-element.204), channel_id=1, source_target_pairs={{0,1},{1,2},{2,3},{3,4},{4,5},{5,6},{6,7},{7,8},{8,9},{9,10},{10,1... | collective-permute-start | bytes 2359304 | tf_op jit(solution)/shard_map/ppermute | solution.py:45
  468.2 33.1 %collective-permute-start.39 = (bf16[256,1536]{1,0:T(8,128)(2,1)S(1)}, bf16[256,1536]{1,0:T(8,128)(2,1)S(1)}, u32[]{:S(2)}, u32[]{:S(2)}) collective-permute-start(bf16[256,1536]{1,0:T(8,128)(2,1)S(1)} %get-tuple-element.205), channel_id=1, source_target_pairs={{1,0},{2,1},{3,2},{4,3},{5,4},{6,5},{7,6},{8,7},{9,8},{10,9},{11,1... | collective-permute-start | bytes 2359304 | tf_op jit(solution)/shard_map/ppermute | solution.py:45
  523.5 34.0 %collective-permute-start.34 = (bf16[480,768]{1,0:T(8,128)(2,1)}, bf16[480,768]{1,0:T(8,128)(2,1)}, u32[]{:S(2)}, u32[]{:S(2)}) collective-permute-start(bf16[480,768]{1,0:T(8,128)(2,1)} %get-tuple-element.214), channel_id=1, source_target_pairs={{0,24},{8,16},{16,8},{24,0},{1,25},{9,17},{17,9},{25,1},{2,26},{10... | collective-permute-start | bytes 2211848 | tf_op jit(solution)/shard_map/ppermute | solution.py:34
  530.6 34.8 %collective-permute-start.41 = (bf16[4,96,1664]{2,1,0:T(8,128)(2,1)}, bf16[4,96,1664]{2,1,0:T(8,128)(2,1)}, u32[]{:S(2)}, u32[]{:S(2)}) collective-permute-start(bf16[4,96,1664]{2,1,0:T(8,128)(2,1)} %dynamic-slice_bitcast_fusion.3), channel_id=1, source_target_pairs={{0,1},{1,0},{2,3},{3,2},{4,5},{5,4},{6,7},{7,6},{8,9},{9,8},{10,11... | collective-permute-start | bytes 3833864 | tf_op jit(solution)/shard_map/ppermute | solution.py:56
  533.4 40.4 %collective-permute-start.47 = (bf16[2,96,1536]{2,1,0:T(8,128)(2,1)}, bf16[2,96,1536]{2,1,0:T(8,128)(2,1)}, u32[]{:S(2)}, u32[]{:S(2)}) collective-permute-start(bf16[2,96,1536]{2,1,0:T(8,128)(2,1)} %get-tuple-element.227), channel_id=1, source_target_pairs={{0,6},{1,7},{2,4},{3,5},{4,2},{5,3},{6,0},{7,1},{8,14},{9,15},{10,... | collective-permute-start | bytes 1769480 | tf_op jit(solution)/shard_map/ppermute | solution.py:56
  539.8 101.6 %collective-permute-start.48 = (bf16[2,96,1536]{2,1,0:T(8,128)(2,1)}, bf16[2,96,1536]{2,1,0:T(8,128)(2,1)S(1)}, u32[]{:S(2)}, u32[]{:S(2)}) collective-permute-start(bf16[2,96,1536]{2,1,0:T(8,128)(2,1)} %get-tuple-element.233), channel_id=1, source_target_pairs={{0,2},{1,3},{2,0},{3,1},{4,6},{5,7},{6,4},{7,5},{8,10},{9,11},{10,... | collective-permute-start | bytes 1769480 | tf_op jit(solution)/shard_map/ppermute | solution.py:56
  544.1 97.3 %collective-permute-start.49 = (bf16[2,96,1536]{2,1,0:T(8,128)(2,1)}, bf16[2,96,1536]{2,1,0:T(8,128)(2,1)S(1)}, u32[]{:S(2)}, u32[]{:S(2)}) collective-permute-start(bf16[2,96,1536]{2,1,0:T(8,128)(2,1)} %get-tuple-element.232), channel_id=1, source_target_pairs={{0,4},{1,5},{2,6},{3,7},{4,0},{5,1},{6,2},{7,3},{8,12},{9,13},{10,... | collective-permute-start | bytes 1769480 | tf_op jit(solution)/shard_map/ppermute | solution.py:56
  557.6 83.8 %collective-permute-start.50 = (bf16[2,96,1536]{2,1,0:T(8,128)(2,1)}, bf16[2,96,1536]{2,1,0:T(8,128)(2,1)S(1)}, u32[]{:S(2)}, u32[]{:S(2)}) collective-permute-start(bf16[2,96,1536]{2,1,0:T(8,128)(2,1)} %get-tuple-element.231), channel_id=1, source_target_pairs={{0,6},{1,7},{2,4},{3,5},{4,2},{5,3},{6,0},{7,1},{8,14},{9,15},{10,... | collective-permute-start | bytes 1769480 | tf_op jit(solution)/shard_map/ppermute | solution.py:56
  573.8 57.4 %collective-permute-start.43 = (bf16[96,1664]{1,0:T(8,128)(2,1)S(1)}, bf16[96,1664]{1,0:T(8,128)(2,1)S(1)}, u32[]{:S(2)}, u32[]{:S(2)}) collective-permute-start(bf16[96,1664]{1,0:T(8,128)(2,1)S(1)} %get-tuple-element.236), channel_id=1, source_target_pairs={{0,4},{1,5},{2,6},{3,7},{4,0},{5,1},{6,2},{7,3},{8,12},{9,13},{10,... | collective-permute-start | bytes 958472 | tf_op jit(solution)/shard_map/ppermute | solution.py:56
  598.4 40.8 %collective-permute-start.44 = (bf16[96,1664]{1,0:T(8,128)(2,1)S(1)}, bf16[96,1664]{1,0:T(8,128)(2,1)S(1)}, u32[]{:S(2)}, u32[]{:S(2)}) collective-permute-start(bf16[96,1664]{1,0:T(8,128)(2,1)S(1)} %get-tuple-element.235), channel_id=1, source_target_pairs={{0,6},{1,7},{2,4},{3,5},{4,2},{5,3},{6,0},{7,1},{8,14},{9,15},{10,... | collective-permute-start | bytes 958472 | tf_op jit(solution)/shard_map/ppermute | solution.py:56
  652.8 42.5 %collective-permute-start.51 = (bf16[2,96,3072]{2,1,0:T(8,128)(2,1)}, bf16[2,96,3072]{2,1,0:T(8,128)(2,1)}, u32[]{:S(2)}, u32[]{:S(2)}) collective-permute-start(bf16[2,96,3072]{2,1,0:T(8,128)(2,1)} %get-tuple-element.238), channel_id=1, source_target_pairs={{0,8},{8,0},{16,24},{24,16},{1,9},{9,1},{17,25},{25,17},{2,10},{10... | collective-permute-start | bytes 3538952 | tf_op jit(solution)/shard_map/ppermute | solution.py:34
  (121 other events, 1490.8 us)

commit v4 on v3

--- a/solution.py
+++ b/solution.py
@@ -23,7 +23,7 @@
 CHIP_BIT = 2
 F32 = jnp.float32
 BF16 = jnp.bfloat16
-EXPERT_COST = pl.CostEstimate(flops=52 * 10**9, bytes_accessed=10**5, transcendentals=0)
+EXPERT_COST = pl.CostEstimate(flops=28 * 10**9, bytes_accessed=10**5, transcendentals=0)
 ATTEND_COST = pl.CostEstimate(flops=30 * 10**9, bytes_accessed=10**5, transcendentals=0)
 BACK_COST = pl.CostEstimate(flops=15 * 10**9, bytes_accessed=10**5, transcendentals=0)
 NT = (((1,), (1,)), ((), ()))
@@ -320,34 +320,35 @@
 
 
 def gelu_both(pre):
-    below = 0.5 + 0.5 * lax.erf(pre * (0.5**0.5))
-    density = jnp.exp(pre * pre * -0.5) * 0.3989422804014327
-    return pre * below, below + pre * density
-
-
-def pack_kernel(rows_ref, rank_ref, *refs):
-    out_ref = refs[-1]
-    slots, tokens = out_ref.shape[1], rows_ref.shape[0]
+    bell = jnp.exp(pre * pre * -0.5)
+    t = 1.0 / (1.0 + jnp.abs(pre) * (0.3275911 * 0.5**0.5))
+    tail = 1.061405429 * t - 1.453152027
+    tail = tail * t + 1.421413741
+    tail = tail * t - 0.284496736
+    tail = (tail * t + 0.254829592) * t * (0.5 * bell)
+    below = jnp.where(pre < 0.0, tail, 1.0 - tail)
+    return pre * below, below + pre * (bell * 0.3989422804014327)
+
+
+def pack_kernel(rows_ref, rank_ref, *out_refs):
+    slots, tokens = out_refs[0].shape[0], rows_ref.shape[0]
     slot = lax.broadcasted_iota(jnp.int32, (slots, tokens), 0)
-    spots = jnp.where(slot == rank_ref[0], 1.0, 0.0).astype(BF16)
-    out_ref[0] = jnp.dot(spots, rows_ref[...], preferred_element_type=F32).astype(BF16)
+    for at, out_ref in enumerate(out_refs):
+        spots = jnp.where(slot == rank_ref[at : at + 1, :], 1.0, 0.0).astype(BF16)
+        out_ref[...] = jnp.dot(spots, rows_ref[...], preferred_element_type=F32).astype(BF16)
 
 
 def pack(rows, ranks, slots):
-    tokens, width = rows.shape
-    count = ranks.shape[0]
+    count, width = ranks.shape[0], rows.shape[1]
+    near_by = pl.BlockSpec(memory_space=pltpu.VMEM)
     return pl.pallas_call(
         pack_kernel,
-        grid=(count,),
-        in_specs=[
-            pl.BlockSpec((tokens, width), lambda e: (0, 0)),
-            pl.BlockSpec((1, 1, tokens), lambda e: (e, 0, 0)),
-        ],
-        out_specs=pl.BlockSpec((1, slots, width), lambda e: (e, 0, 0)),
-        out_shape=jax.ShapeDtypeStruct((count, slots, width), BF16),
+        in_specs=[near_by, near_by],
+        out_specs=[near_by] * count,
+        out_shape=[jax.ShapeDtypeStruct((slots, width), BF16)] * count,
         compiler_params=pltpu.CompilerParams(vmem_limit_bytes=56 * 2**20),
         name="pack",
-    )(rows, ranks.reshape(count, 1, tokens))
+    )(rows, ranks)
 
 
 def token_spots(rank_col, slots):
@@ -415,18 +416,34 @@
     )(residual, *parts, *rank_cols, *gate_cols, *after)
 
 
-def expert_kernel(count, near, first, expert_count, place_ref, router_ref, *refs):
-    x_parts, dy_parts = refs[:count], refs[count : 2 * count]
-    sources = refs[2 * count : 2 * count + near]
-    refs = refs[2 * count + near :]
-    before, refs = (None, refs) if first else (refs[:2], refs[2:])
-    out_ref, xgrad_ref, grad_ref = refs[-15:-12]
-    weights, arrived, part_sems, x_rows, xt_rows, g_rows, gt_rows, dy_rows = refs[-12:-4]
-    act_rows, pg_rows, eout, xgrad = refs[-4:]
+def expert_kernel(count, others, near, first, expert_count, place_ref, router_ref, *refs):
+    refs = list(refs)
+
+    def take(number):
+        taken = refs[:number]
+        del refs[:number]
+        return taken
+
+    x_parts, dy_parts, sources = take(count), take(count), take(near)
+    with_grads = others > 0
+    before = [[], [], []] if first else [take(count), take(count), take(count)]
+    other_x, other_g, other_act, other_pg = take(others), take(others), take(others), take(others)
+    scratch = 9 if first else 11
+    scratch_refs = refs[-scratch:]
+    outs = refs[:-scratch]
+    outs = outs[-(3 if first else 2) * count - (1 if with_grads else 2 * count) :]
+    weights, arrived, part_sems, x_rows, g_rows, dy_rows, xt_rows, gt_rows, both_rows = scratch_refs[:9]
+    act_rows, pg_rows = both_rows.at[0], both_rows.at[1]
+    if first:
+        eout, xgrad = outs[:count], outs[count : 2 * count]
+    else:
+        eout = [scratch_refs[9].at[part] for part in range(count)]
+        xgrad = [scratch_refs[10].at[part] for part in range(count)]
     step = pl.program_id(0)
     steps = pl.num_programs(0)
     slots, width = x_parts[0].shape
     hidden = weights.shape[-1]
+    own = count * slots
 
     def fetch(number, slot):
         columns = pl.ds(pl.multiple_of(number * hidden, LANES), hidden)
@@ -452,8 +469,14 @@
             rows = pl.ds(part * slots, slots)
             copies.append((x_parts[part], x_rows.at[rows]))
             copies.append((dy_parts[part], dy_rows.at[rows]))
-        if before is not None:
-            copies += [(before[0], eout), (before[1], xgrad)]
+            if not first:
+                copies.append((before[0][part], eout[part]))
+                copies.append((before[1][part], xgrad[part]))
+                copies.append((before[2][part], g_rows.at[rows]))
+        for part in range(others):
+            rows = pl.ds(own + part * slots, slots)
+            copies.append((other_x[part], x_rows.at[rows]))
+            copies.append((other_g[part], g_rows.at[rows]))
         copies = [
             pltpu.make_async_copy(source, target, part_sems.at[at])
             for at, (source, target) in enumerate(copies)
@@ -462,24 +485,23 @@
             copy.start()
         for copy in copies:
             copy.wait()
-        if before is None:
-            eout[...] = jnp.zeros_like(eout)
-            xgrad[...] = jnp.zeros_like(xgrad)
-
-        def scale_part(part, carry):
-            rows = pl.ds(pl.multiple_of(part * slots, 16), slots)
-            logits = jnp.dot(x_rows[rows, :], router_ref[...], preferred_element_type=F32)
-            lane = lax.broadcasted_iota(jnp.int32, logits.shape, 1)
-            logits = jnp.where(lane < expert_count, logits, MASKED)
-            expo = jnp.exp(logits - jnp.max(logits, axis=1, keepdims=True))
-            mine = jnp.sum(jnp.where(lane == place_ref[3], expo, 0.0), axis=1, keepdims=True)
-            gate = mine / jnp.sum(expo, axis=1, keepdims=True)
-            g_rows[rows, :] = (dy_rows[rows, :].astype(F32) * gate).astype(BF16)
-            return carry
-
-        lax.fori_loop(0, count, scale_part, 0)
-        xt_rows[...] = x_rows[...].T
-        gt_rows[...] = g_rows[...].T
+        if first:
+            for part in range(count):
+                rows = slice(part * slots, (part + 1) * slots)
+                eout[part][...] = jnp.zeros(eout[part].shape, F32)
+                xgrad[part][...] = jnp.zeros(xgrad[part].shape, F32)
+                logits = jnp.dot(x_rows[rows, :], router_ref[...], preferred_element_type=F32)
+                lane = lax.broadcasted_iota(jnp.int32, logits.shape, 1)
+                logits = jnp.where(lane < expert_count, logits, MASKED)
+                expo = jnp.exp(logits - jnp.max(logits, axis=1, keepdims=True))
+                mine = jnp.sum(jnp.where(lane == place_ref[3], expo, 0.0), axis=1, keepdims=True)
+                gate = mine / jnp.sum(expo, axis=1, keepdims=True)
+                weighted = (dy_rows[rows, :].astype(F32) * gate).astype(BF16)
+                g_rows[rows, :] = weighted
+                outs[2 * count + part][...] = weighted
+        if with_grads:
+            xt_rows[...] = x_rows[...].T
+            gt_rows[...] = g_rows[...].T
 
     @pl.when(step + 1 < steps)
     def _():
@@ -490,92 +512,113 @@
         copy.wait()
     inner = weights[slot_of, 0].reshape(width, hidden)
     outer = weights[slot_of, 1].reshape(width, hidden)
-
-    def part_step(part, carry):
-        rows = pl.ds(pl.multiple_of(part * slots, 16), slots)
+    for part in range(count):
+        rows = slice(part * slots, (part + 1) * slots)
         pre = jnp.dot(x_rows[rows, :], inner, preferred_element_type=F32)
         act_grad = jnp.dot(g_rows[rows, :], outer, preferred_element_type=F32)
         act, slope = gelu_both(pre)
         act = act.astype(BF16)
         pre_grad = (act_grad * slope).astype(BF16)
-        act_rows[rows, :] = act
-        pg_rows[rows, :] = pre_grad
-        eout[rows, :] += lax.dot_general(act, outer, NT, preferred_element_type=F32)
-        xgrad[rows, :] += lax.dot_general(pre_grad, inner, NT, preferred_element_type=F32)
-        return carry
-
-    lax.fori_loop(0, count, part_step, 0)
-    grad_ref[0] = jnp.dot(xt_rows[...], pg_rows[...], preferred_element_type=F32).astype(BF16)
-    grad_ref[1] = jnp.dot(gt_rows[...], act_rows[...], preferred_element_type=F32).astype(BF16)
+        if with_grads:
+            act_rows[rows, :] = act
+            pg_rows[rows, :] = pre_grad
+        else:
+            outs[-2 * count + part][...] = act
+            outs[-count + part][...] = pre_grad
+        eout[part][...] += lax.dot_general(act, outer, NT, preferred_element_type=F32)
+        xgrad[part][...] += lax.dot_general(pre_grad, inner, NT, preferred_element_type=F32)
+    if with_grads:
+        grad_ref = outs[-1]
+        for part in range(others):
+            rows = slice(own + part * slots, own + (part + 1) * slots)
+            act_rows[rows, :] = other_act[part][...]
+            pg_rows[rows, :] = other_pg[part][...]
+        grad = jnp.dot(xt_rows[...], pg_rows[...], preferred_element_type=F32)
+        grad_ref[0] = grad.astype(BF16)
+        grad = jnp.dot(gt_rows[...], act_rows[...], preferred_element_type=F32)
+        grad_ref[1] = grad.astype(BF16)
+    if first:
+        return
 
     @pl.when(step == steps - 1)
     def _():
-        if first:
-            out_ref[...] = eout[...]
-            xgrad_ref[...] = xgrad[...]
-            return
         for part in range(count):
+            out_ref, xgrad_ref = outs[part], outs[count + part]
             rows = slice(part * slots, (part + 1) * slots)
-            out = eout[rows, :]
-            out_ref[part] = out.astype(BF16)
-            xgrad_ref[part, :slots, :] = xgrad[rows, :].astype(BF16)
+            out = eout[part][...]
+            out_ref[...] = out.astype(BF16)
+            xgrad_ref[:slots, :] = xgrad[part][...].astype(BF16)
             slot_grad = jnp.sum(dy_rows[rows, :].astype(F32) * out, axis=1, keepdims=True)
             row = jnp.broadcast_to(slot_grad, (slots, LANES)).T[0:1, :]
             row = jnp.concatenate([row, jnp.zeros((1, width - slots), F32)], axis=1)
             high = row.astype(BF16).astype(F32)
             at = lax.broadcasted_iota(jnp.int32, (TAIL, width), 0)
             tail = jnp.where(at == 0, high, jnp.where(at == 1, row - high, 0.0))
-            xgrad_ref[part, slots:, :] = tail.astype(BF16)
-
-
-def expert(place, router, x_parts, dy_parts, sources, expert_count, before=(), after=()):
+            xgrad_ref[slots:, :] = tail.astype(BF16)
+
+
+def expert(
+    place, router, x_parts, dy_parts, sources, expert_count, before=(), other=(), after=()
+):
     count, near = len(x_parts), len(sources)
     slots, width = x_parts[0].shape
     group = lax.axis_size("group")
     columns = sources[0].shape[-1]
     hidden = 512 if columns % 512 == 0 else columns
     raw = pl.BlockSpec(memory_space=pl.ANY)
-    first = len(before) == 0
+    first, with_grads = len(before) == 0, len(other) > 0
+    others = len(other[0]) if with_grads else 0
+    rows = (count + others) * slots
+    sums = jax.ShapeDtypeStruct((slots, width), F32)
+    slot_rows = jax.ShapeDtypeStruct((slots, width), BF16)
     if first:
-        shapes = [jax.ShapeDtypeStruct((count * slots, width), F32)] * 2
+        shapes = [sums] * (2 * count) + [slot_rows] * count
     else:
-        shapes = [
-            jax.ShapeDtypeStruct((count, slots, width), BF16),
-            jax.ShapeDtypeStruct((count, slots + TAIL, width), BF16),
-        ]
-    rows = count * slots
-    return pl.pallas_call(
-        partial(expert_kernel, count, near, first, expert_count),
+        shapes = [slot_rows] * count
+        shapes += [jax.ShapeDtypeStruct((slots + TAIL, width), BF16)] * count
+    out_specs = [pl.BlockSpec(shape.shape, lambda i: (0, 0)) for shape in shapes]
+    hidden_rows = pl.BlockSpec((slots, hidden), lambda i: (0, i))
+    if with_grads:
+        out_specs.append(pl.BlockSpec((2, width, hidden), lambda i: (0, 0, i)))
+        shapes.append(jax.ShapeDtypeStruct((2, width, columns), BF16))
+    else:
+        out_specs += [hidden_rows] * (2 * count)
+        shapes += [jax.ShapeDtypeStruct((slots, columns), BF16)] * (2 * count)
+    turned = (width, rows) if with_grads else (16, LANES)
+    sums_scratch = [] if first else [pltpu.VMEM((count, slots, width), F32)] * 2
+    before = [array for arrays in before for array in arrays]
+    other = [array for arrays in other for array in arrays]
+    outs = pl.pallas_call(
+        partial(expert_kernel, count, others, near, first, expert_count),
         grid=(columns // hidden,),
         in_specs=[
             pl.BlockSpec(memory_space=pltpu.SMEM),
             pl.BlockSpec(router.shape, lambda i: (0, 0), pipeline_mode=pl.Buffered(1)),
-            *[raw] * (2 * count + near + len(before) + len(after)),
-        ],
-        out_specs=[
-            pl.BlockSpec(shapes[0].shape, lambda i: (0,) * len(shapes[0].shape)),
-            pl.BlockSpec(shapes[1].shape, lambda i: (0,) * len(shapes[1].shape)),
-            pl.BlockSpec((2, width, hidden), lambda i: (0, 0, i)),
-        ],
-        out_shape=[*shapes, jax.ShapeDtypeStruct((2, width, columns), BF16)],
+            *[raw] * (2 * count + near + len(before) + 2 * others),
+            *[hidden_rows] * (2 * others),
+            *[raw] * len(after),
+        ],
+        out_specs=out_specs,
+        out_shape=shapes,
         scratch_shapes=[
             pltpu.VMEM((2, 2, group, width // group, hidden), BF16),
             pltpu.SemaphoreType.DMA((2, group)),
-            pltpu.SemaphoreType.DMA((2 * count + 2,)),
+            pltpu.SemaphoreType.DMA((5 * count + 2 * others,)),
             pltpu.VMEM((rows, width), BF16),
-            pltpu.VMEM((width, rows), BF16),
             pltpu.VMEM((rows, width), BF16),
-            pltpu.VMEM((width, rows), BF16),
-            pltpu.VMEM((rows, width), BF16),
-            pltpu.VMEM((rows, hidden), BF16),
-            pltpu.VMEM((rows, hidden), BF16),
-            pltpu.VMEM((rows, width), F32),
-            pltpu.VMEM((rows, width), F32),
+            pltpu.VMEM((count * slots, width), BF16),
+            pltpu.VMEM(turned, BF16),
+            pltpu.VMEM(turned, BF16),
+            pltpu.VMEM((2, rows if with_grads else 16, hidden), BF16),
+            *sums_scratch,
         ],
         compiler_params=pltpu.CompilerParams(vmem_limit_bytes=62 * 2**20),
         cost_estimate=EXPERT_COST,
         name="expert",
-    )(place, router, *x_parts, *dy_parts, *sources, *before, *after)
+    )(place, router, *x_parts, *dy_parts, *sources, *before, *other, *after)
+    lists = (3 if first else 2) if with_grads else (5 if first else 4)
+    split = [outs[at * count : (at + 1) * count] for at in range(lists)]
+    return (*split, outs[-1]) if with_grads else split
 
 
 def per_device(
@@ -639,7 +682,8 @@
     rank_cols = [ranks[j][:, None] for j in range(expert_count)]
 
     def exchange(packed):
-        return [packed[0]] + [swap(packed[j], j) for j in range(expert_count - 1, 0, -1)][::-1]
+        moved = {j: swap(packed[j], j) for j in (2, 3, 1)}
+        return [packed[0], moved[1], moved[2], moved[3]]
 
     def expert_cut(part):
         size = hidden // HALVES
@@ -656,8 +700,8 @@
     far_pieces = [gather_far(tie(expert_cut(0), qkv_far[-1]))]
     far_pieces.append(gather_far(tie(expert_cut(1), far_pieces[0][-1])))
     dy_parts = exchange(pack(out_grad, ranks, capacity))
-    qkv_full, small_full = dense_place(qkv_far, (far_pieces[0][1], *proj_far[1:]))
-    proj_full, _ = dense_place(proj_far)
+    qkv_full, small_full = dense_place(qkv_far)
+    proj_full, _ = dense_place(proj_far, tuple(dy_parts[2:]))
     small_rows = small_full[:, :8].T
     norm_full = small_rows[:4].astype(F32)
     router_t = small_rows[4:8]
@@ -678,10 +722,7 @@
     first_key = jnp.tile(first_key.reshape(-1, QB), (1, 2))
     last_key = jnp.tile(last_key.reshape(-1, QB), (1, 2))
     context, lse = attend(qkv_rows, kv_window, first_key, last_key, scale)
-    sources, stacks = [], []
-    for pieces in far_pieces:
-        stacks.append(jnp.stack([tie(pieces[0], context), *pieces[1:]]))
-        sources.append(gather_near(stacks[-1]))
+    sources = [gather_near(jnp.stack([tie(far_pieces[0][0], context), *far_pieces[0][1:]]))]
     residual = x_float + jnp.dot(context, proj_full, preferred_element_type=F32)
     normed_two, scale_two = standardize(residual)
     second_in = (normed_two * norm_full[2] + norm_full[3]).astype(BF16)
@@ -695,15 +736,40 @@
     ]
 
     x_parts = exchange(pack(second_in, ranks, capacity))
-    *sums, low_grad = expert(
-        place, router_pad, x_parts, dy_parts, sources[0], expert_count, (), (stacks[1],)
-    )
-    out_slots, grad_slots, high_grad = expert(
-        place, router_pad, x_parts, dy_parts, sources[1], expert_count, sums
-    )
+
+    def run(at, part, before=(), other=(), after=()):
+        return expert(
+            place,
+            router_pad,
+            [x_parts[j] for j in at],
+            [dy_parts[j] for j in at],
+            sources[part],
+            expert_count,
+            before,
+            other,
+            after,
+        )
+
+    near_sums, near_back, near_g, near_act, near_pg = run((0, 1), 0)
+    far_stack = jnp.stack([tie(far_pieces[1][0], near_g[0]), *far_pieces[1][1:]])
+    sources.append(gather_near(far_stack))
+    far_sums, far_back, far_g, low_grad = run(
+        (2, 3), 0, other=(x_parts[:2], near_g, near_act, near_pg), after=(far_stack,)
+    )
+    outs, backs, weighted = near_sums + far_sums, near_back + far_back, near_g + far_g
+    sent_out, sent_back, sent_act, sent_pg = run(
+        (1, 2, 3), 1, before=(outs[1:], backs[1:], weighted[1:])
+    )
+    own_out, own_back, high_grad = run(
+        (0,),
+        1,
+        before=(outs[:1], backs[:1], weighted[:1]),
+        other=(x_parts[1:], weighted[1:], sent_act, sent_pg),
+    )
+    out_parts = exchange(own_out + sent_out)
+    grad_parts = exchange(own_back + sent_back)
     near_sums = {0: add_near(low_grad)}
-    s_sum, gate_grads = unpack_grad(exchange(grad_slots), rank_cols, (near_sums[0],))
-    out_parts = exchange(tie(out_slots, s_sum))
+    s_sum, gate_grads = unpack_grad(grad_parts, rank_cols, (near_sums[0],))
 
     gate_grads = gate_grads[:, :expert_count].T
     prob_grad = jnp.concatenate(
@@ -735,7 +801,6 @@
         lse,
         scale,
         range(0, pairs // 2),
-        (low_parts[1],),
     )
     near_sums[1] = add_near(high_grad, first_half[0])
     second_half = attend_back(
@@ -747,27 +812,29 @@
         lse,
         scale,
         range(pairs // 2, pairs),
-        (near_sums[1], low_parts[2]),
+        (near_sums[1], low_parts[1], low_parts[2]),
     )
     block_output = unpack_out(residual, out_parts, rank_cols, gate_cols, (second_half[0],))
-    query_grad, key_grad, value_grad = [
-        jnp.concatenate(both, axis=1) for both in zip(first_half, second_half)
-    ]
-    window_grad = jnp.concatenate([key_grad, value_grad], axis=1)
-    from_below, from_above = shift(
-        window_grad[:HALO], window_grad[HALO + row_count :], ("replica", "group")
-    )
-    own_grad = window_grad[HALO : HALO + row_count].astype(F32)
-    outside = jnp.concatenate(
-        [
-            from_below,
-            jnp.zeros((row_count - 2 * HALO, 2 * width), BF16),
-            from_above,
-        ],
-        axis=0,
-    ).astype(F32)
-    kv_grad = (own_grad + outside).astype(BF16)
-    qkv_grad_rows = jnp.concatenate([query_grad, kv_grad], axis=1)
+    high_parts = far_parts(near_sums[1])
+    query_grads, own_grads, outside_grads = [], [], []
+    for query_grad, *window_grads in (first_half, second_half):
+        query_grads.append(query_grad)
+        edges = [
+            jnp.concatenate([grad[rows] for grad in window_grads], axis=1)
+            for rows in (slice(0, HALO), slice(HALO + row_count, None))
+        ]
+        from_below, from_above = shift(*edges, ("replica", "group"))
+        outside = jnp.concatenate(
+            [from_below, jnp.zeros((row_count - 2 * HALO, from_below.shape[1]), BF16), from_above],
+            axis=0,
+        )
+        size = from_below.shape[1] // 2
+        for at, grad in enumerate(window_grads):
+            own_grads.append(grad[HALO : HALO + row_count])
+            outside_grads.append(outside[:, at * size : (at + 1) * size])
+    kv_grads = [summed([own_grads[at], outside_grads[at]]) for at in (0, 2, 1, 3)]
+    qkv_grad_rows = jnp.concatenate([*query_grads, *kv_grads], axis=1)
+    qkv_grad_rows = tie(qkv_grad_rows, low_parts[3], high_parts[1])
     qkv_grad = jnp.dot(first_in.T, qkv_grad_rows, preferred_element_type=F32)
     first_grad = lax.dot_general(qkv_grad_rows, qkv_full, NT, preferred_element_type=F32)
     gain_one_grad = jnp.sum(first_grad * normed_one, axis=0)
@@ -796,7 +863,7 @@
     owned = jnp.concatenate(
         [
             summed([tie(parts[0], dense_near), *parts[1:]])
-            for parts in (low_parts, far_parts(near_sums[1]))
+            for parts in (low_parts, high_parts)
         ],
         axis=2,
     )

time: 727 us -> 673 us (0.926)
  waiting for transfers between devices: 285 us -> 221 us
  local copies, waits for them, and re-layouts: 80.7 us -> 67.5 us
  Pallas kernels: 180 us -> 193 us
  starting transfers between devices: 75.9 us -> 86.8 us
    ppermute x22, waiting for transfers between devices: 88.8 us -> 46.3 us  [swap(): return lax.ppermute(block, 'replica', [(r, r ^ bit) for r in range(count)])]
    ppermute x28, waiting for transfers between devices: 168 us -> 140 us  [group_swap(): return lax.ppermute(block, 'group', [(g, g ^ flip) for g in range(count)])]
    pallas_call x4 -> x6, Pallas kernels: 104 us -> 118 us  [the longest x4 109 us: expert(): pl.pallas_call(partial(expert_kernel, count, others, near, first, expert_...]
    squeeze x4 -> x0, local copies, waits for them, and re-layouts: 13.4 us -> none  [exchange(): packed[j]]
    ppermute x4 -> x6, starting transfers between devices: 15.8 us -> 24.6 us  [shift(): return (lax.ppermute(tail, axes, up), lax.ppermute(head, axes, down))]
    ppermute x4 -> x6, waiting for transfers between devices: 28.7 us -> 34 us  [shift(): return (lax.ppermute(tail, axes, up), lax.ppermute(head, axes, down))]
    unnamed x212 -> x171, local copies, waits for them, and re-layouts: 24.3 us -> 21.1 us
  transfers between devices with their start and end apart: 54 -> 56, of which waited for: 21 -> 20; matrix products, arithmetic and copies ran while one was open for 17% -> 17% of each run, Pallas kernels for 23% -> 29%
where the time goes in v4:
time: 673 us; the launch traced here: 667 us
  waiting for transfers between devices  221 us (33%)
  Pallas kernels  193 us (29%)
  starting transfers between devices  86.8 us (13%)
  other arithmetic  70.2 us (10%)
  local copies, waits for them, and re-layouts  67.5 us (10%)
  matrix products  27 us (4%)
    ppermute x28, waiting for transfers between devices, group_swap(): return lax.ppermute(block, 'group', [(g, g ^ flip) for g in range(count)])  140 us
    pallas_call x4, Pallas kernels, expert(): pl.pallas_call(partial(expert_kernel, count, others, near, first, expert_...  109 us
    ppermute x22, waiting for transfers between devices, swap(): return lax.ppermute(block, 'replica', [(r, r ^ bit) for r in range(count)])  46.3 us
    ppermute x28, starting transfers between devices, group_swap(): return lax.ppermute(block, 'group', [(g, g ^ flip) for g in range(count)])  36.5 us
    ppermute x6, waiting for transfers between devices, shift(): return (lax.ppermute(tail, axes, up), lax.ppermute(head, axes, down))  34 us
    pallas_call x2, Pallas kernels, attend_back(): pl.pallas_call(partial(attend_back_kernel, scale), grid=(count,), in_spec...  27.1 us
    pallas_call x1, Pallas kernels, attend(): pl.pallas_call(partial(attend_kernel, scale), grid=(pairs,), in_specs=[pl...  25.9 us
    ppermute x22, starting transfers between devices, swap(): return lax.ppermute(block, 'replica', [(r, r ^ bit) for r in range(count)])  25.7 us
  transfers between devices with their start and end apart: 56, of which 20 were waited for; matrix products, arithmetic and copies ran while one was open for 17% of the time, Pallas kernels for 29%

profile of v4, /device:TPU:23, one launch (start us, length us, event | category | flops | bytes accessed | tf_op | source)
XLA Modules:
  0.0 667.0 jit_solution(6197379689713625601)
XLA Ops:
  15.1 12.5 %collective-permute-done.1 = bf16[96,1280]{1,0:T(8,128)(2,1)S(1)} collective-permute-done((bf16[96,1280]{1,0:T(8,128)(2,1)S(1)}, bf16[96,1280]{1,0:T(8,128)(2,1)S(1)}, u32[]{:S(2)}, u32[]{:S(2)}) %collective-permute-start.1) | collective-permute-done | bytes 245792 | tf_op jit(solution)/shard_map/ppermute | solution.py:56
  32.6 16.1 %collective-permute-done.3.refs_1_ = bf16[4,96,1280]{2,1,0:T(8,128)(2,1)S(1)} collective-permute-done((bf16[4,96,1280]{2,1,0:T(8,128)(2,1)S(1)}, bf16[4,96,1280]{2,1,0:T(8,128)(2,1)S(1)}, u32[]{:S(2)}, u32[]{:S(2)}) %collective-permute-start.3) | collective-permute-done | bytes 983072 | tf_op jit(solution)/shard_map/ppermute | solution.py:56
  61.2 5.5 convolution_convert_fusion.1.q_ref
  66.9 4.9 collective-permute-start.6
  76.9 4.6 pack.2
  85.5 19.3 %collective-permute-done.6 = bf16[256,1536]{1,0:T(8,128)(2,1)} collective-permute-done((bf16[256,1536]{1,0:T(8,128)(2,1)S(1)}, bf16[256,1536]{1,0:T(8,128)(2,1)}, u32[]{:S(2)}, u32[]{:S(2)}) %collective-permute-start.6) | collective-permute-done | bytes 786464 | tf_op jit(solution)/shard_map/ppermute | solution.py:45
  117.7 25.9 %attend.1 = (bf16[768,768]{1,0:T(8,128)(2,1)}, f32[6,8,256]{2,1,0:T(8,128)}) custom-call(bf16[768,2304]{1,0:T(8,128)(2,1)} %copy-done.21, bf16[1280,1536]{1,0:T(8,128)(2,1)} %pad_maximum_fusion.1.k_ref.v_ref, bf16[1280,1536]{1,0:T(8,128)(2,1)} %pad_maximum_fusion.1.k_ref.v_ref, s32[6,256]{1,0:T(8,128)} %bitcast.222, s32[6,256]{1,0:T(8,128)} %bitcast.219), custom_call_target="tpu_custom_call" | custom-call | flops 30000001024 | bytes 100000 | tf_op jit(solution)/shard_map/attend/pallas_call | solution.py:256
  144.7 9.6 %collective-permute-done.20 = bf16[2,96,1536]{2,1,0:T(8,128)(2,1)S(1)} collective-permute-done((bf16[2,96,1536]{2,1,0:T(8,128)(2,1)S(1)}, bf16[2,96,1536]{2,1,0:T(8,128)(2,1)S(1)}, u32[]{:S(2)}, u32[]{:S(2)}) %collective-permute-start.20) | collective-permute-done | bytes 589856 | tf_op jit(solution)/shard_map/ppermute | solution.py:56
  184.8 23.3 %collective-permute-done.21.refs_5_ = bf16[4,2,96,1536]{3,2,1,0:T(8,128)(2,1)} collective-permute-done((bf16[4,2,96,1536]{3,2,1,0:T(8,128)(2,1)}, bf16[4,2,96,1536]{3,2,1,0:T(8,128)(2,1)}, u32[]{:S(2)}, u32[]{:S(2)}) %collective-permute-start.21) | collective-permute-done | bytes 2359328 | tf_op jit(solution)/shard_map/ppermute | solution.py:56
  211.2 20.3 %expert.4 = (f32[480,768]{1,0:T(8,128)}, f32[480,768]{1,0:T(8,128)}, f32[480,768]{1,0:T(8,128)}, f32[480,768]{1,0:T(8,128)}, bf16[480,768]{1,0:T(8,128)(2,1)}, /...) custom-call(s32[4]{0:T(128)} %pad_add_fusion.place_ref, ...), custom_call_target="tpu_custom_call" | custom-call | flops 28000000000 | bytes 100000 | tf_op jit(solution)/shard_map/expert/pallas_call | solution.py:591
  238.9 31.3 %expert.5 = (f32[480,768]{1,0:T(8,128)}, f32[480,768]{1,0:T(8,128)}, f32[480,768]{1,0:T(8,128)}, f32[480,768]{1,0:T(8,128)}, bf16[480,768]{1,0:T(8,128)(2,1)}, /...) custom-call(s32[4]{0:T(128)} %pad_add_fusion.place_ref, bf16[768,128]{1,0:T(8,128)(2,1)} %pad.16.router_ref, ...), custom_call_target="tpu_custom_call" | custom-call | flops 28000000000 | bytes 100000 | tf_op jit(solution)/shard_map/expert/pallas_call | solution.py:591
  273.5 15.8 %collective-permute-done.25.refs_7_.refs_3_ = bf16[4,2,96,1536]{3,2,1,0:T(8,128)(2,1)} collective-permute-done((bf16[4,2,96,1536]{3,2,1,0:T(8,128)(2,1)}, bf16[4,2,96,1536]{3,2,1,0:T(8,128)(2,1)}, u32[]{:S(2)}, u32[]{:S(2)}) %collective-permute-start.25) | collective-permute-done | bytes 2359328 | tf_op jit(solution)/shard_map/ppermute | solution.py:56
  289.3 30.4 %expert.6 = (bf16[480,768]{1,0:T(8,128)(2,1)}, bf16[480,768]{1,0:T(8,128)(2,1)}, bf16[480,768]{1,0:T(8,128)(2,1)}, bf16[496,768]{1,0:T(8,128)(2,1)}, bf16[496,76...) custom-call(s32[4]{0:T(128)} %pad_add_fusion.place_ref, ...), custom_call_target="tpu_custom_call" | custom-call | flops 28000000000 | bytes 100000 | tf_op jit(solution)/shard_map/expert/pallas_call | solution.py:591
  325.3 26.5 %expert.7 = (bf16[480,768]{1,0:T(8,128)(2,1)}, bf16[496,768]{1,0:T(8,128)(2,1)}, bf16[2,768,1536]{2,1,0:T(8,128)(2,1)}) custom-call(s32[4]{0:T(128)} %pad_add_fusion.place_ref, bf16[768,128]{1,0:T(8,128)(2,1)} %pad.16.router_ref, bf16[480,768]{1,0:T(8,128)(2,1)} %get-tuple-element.79.refs_0_.refs_6_, bf16[480,768]{1,0:T(8,128)(2,1)} %get-tuple-element.80.refs_2_.refs_1_, ...), custom_call_target="tpu_custom_call" | custom-call | flops 28000000000 | bytes 100000 | tf_op jit(solution)/shard_map/expert/pallas_call | solution.py:591
  351.8 5.0 dynamic-slice_bitcast_fusion.1
  366.4 7.1 %unpack_grad.1 = (f32[768,768]{1,0:T(8,128)}, f32[768,128]{1,0:T(8,128)}) custom-call(bf16[496,768]{1,0:T(8,128)(2,1)} %get-tuple-element.111.refs_0_, bf16[496,768]{1,0:T(8,128)(2,1)} %copy-done.46, bf16[496,768]{1,0:T(8,128)(2,1)} %copy-done.47, bf16[496,768]{1,0:T(8,128)(2,1)} %collective-permute-done.33.refs_3_, s32[768,1]{1,0:T(8,128)} %copy.235.refs_4_, ...), custom_call_target="tpu_custom_call" | custom-call | tf_op jit(solution)/shard_map/unpack_grad/pallas_call | solution.py:383
  383.0 13.6 %attend_back.2 = (bf16[768,384]{1,0:T(8,128)(2,1)}, bf16[1280,384]{1,0:T(8,128)(2,1)}, bf16[1280,384]{1,0:T(8,128)(2,1)}) custom-call(bf16[768,2304]{1,0:T(8,128)(2,1)} %copy-done.21, bf16[1280,1536]{1,0:T(8,128)(2,1)} %pad_maximum_fusion.1.k_ref.v_ref, bf16[1280,1536]{1,0:T(8,128)(2,1)} %pad_maximum_fusion.1.k_ref.v_ref, ...), custom_call_target="tpu_custom_call" | custom-call | flops 15000000512 | bytes 100000 | tf_op jit(solution)/shard_map/attend_back/pallas_call | solution.py:288
  417.1 13.6 %attend_back.3 = (bf16[768,384]{1,0:T(8,128)(2,1)}, bf16[1280,384]{1,0:T(8,128)(2,1)}, bf16[1280,384]{1,0:T(8,128)(2,1)}) custom-call(bf16[768,2304]{1,0:T(8,128)(2,1)} %copy-done.21, bf16[1280,1536]{1,0:T(8,128)(2,1)} %pad_maximum_fusion.1.k_ref.v_ref, bf16[1280,1536]{1,0:T(8,128)(2,1)} %pad_maximum_fusion.1.k_ref.v_ref, ...), custom_call_target="tpu_custom_call" | custom-call | flops 15000000512 | bytes 100000 | tf_op jit(solution)/shard_map/attend_back/pallas_call | solution.py:288
  433.0 7.3 %collective-permute-start.40 = (bf16[256,768]{1,0:T(8,128)(2,1)S(1)}, bf16[256,768]{1,0:T(8,128)(2,1)S(1)}, u32[]{:S(2)}, u32[]{:S(2)}) collective-permute-start(bf16[256,768]{1,0:T(8,128)(2,1)S(1)} %pad_maximum_fusion.14), channel_id=1, source_target_pairs={{0,1},{1,2},{2,3},{3,4},{4,5},{5,6},{6,7},{7,8},{8,9},{9,10},{10,1... | collective-permute-start | bytes 1179656 | tf_op jit(solution)/shard_map/ppermute | solution.py:45
  446.1 13.1 %collective-permute-done.40 = bf16[256,768]{1,0:T(8,128)(2,1)S(1)} collective-permute-done((bf16[256,768]{1,0:T(8,128)(2,1)S(1)}, bf16[256,768]{1,0:T(8,128)(2,1)S(1)}, u32[]{:S(2)}, u32[]{:S(2)}) %collective-permute-start.40) | collective-permute-done | bytes 393248 | tf_op jit(solution)/shard_map/ppermute | solution.py:45
  465.6 5.8 convolution_convert_fusion
  471.5 4.6 fusion.25
  495.2 5.3 collective-permute-start.45
  509.0 10.5 %collective-permute-done.30.refs_3_ = bf16[480,768]{1,0:T(8,128)(2,1)} collective-permute-done((bf16[480,768]{1,0:T(8,128)(2,1)}, bf16[480,768]{1,0:T(8,128)(2,1)}, u32[]{:S(2)}, u32[]{:S(2)}) %collective-permute-start.30) | collective-permute-done | bytes 737312 | tf_op jit(solution)/shard_map/ppermute | solution.py:34
  519.5 7.3 %unpack_out.1 = bf16[768,768]{1,0:T(8,128)(2,1)} custom-call(f32[768,768]{1,0:T(8,128)} %copy-done, bf16[480,768]{1,0:T(8,128)(2,1)} %get-tuple-element.107.refs_0_, bf16[480,768]{1,0:T(8,128)(2,1)} %copy-done.48, bf16[480,768]{1,0:T(8,128)(2,1)} %collective-permute-done.29.refs_2_, bf16[480,768]{1,0:T(8,128)(2,1)} %collective-permute-done.30.refs_3_, ...), custom_call_target="tpu_custom_call" | custom-call | tf_op jit(solution)/shard_map/unpack_out/pallas_call | solution.py:409
  534.9 12.5 %collective-permute-done.46 = bf16[96,1664]{1,0:T(8,128)(2,1)S(1)} collective-permute-done((bf16[96,1664]{1,0:T(8,128)(2,1)S(1)}, bf16[96,1664]{1,0:T(8,128)(2,1)S(1)}, u32[]{:S(2)}, u32[]{:S(2)}) %collective-permute-start.46) | collective-permute-done | bytes 319520 | tf_op jit(solution)/shard_map/ppermute | solution.py:56
  547.4 30.5 %collective-permute-done.47 = bf16[96,1664]{1,0:T(8,128)(2,1)S(1)} collective-permute-done((bf16[96,1664]{1,0:T(8,128)(2,1)S(1)}, bf16[96,1664]{1,0:T(8,128)(2,1)S(1)}, u32[]{:S(2)}, u32[]{:S(2)}) %collective-permute-start.47) | collective-permute-done | bytes 319520 | tf_op jit(solution)/shard_map/ppermute | solution.py:56
  577.9 9.3 %collective-permute-done.48 = bf16[96,1664]{1,0:T(8,128)(2,1)S(1)} collective-permute-done((bf16[96,1664]{1,0:T(8,128)(2,1)S(1)}, bf16[96,1664]{1,0:T(8,128)(2,1)S(1)}, u32[]{:S(2)}, u32[]{:S(2)}) %collective-permute-start.48) | collective-permute-done | bytes 319520 | tf_op jit(solution)/shard_map/ppermute | solution.py:56
  590.3 6.8 %collective-permute-done.49 = bf16[96,1664]{1,0:T(8,128)(2,1)S(1)} collective-permute-done((bf16[96,1664]{1,0:T(8,128)(2,1)S(1)}, bf16[96,1664]{1,0:T(8,128)(2,1)S(1)}, u32[]{:S(2)}, u32[]{:S(2)}) %collective-permute-start.49) | collective-permute-done | bytes 319520 | tf_op jit(solution)/shard_map/ppermute | solution.py:34
  602.0 25.8 %collective-permute-done.54 = bf16[2,96,3072]{2,1,0:T(8,128)(2,1)} collective-permute-done((bf16[2,96,3072]{2,1,0:T(8,128)(2,1)}, bf16[2,96,3072]{2,1,0:T(8,128)(2,1)}, u32[]{:S(2)}, u32[]{:S(2)}) %collective-permute-start.54) | collective-permute-done | bytes 1179680 | tf_op jit(solution)/shard_map/ppermute | solution.py:34
  649.5 8.4 %multiply_subtract_fusion = (f32[4,3072,96]{1,2,0:T(8,128)}, f32[4,3072,96]{1,2,0:T(8,128)}, f32[4,3072,96]{1,2,0:T(8,128)}) fusion(f32[4,3072,96]{1,2,0:T(8,128)S(1)} %bitcast.196, f32[4,2,96,3072]{3,2,1,0:T(8,128)S(1)} %maximum_convert_fusion, f32[4,3072,96]{1,2,0:T(8,128)S(1)} %bitcast.203, f32[4,3072,96]{1,2,0:T(8,128)} %param.42), kind=kLoop, calls=%fused_computation.20 | loop fusion | flops 17694720 | bytes 33030144 | tf_op jit(solution)/shard_map/sub | solution.py:175
  657.9 8.9 %multiply_subtract_fusion.1 = (f32[4,96,3072]{2,1,0:T(8,128)}, f32[4,96,3072]{2,1,0:T(8,128)}, f32[4,96,3072]{2,1,0:T(8,128)}) fusion(f32[4,96,3072]{2,1,0:T(8,128)S(1)} %bitcast.198, f32[4,2,96,3072]{3,2,1,0:T(8,128)S(1)} %maximum_convert_fusion, f32[4,96,3072]{2,1,0:T(8,128)} %param.40, f32[4,96,3072]{2,1,0:T(8,128)} %param.39), kind=kLoop, calls=%fused_computation.22 | loop fusion | flops 17694720 | bytes 33030144 | tf_op jit(solution)/shard_map/sub | solution.py:175
  (422 shorter events, 223.0 us)
Async XLA Ops:
  7.0 74.5 %collective-permute-start.8 = (bf16[96,512]{1,0:T(8,128)(2,1)S(1)}, bf16[96,512]{1,0:T(8,128)(2,1)S(1)}, u32[]{:S(2)}, u32[]{:S(2)}) collective-permute-start(bf16[96,512]{1,0:T(8,128)(2,1)S(1)} %get-tuple-element.310), channel_id=1, source_target_pairs={{0,2},{1,3},{2,0},{3,1},{4,6},{5,7},{6,4},{7,5},{8,10},{9,11},{10,... | collective-permute-start | bytes 294920 | tf_op jit(solution)/shard_map/ppermute | solution.py:56
  8.5 73.2 %collective-permute-start.9 = (bf16[96,512]{1,0:T(8,128)(2,1)S(1)}, bf16[96,512]{1,0:T(8,128)(2,1)S(1)}, u32[]{:S(2)}, u32[]{:S(2)}) collective-permute-start(bf16[96,512]{1,0:T(8,128)(2,1)S(1)} %get-tuple-element.310), channel_id=1, source_target_pairs={{0,4},{1,5},{2,6},{3,7},{4,0},{5,1},{6,2},{7,3},{8,12},{9,13},{10,... | collective-permute-start | bytes 294920 | tf_op jit(solution)/shard_map/ppermute | solution.py:56
  14.8 68.7 %collective-permute-start.10 = (bf16[96,512]{1,0:T(8,128)(2,1)S(1)}, bf16[96,512]{1,0:T(8,128)(2,1)S(1)}, u32[]{:S(2)}, u32[]{:S(2)}) collective-permute-start(bf16[96,512]{1,0:T(8,128)(2,1)S(1)} %get-tuple-element.310), channel_id=1, source_target_pairs={{0,6},{1,7},{2,4},{3,5},{4,2},{5,3},{6,0},{7,1},{8,14},{9,15},{10,... | collective-permute-start | bytes 294920 | tf_op jit(solution)/shard_map/ppermute | solution.py:56
  66.9 38.0 %collective-permute-start.6 = (bf16[256,1536]{1,0:T(8,128)(2,1)S(1)}, bf16[256,1536]{1,0:T(8,128)(2,1)}, u32[]{:S(2)}, u32[]{:S(2)}) collective-permute-start(bf16[256,1536]{1,0:T(8,128)(2,1)S(1)} %get-tuple-element.274), channel_id=1, source_target_pairs={{0,1},{1,2},{2,3},{3,4},{4,5},{5,6},{6,7},{7,8},{8,9},{9,10},{10,1... | collective-permute-start | bytes 2359304 | tf_op jit(solution)/shard_map/ppermute | solution.py:45
  81.5 77.6 %collective-permute-start.14 = (bf16[480,768]{1,0:T(8,128)(2,1)}, bf16[480,768]{1,0:T(8,128)(2,1)}, u32[]{:S(2)}, u32[]{:S(2)}) collective-permute-start(bf16[480,768]{1,0:T(8,128)(2,1)} %get-tuple-element.76), channel_id=1, source_target_pairs={{0,16},{8,24},{16,0},{24,8},{1,17},{9,25},{17,1},{25,9},{2,18},{10... | collective-permute-start | bytes 2211848 | tf_op jit(solution)/shard_map/ppermute | solution.py:34
  81.7 77.4 %collective-permute-start.15 = (bf16[480,768]{1,0:T(8,128)(2,1)}, bf16[480,768]{1,0:T(8,128)(2,1)}, u32[]{:S(2)}, u32[]{:S(2)}) collective-permute-start(bf16[480,768]{1,0:T(8,128)(2,1)} %get-tuple-element.77), channel_id=1, source_target_pairs={{0,24},{8,16},{16,8},{24,0},{1,25},{9,17},{17,9},{25,1},{2,26},{10... | collective-permute-start | bytes 2211848 | tf_op jit(solution)/shard_map/ppermute | solution.py:34
  104.8 38.8 %collective-permute-start.16 = (bf16[2,96,1536]{2,1,0:T(8,128)(2,1)S(1)}, bf16[2,96,1536]{2,1,0:T(8,128)(2,1)S(1)}, u32[]{:S(2)}, u32[]{:S(2)}) collective-permute-start(bf16[2,96,1536]{2,1,0:T(8,128)(2,1)S(1)} %copy-done.16), channel_id=1, source_target_pairs={{0,6},{1,7},{2,4},{3,5},{4,2},{5,3},{6,0},{7,1},{8,14},{9,15},{10,... | collective-permute-start | bytes 1769480 | tf_op jit(solution)/shard_map/ppermute | solution.py:56
  104.8 39.7 %collective-permute-start.19 = (bf16[2,96,1536]{2,1,0:T(8,128)(2,1)S(1)}, bf16[2,96,1536]{2,1,0:T(8,128)(2,1)S(1)}, u32[]{:S(2)}, u32[]{:S(2)}) collective-permute-start(bf16[2,96,1536]{2,1,0:T(8,128)(2,1)S(1)} %copy-done.16), channel_id=1, source_target_pairs={{0,2},{1,3},{2,0},{3,1},{4,6},{5,7},{6,4},{7,5},{8,10},{9,11},{10,... | collective-permute-start | bytes 1769480 | tf_op jit(solution)/shard_map/ppermute | solution.py:56
  113.2 41.1 %collective-permute-start.20 = (bf16[2,96,1536]{2,1,0:T(8,128)(2,1)S(1)}, bf16[2,96,1536]{2,1,0:T(8,128)(2,1)S(1)}, u32[]{:S(2)}, u32[]{:S(2)}) collective-permute-start(bf16[2,96,1536]{2,1,0:T(8,128)(2,1)S(1)} %copy-done.16), channel_id=1, source_target_pairs={{0,4},{1,5},{2,6},{3,7},{4,0},{5,1},{6,2},{7,3},{8,12},{9,13},{10,... | collective-permute-start | bytes 1769480 | tf_op jit(solution)/shard_map/ppermute | solution.py:56
  157.1 51.1 %collective-permute-start.21 = (bf16[4,2,96,1536]{3,2,1,0:T(8,128)(2,1)}, bf16[4,2,96,1536]{3,2,1,0:T(8,128)(2,1)}, u32[]{:S(2)}, u32[]{:S(2)}) collective-permute-start(bf16[4,2,96,1536]{3,2,1,0:T(8,128)(2,1)} %pad_maximum_fusion.2.refs_4_), channel_id=1, source_target_pairs={{0,1},{1,0},{2,3},{3,2},{4,5},{5,4},{6,7},{7,6},{8,9},{9,8},{10,11... | collective-permute-start | bytes 7077896 | tf_op jit(solution)/shard_map/ppermute | solution.py:56
  178.5 53.0 %collective-permute-start.22 = (bf16[2,96,1536]{2,1,0:T(8,128)(2,1)}, bf16[2,96,1536]{2,1,0:T(8,128)(2,1)S(1)}, u32[]{:S(2)}, u32[]{:S(2)}) collective-permute-start(bf16[2,96,1536]{2,1,0:T(8,128)(2,1)} %tie.9.refs_0_), channel_id=1, source_target_pairs={{0,2},{1,3},{2,0},{3,1},{4,6},{5,7},{6,4},{7,5},{8,10},{9,11},{10,... | collective-permute-start | bytes 1769480 | tf_op jit(solution)/shard_map/ppermute | solution.py:56
  181.9 49.7 %collective-permute-start.23 = (bf16[2,96,1536]{2,1,0:T(8,128)(2,1)}, bf16[2,96,1536]{2,1,0:T(8,128)(2,1)S(1)}, u32[]{:S(2)}, u32[]{:S(2)}) collective-permute-start(bf16[2,96,1536]{2,1,0:T(8,128)(2,1)} %tie.9.refs_0_), channel_id=1, source_target_pairs={{0,4},{1,5},{2,6},{3,7},{4,0},{5,1},{6,2},{7,3},{8,12},{9,13},{10,... | collective-permute-start | bytes 1769480 | tf_op jit(solution)/shard_map/ppermute | solution.py:56
  183.3 51.0 %collective-permute-start.24 = (bf16[2,96,1536]{2,1,0:T(8,128)(2,1)}, bf16[2,96,1536]{2,1,0:T(8,128)(2,1)}, u32[]{:S(2)}, u32[]{:S(2)}) collective-permute-start(bf16[2,96,1536]{2,1,0:T(8,128)(2,1)} %tie.9.refs_0_), channel_id=1, source_target_pairs={{0,6},{1,7},{2,4},{3,5},{4,2},{5,3},{6,0},{7,1},{8,14},{9,15},{10,... | collective-permute-start | bytes 1769480 | tf_op jit(solution)/shard_map/ppermute | solution.py:56
  184.6 54.3 %collective-permute-start.26 = (bf16[480,768]{1,0:T(8,128)(2,1)}, bf16[480,768]{1,0:T(8,128)(2,1)}, u32[]{:S(2)}, u32[]{:S(2)}) collective-permute-start(bf16[480,768]{1,0:T(8,128)(2,1)} %get-tuple-element.86), channel_id=1, source_target_pairs={{0,16},{8,24},{16,0},{24,8},{1,17},{9,25},{17,1},{25,9},{2,18},{10... | collective-permute-start | bytes 2211848 | tf_op jit(solution)/shard_map/ppermute | solution.py:34
  237.2 52.1 %collective-permute-start.25 = (bf16[4,2,96,1536]{3,2,1,0:T(8,128)(2,1)}, bf16[4,2,96,1536]{3,2,1,0:T(8,128)(2,1)}, u32[]{:S(2)}, u32[]{:S(2)}) collective-permute-start(bf16[4,2,96,1536]{3,2,1,0:T(8,128)(2,1)} %pad_maximum_fusion.3.refs_14_.refs_6_.refs_2_), channel_id=1, source_target_pairs={{0,1},{1,0},{2,3},{3,2},{4,5},{5,4},{6,7},{7,6},{8,9},{9,8},{10,11... | collective-permute-start | bytes 7077896 | tf_op jit(solution)/shard_map/ppermute | solution.py:56
  273.4 85.0 %collective-permute-start.34 = (bf16[2,4,96,1536]{3,2,1,0:T(8,128)(2,1)}, bf16[2,4,96,1536]{3,2,1,0:T(8,128)(2,1)}, u32[]{:S(2)}, u32[]{:S(2)}) collective-permute-start(bf16[2,4,96,1536]{3,2,1,0:T(8,128)(2,1)} %dynamic-slice_bitcast_fusion.2), channel_id=1, source_target_pairs={{0,1},{1,0},{2,3},{3,2},{4,5},{5,4},{6,7},{7,6},{8,9},{9,8},{10,11... | collective-permute-start | bytes 7077896 | tf_op jit(solution)/shard_map/ppermute | solution.py:56
  319.8 43.9 %collective-permute-start.31 = (bf16[496,768]{1,0:T(8,128)(2,1)}, bf16[496,768]{1,0:T(8,128)(2,1)S(1)}, u32[]{:S(2)}, u32[]{:S(2)}) collective-permute-start(bf16[496,768]{1,0:T(8,128)(2,1)} %get-tuple-element.112), channel_id=1, source_target_pairs={{0,8},{8,0},{16,24},{24,16},{1,9},{9,1},{17,25},{25,17},{2,10},{10... | collective-permute-start | bytes 2285576 | tf_op jit(solution)/shard_map/ppermute | solution.py:34
  323.6 41.6 %collective-permute-start.32 = (bf16[496,768]{1,0:T(8,128)(2,1)}, bf16[496,768]{1,0:T(8,128)(2,1)S(1)}, u32[]{:S(2)}, u32[]{:S(2)}) collective-permute-start(bf16[496,768]{1,0:T(8,128)(2,1)} %get-tuple-element.113), channel_id=1, source_target_pairs={{0,16},{8,24},{16,0},{24,8},{1,17},{9,25},{17,1},{25,9},{2,18},{10... | collective-permute-start | bytes 2285576 | tf_op jit(solution)/shard_map/ppermute | solution.py:34
  323.8 42.5 %collective-permute-start.33 = (bf16[496,768]{1,0:T(8,128)(2,1)}, bf16[496,768]{1,0:T(8,128)(2,1)}, u32[]{:S(2)}, u32[]{:S(2)}) collective-permute-start(bf16[496,768]{1,0:T(8,128)(2,1)} %get-tuple-element.114), channel_id=1, source_target_pairs={{0,24},{8,16},{16,8},{24,0},{1,25},{9,17},{17,9},{25,1},{2,26},{10... | collective-permute-start | bytes 2285576 | tf_op jit(solution)/shard_map/ppermute | solution.py:34
  356.8 53.4 %collective-permute-start.35 = (bf16[2,4,96,1536]{3,2,1,0:T(8,128)(2,1)}, bf16[2,4,96,1536]{3,2,1,0:T(8,128)(2,1)}, u32[]{:S(2)}, u32[]{:S(2)}) collective-permute-start(bf16[2,4,96,1536]{3,2,1,0:T(8,128)(2,1)} %get-tuple-element.271), channel_id=1, source_target_pairs={{0,1},{1,0},{2,3},{3,2},{4,5},{5,4},{6,7},{7,6},{8,9},{9,8},{10,11... | collective-permute-start | bytes 7077896 | tf_op jit(solution)/shard_map/ppermute | solution.py:56
  363.7 53.4 %collective-permute-start.36 = (bf16[2,96,1536]{2,1,0:T(8,128)(2,1)}, bf16[2,96,1536]{2,1,0:T(8,128)(2,1)}, u32[]{:S(2)}, u32[]{:S(2)}) collective-permute-start(bf16[2,96,1536]{2,1,0:T(8,128)(2,1)} %get-tuple-element.279), channel_id=1, source_target_pairs={{0,2},{1,3},{2,0},{3,1},{4,6},{5,7},{6,4},{7,5},{8,10},{9,11},{10,... | collective-permute-start | bytes 1769480 | tf_op jit(solution)/shard_map/ppermute | solution.py:56
  363.7 53.4 %collective-permute-start.37 = (bf16[2,96,1536]{2,1,0:T(8,128)(2,1)}, bf16[2,96,1536]{2,1,0:T(8,128)(2,1)}, u32[]{:S(2)}, u32[]{:S(2)}) collective-permute-start(bf16[2,96,1536]{2,1,0:T(8,128)(2,1)} %get-tuple-element.278), channel_id=1, source_target_pairs={{0,4},{1,5},{2,6},{3,7},{4,0},{5,1},{6,2},{7,3},{8,12},{9,13},{10,... | collective-permute-start | bytes 1769480 | tf_op jit(solution)/shard_map/ppermute | solution.py:56
  365.2 97.8 %collective-permute-start.42 = (bf16[2,96,1536]{2,1,0:T(8,128)(2,1)}, bf16[2,96,1536]{2,1,0:T(8,128)(2,1)}, u32[]{:S(2)}, u32[]{:S(2)}) collective-permute-start(bf16[2,96,1536]{2,1,0:T(8,128)(2,1)} %get-tuple-element.277), channel_id=1, source_target_pairs={{0,6},{1,7},{2,4},{3,5},{4,2},{5,3},{6,0},{7,1},{8,14},{9,15},{10,... | collective-permute-start | bytes 1769480 | tf_op jit(solution)/shard_map/ppermute | solution.py:56
  399.5 46.5 %collective-permute-start.38 = (bf16[256,768]{1,0:T(8,128)(2,1)}, bf16[256,768]{1,0:T(8,128)(2,1)S(1)}, u32[]{:S(2)}, u32[]{:S(2)}) collective-permute-start(bf16[256,768]{1,0:T(8,128)(2,1)} %pad_maximum_fusion.12), channel_id=1, source_target_pairs={{0,1},{1,2},{2,3},{3,4},{4,5},{5,6},{6,7},{7,8},{8,9},{9,10},{10,1... | collective-permute-start | bytes 1179656 | tf_op jit(solution)/shard_map/ppermute | solution.py:45
  410.2 35.9 %collective-permute-start.39 = (bf16[256,768]{1,0:T(8,128)(2,1)}, bf16[256,768]{1,0:T(8,128)(2,1)S(1)}, u32[]{:S(2)}, u32[]{:S(2)}) collective-permute-start(bf16[256,768]{1,0:T(8,128)(2,1)} %pad_maximum_fusion.13), channel_id=1, source_target_pairs={{1,0},{2,1},{3,2},{4,3},{5,4},{6,5},{7,6},{8,7},{9,8},{10,9},{11,1... | collective-permute-start | bytes 1179656 | tf_op jit(solution)/shard_map/ppermute | solution.py:45
  486.3 33.2 %collective-permute-start.30 = (bf16[480,768]{1,0:T(8,128)(2,1)}, bf16[480,768]{1,0:T(8,128)(2,1)}, u32[]{:S(2)}, u32[]{:S(2)}) collective-permute-start(bf16[480,768]{1,0:T(8,128)(2,1)} %get-tuple-element.110), channel_id=1, source_target_pairs={{0,24},{8,16},{16,8},{24,0},{1,25},{9,17},{17,9},{25,1},{2,26},{10... | collective-permute-start | bytes 2211848 | tf_op jit(solution)/shard_map/ppermute | solution.py:34
  495.2 33.6 %collective-permute-start.45 = (bf16[4,96,1664]{2,1,0:T(8,128)(2,1)}, bf16[4,96,1664]{2,1,0:T(8,128)(2,1)S(1)}, u32[]{:S(2)}, u32[]{:S(2)}) collective-permute-start(bf16[4,96,1664]{2,1,0:T(8,128)(2,1)} %dynamic-slice_bitcast_fusion.3), channel_id=1, source_target_pairs={{0,1},{1,0},{2,3},{3,2},{4,5},{5,4},{6,7},{7,6},{8,9},{9,8},{10,11... | collective-permute-start | bytes 3833864 | tf_op jit(solution)/shard_map/ppermute | solution.py:56
  505.6 82.9 %collective-permute-start.51 = (bf16[2,96,1536]{2,1,0:T(8,128)(2,1)}, bf16[2,96,1536]{2,1,0:T(8,128)(2,1)}, u32[]{:S(2)}, u32[]{:S(2)}) collective-permute-start(bf16[2,96,1536]{2,1,0:T(8,128)(2,1)} %get-tuple-element.282), channel_id=1, source_target_pairs={{0,4},{1,5},{2,6},{3,7},{4,0},{5,1},{6,2},{7,3},{8,12},{9,13},{10,... | collective-permute-start | bytes 1769480 | tf_op jit(solution)/shard_map/ppermute | solution.py:56
  507.1 81.4 %collective-permute-start.52 = (bf16[2,96,1536]{2,1,0:T(8,128)(2,1)}, bf16[2,96,1536]{2,1,0:T(8,128)(2,1)}, u32[]{:S(2)}, u32[]{:S(2)}) collective-permute-start(bf16[2,96,1536]{2,1,0:T(8,128)(2,1)} %get-tuple-element.281), channel_id=1, source_target_pairs={{0,6},{1,7},{2,4},{3,5},{4,2},{5,3},{6,0},{7,1},{8,14},{9,15},{10,... | collective-permute-start | bytes 1769480 | tf_op jit(solution)/shard_map/ppermute | solution.py:56
  531.6 46.3 %collective-permute-start.47 = (bf16[96,1664]{1,0:T(8,128)(2,1)S(1)}, bf16[96,1664]{1,0:T(8,128)(2,1)S(1)}, u32[]{:S(2)}, u32[]{:S(2)}) collective-permute-start(bf16[96,1664]{1,0:T(8,128)(2,1)S(1)} %get-tuple-element.286), channel_id=1, source_target_pairs={{0,4},{1,5},{2,6},{3,7},{4,0},{5,1},{6,2},{7,3},{8,12},{9,13},{10,... | collective-permute-start | bytes 958472 | tf_op jit(solution)/shard_map/ppermute | solution.py:56
  533.0 54.3 %collective-permute-start.48 = (bf16[96,1664]{1,0:T(8,128)(2,1)S(1)}, bf16[96,1664]{1,0:T(8,128)(2,1)S(1)}, u32[]{:S(2)}, u32[]{:S(2)}) collective-permute-start(bf16[96,1664]{1,0:T(8,128)(2,1)S(1)} %get-tuple-element.285), channel_id=1, source_target_pairs={{0,6},{1,7},{2,4},{3,5},{4,2},{5,3},{6,0},{7,1},{8,14},{9,15},{10,... | collective-permute-start | bytes 958472 | tf_op jit(solution)/shard_map/ppermute | solution.py:56
  599.9 43.5 %collective-permute-start.53 = (bf16[2,96,3072]{2,1,0:T(8,128)(2,1)}, bf16[2,96,3072]{2,1,0:T(8,128)(2,1)}, u32[]{:S(2)}, u32[]{:S(2)}) collective-permute-start(bf16[2,96,3072]{2,1,0:T(8,128)(2,1)} %get-tuple-element.288), channel_id=1, source_target_pairs={{0,8},{8,0},{16,24},{24,16},{1,9},{9,1},{17,25},{25,17},{2,10},{10... | collective-permute-start | bytes 3538952 | tf_op jit(solution)/shard_map/ppermute | solution.py:34
  (103 other events, 1264.2 us)

commit v5 on v4

--- a/solution.py
+++ b/solution.py
@@ -15,9 +15,10 @@
 RATES = (0.5, 0.08, 0.6, 0.06, 0.08, 0.15)
 LANES = 128
 QB = 128
-HALO = 256
+HALO = 208
 SPAN = QB + 2 * HALO
 TAIL = 16
+BLOCK = 768
 HALVES = 2
 CORE_BIT = 1
 CHIP_BIT = 2
@@ -25,6 +26,7 @@
 BF16 = jnp.bfloat16
 EXPERT_COST = pl.CostEstimate(flops=28 * 10**9, bytes_accessed=10**5, transcendentals=0)
 ATTEND_COST = pl.CostEstimate(flops=30 * 10**9, bytes_accessed=10**5, transcendentals=0)
+UPDATE_COST = pl.CostEstimate(flops=10**10, bytes_accessed=10**5, transcendentals=0)
 BACK_COST = pl.CostEstimate(flops=15 * 10**9, bytes_accessed=10**5, transcendentals=0)
 NT = (((1,), (1,)), ((), ()))
 
@@ -330,7 +332,8 @@
     return pre * below, below + pre * (bell * 0.3989422804014327)
 
 
-def pack_kernel(rows_ref, rank_ref, *out_refs):
+def pack_kernel(count, rows_ref, rank_ref, *refs):
+    out_refs = refs[-count:]
     slots, tokens = out_refs[0].shape[0], rows_ref.shape[0]
     slot = lax.broadcasted_iota(jnp.int32, (slots, tokens), 0)
     for at, out_ref in enumerate(out_refs):
@@ -338,17 +341,17 @@
         out_ref[...] = jnp.dot(spots, rows_ref[...], preferred_element_type=F32).astype(BF16)
 
 
-def pack(rows, ranks, slots):
+def pack(rows, ranks, slots, after=()):
     count, width = ranks.shape[0], rows.shape[1]
     near_by = pl.BlockSpec(memory_space=pltpu.VMEM)
     return pl.pallas_call(
-        pack_kernel,
-        in_specs=[near_by, near_by],
+        partial(pack_kernel, count),
+        in_specs=[near_by, near_by] + [pl.BlockSpec(memory_space=pl.ANY)] * len(after),
         out_specs=[near_by] * count,
         out_shape=[jax.ShapeDtypeStruct((slots, width), BF16)] * count,
         compiler_params=pltpu.CompilerParams(vmem_limit_bytes=56 * 2**20),
         name="pack",
-    )(rows, ranks)
+    )(rows, ranks, *after)
 
 
 def token_spots(rank_col, slots):
@@ -564,7 +567,7 @@
     slots, width = x_parts[0].shape
     group = lax.axis_size("group")
     columns = sources[0].shape[-1]
-    hidden = 512 if columns % 512 == 0 else columns
+    hidden = BLOCK if columns % BLOCK == 0 else columns
     raw = pl.BlockSpec(memory_space=pl.ANY)
     first, with_grads = len(before) == 0, len(other) > 0
     others = len(other[0]) if with_grads else 0
@@ -621,6 +624,49 @@
     return (*split, outs[-1]) if with_grads else split
 
 
+def update_kernel(base, mine_ref, *refs):
+    states, grads, outs = refs[:6], refs[6:10], refs[-6:]
+    half = grads[0].shape[-1]
+    for at in range(2):
+
+        @pl.when(pl.program_id(0) == at)
+        def _():
+            for matrix in range(2):
+                weight, moment, squares = states[3 * matrix : 3 * matrix + 3]
+                for part in range(2):
+                    columns = slice(part * half, (part + 1) * half)
+                    new = adam_step(
+                        weight[0, :, columns],
+                        moment[0, :, columns],
+                        squares[0, :, columns],
+                        grads[2 * at + part][matrix].astype(F32),
+                        RATES[4 + matrix],
+                    )
+                    for out, value in zip(outs[3 * matrix : 3 * matrix + 3], new):
+                        out[0, :, columns] = value
+
+
+def update_experts(mine, base, states, grads, done=()):
+    shape = states[0].shape
+    block = pl.BlockSpec((1, *shape[1:]), lambda i, at: (at[0] ^ (base + i), 0, 0))
+    whole = pl.BlockSpec(grads[0].shape, lambda i, at: (0, 0, 0))
+    raw = pl.BlockSpec(memory_space=pl.ANY)
+    return pl.pallas_call(
+        partial(update_kernel, base),
+        grid_spec=pltpu.PrefetchScalarGridSpec(
+            num_scalar_prefetch=1,
+            grid=(2,),
+            in_specs=[block] * 6 + [whole] * 4 + [raw] * len(done),
+            out_specs=[block] * 6,
+        ),
+        out_shape=[jax.ShapeDtypeStruct(shape, F32)] * 6,
+        input_output_aliases={11 + at: at for at in range(len(done))},
+        compiler_params=pltpu.CompilerParams(vmem_limit_bytes=56 * 2**20),
+        cost_estimate=UPDATE_COST,
+        name="update_experts",
+    )(jnp.reshape(mine, (1,)), *states, *grads, *done)
+
+
 def per_device(
     block_input,
     out_grad,
@@ -699,7 +745,9 @@
     group = far * near
     far_pieces = [gather_far(tie(expert_cut(0), qkv_far[-1]))]
     far_pieces.append(gather_far(tie(expert_cut(1), far_pieces[0][-1])))
-    dy_parts = exchange(pack(out_grad, ranks, capacity))
+    dy_parts = exchange(
+        pack(out_grad, ranks, capacity, (far_pieces[0][1], far_pieces[0][3]))
+    )
     qkv_full, small_full = dense_place(qkv_far)
     proj_full, _ = dense_place(proj_far, tuple(dy_parts[2:]))
     small_rows = small_full[:, :8].T
@@ -735,7 +783,7 @@
         for j in range(expert_count)
     ]
 
-    x_parts = exchange(pack(second_in, ranks, capacity))
+    x_parts = exchange(pack(second_in, ranks, capacity, (far_pieces[1][1],)))
 
     def run(at, part, before=(), other=(), after=()):
         return expert(
@@ -860,20 +908,13 @@
     got = swap(lax.dynamic_index_in_dim(dense_grads, 1 - core, 0, keepdims=False), CORE_BIT)
     dense_half = summed([lax.dynamic_index_in_dim(dense_grads, core, 0, keepdims=False), got])
     dense_near = scatter_near(dense_half.reshape(group, width // group, -1))
-    owned = jnp.concatenate(
-        [
-            summed([tie(parts[0], dense_near), *parts[1:]])
-            for parts in (low_parts, high_parts)
-        ],
-        axis=2,
-    )
-    owned = sum_chips(owned, expert_count)
+    owned = []
+    for parts, wait_for in ((low_parts, qkv_grad), (high_parts, dense_near)):
+        share = sum_chips(summed([tie(parts[0], wait_for), *parts[1:]]), expert_count)
+        other_chip = swap(share, CHIP_BIT)
+        owned.append([share, swap(share, CORE_BIT), other_chip, swap(other_chip, CORE_BIT)])
     dense_half = sum_chips(summed(far_parts(dense_near)), CHIP_BIT)
     low, high = [part.astype(F32) for part in halves(dense_half, swap(dense_half, CORE_BIT), core)]
-
-    other_chip = swap(owned, CHIP_BIT)
-    parts = [owned, swap(owned, CORE_BIT), other_chip, swap(other_chip, CORE_BIT)]
-    expert_sum = jnp.stack([pick(parts, mine ^ e) for e in range(expert_count)]).astype(F32)
 
     small_sum = low[:, columns + width // 2 :][:, :8]
     qkv_sum = jnp.concatenate([low[:, :columns], high[:, :columns]], axis=1)
@@ -886,14 +927,20 @@
     router_new = adam_step(
         router_weight, router_moment, router_squares, small_sum[:, 4:8], RATES[3]
     )
-    inner_new = adam_step(inner_weight, inner_moment, inner_squares, expert_sum[:, 0], RATES[4])
-    outer_new = adam_step(
-        outer_weight,
-        outer_moment,
-        outer_squares,
-        expert_sum[:, 1].transpose(0, 2, 1),
-        RATES[5],
-    )
+    states = (
+        inner_weight,
+        inner_moment,
+        inner_squares,
+        outer_weight.transpose(0, 2, 1),
+        outer_moment.transpose(0, 2, 1),
+        outer_squares.transpose(0, 2, 1),
+    )
+    done = ()
+    for base in range(0, expert_count, 2):
+        grads = [owned[part][base + at] for at in range(2) for part in range(2)]
+        done = update_experts(mine, base, states, grads, done)
+    inner_new = done[:3]
+    outer_new = [array.transpose(0, 2, 1) for array in done[3:]]
     return (
         block_output,
         input_grad,

time: 673 us -> 662 us (0.984)
  waiting for transfers between devices: 221 us -> 196 us
  other arithmetic: 70.2 us -> 50.8 us
  Pallas kernels: 193 us -> 212 us
  local copies, waits for them, and re-layouts: 67.5 us -> 74.5 us
    pallas_call x2 -> x4, Pallas kernels: 9.2 us -> 34.4 us  [the longest x2 25.2 us: update_experts(): pl.pallas_call(partial(update_kernel, base), grid_spec=pltpu.PrefetchScal...]
    ppermute x6, waiting for transfers between devices: 34 us -> 10.3 us  [shift(): return (lax.ppermute(tail, axes, up), lax.ppermute(head, axes, down))]
    sub x6 -> x4, other arithmetic: 22.4 us -> 5.71 us  [adam_step(): weight - rate_value * (first_hat / (jnp.sqrt(second_hat) + 1e-08) + 0.1 *...]
    ppermute x22 -> x25, waiting for transfers between devices: 46.3 us -> 32.3 us  [swap(): return lax.ppermute(block, 'replica', [(r, r ^ bit) for r in range(count)])]
    ppermute x22 -> x25, starting transfers between devices: 25.7 us -> 39.5 us  [swap(): return lax.ppermute(block, 'replica', [(r, r ^ bit) for r in range(count)])]
    ppermute x28, waiting for transfers between devices: 140 us -> 153 us  [group_swap(): return lax.ppermute(block, 'group', [(g, g ^ flip) for g in range(count)])]
    ppermute x6, starting transfers between devices: 24.6 us -> 17.1 us  [shift(): return (lax.ppermute(tail, axes, up), lax.ppermute(head, axes, down))]
    unnamed x171 -> x169, local copies, waits for them, and re-layouts: 21.1 us -> 23.4 us
  transfers between devices with their start and end apart: 56 -> 59, of which waited for: 20 -> 21; matrix products, arithmetic and copies ran while one was open for 17% -> 19% of each run, Pallas kernels for 29% -> 31%
where the time goes in v5:
time: 662 us; the launch traced here: 652 us
  Pallas kernels  212 us (32%)
  waiting for transfers between devices  196 us (30%)
  starting transfers between devices  89.5 us (14%)
  local copies, waits for them, and re-layouts  74.5 us (11%)
  other arithmetic  50.8 us (8%)
  matrix products  27.6 us (4%)
    ppermute x28, waiting for transfers between devices, group_swap(): return lax.ppermute(block, 'group', [(g, g ^ flip) for g in range(count)])  153 us
    pallas_call x4, Pallas kernels, expert(): pl.pallas_call(partial(expert_kernel, count, others, near, first, expert_...  107 us
    ppermute x25, starting transfers between devices, swap(): return lax.ppermute(block, 'replica', [(r, r ^ bit) for r in range(count)])  39.5 us
    ppermute x28, starting transfers between devices, group_swap(): return lax.ppermute(block, 'group', [(g, g ^ flip) for g in range(count)])  32.8 us
    ppermute x25, waiting for transfers between devices, swap(): return lax.ppermute(block, 'replica', [(r, r ^ bit) for r in range(count)])  32.3 us
    pallas_call x2, Pallas kernels, update_experts(): pl.pallas_call(partial(update_kernel, base), grid_spec=pltpu.PrefetchScal...  25.2 us
    pallas_call x2, Pallas kernels, attend_back(): pl.pallas_call(partial(attend_back_kernel, scale), grid=(count,), in_spec...  25.1 us
    pallas_call x1, Pallas kernels, attend(): pl.pallas_call(partial(attend_kernel, scale), grid=(pairs,), in_specs=[pl...  23.8 us
  transfers between devices with their start and end apart: 59, of which 21 were waited for; matrix products, arithmetic and copies ran while one was open for 19% of the time, Pallas kernels for 31%

profile of v5, /device:TPU:23, one launch (start us, length us, event | category | flops | bytes accessed | tf_op | source)
XLA Modules:
  0.0 652.5 jit_solution(15429001110226166687)
XLA Ops:
  12.3 14.5 %collective-permute-done.2.refs_1_ = bf16[96,1280]{1,0:T(8,128)(2,1)S(1)} collective-permute-done((bf16[96,1280]{1,0:T(8,128)(2,1)S(1)}, bf16[96,1280]{1,0:T(8,128)(2,1)S(1)}, u32[]{:S(2)}, u32[]{:S(2)}) %collective-permute-start.2) | collective-permute-done | bytes 245792 | tf_op jit(solution)/shard_map/ppermute | solution.py:58
  36.2 13.0 %collective-permute-done.3.refs_1_ = bf16[4,96,1280]{2,1,0:T(8,128)(2,1)} collective-permute-done((bf16[4,96,1280]{2,1,0:T(8,128)(2,1)S(1)}, bf16[4,96,1280]{2,1,0:T(8,128)(2,1)}, u32[]{:S(2)}, u32[]{:S(2)}) %collective-permute-start.3) | collective-permute-done | bytes 983072 | tf_op jit(solution)/shard_map/ppermute | solution.py:58
  67.7 5.5 convolution_convert_fusion.1.q_ref
  84.1 30.3 %collective-permute-done.11.refs_1_ = bf16[4,96,512]{2,1,0:T(8,128)(2,1)} collective-permute-done((bf16[4,96,512]{2,1,0:T(8,128)(2,1)S(1)}, bf16[4,96,512]{2,1,0:T(8,128)(2,1)}, u32[]{:S(2)}, u32[]{:S(2)}) %collective-permute-start.11) | collective-permute-done | bytes 393248 | tf_op jit(solution)/shard_map/ppermute | solution.py:58
  118.2 4.6 pack.2
  129.7 23.8 %attend.1 = (bf16[768,768]{1,0:T(8,128)(2,1)}, f32[6,8,256]{2,1,0:T(8,128)}) custom-call(bf16[768,2304]{1,0:T(8,128)(2,1)} %copy-done.26, bf16[1184,1536]{1,0:T(8,128)(2,1)} %pad_maximum_fusion.k_ref.v_ref, bf16[1184,1536]{1,0:T(8,128)(2,1)} %pad_maximum_fusion.k_ref.v_ref, s32[6,256]{1,0:T(8,128)} %bitcast.206, s32[6,256]{1,0:T(8,128)} %bitcast.203), custom_call_target="tpu_custom_call" | custom-call | flops 30000001024 | bytes 100000 | tf_op jit(solution)/shard_map/attend/pallas_call | solution.py:258
  169.7 6.0 collective-permute-done.18.refs_0_
  176.6 4.6 pack.3
  194.5 17.4 %collective-permute-done.22.refs_5_ = bf16[4,2,96,1536]{3,2,1,0:T(8,128)(2,1)} collective-permute-done((bf16[4,2,96,1536]{3,2,1,0:T(8,128)(2,1)}, bf16[4,2,96,1536]{3,2,1,0:T(8,128)(2,1)}, u32[]{:S(2)}, u32[]{:S(2)}) %collective-permute-start.22) | collective-permute-done | bytes 2359328 | tf_op jit(solution)/shard_map/ppermute | solution.py:58
  211.8 19.1 %expert.4 = (f32[480,768]{1,0:T(8,128)}, f32[480,768]{1,0:T(8,128)}, f32[480,768]{1,0:T(8,128)}, f32[480,768]{1,0:T(8,128)}, bf16[480,768]{1,0:T(8,128)(2,1)}, /...) custom-call(s32[4]{0:T(128)} %pad_add_fusion.place_ref, ...), custom_call_target="tpu_custom_call" | custom-call | flops 28000000000 | bytes 100000 | tf_op jit(solution)/shard_map/expert/pallas_call | solution.py:594
  230.9 7.1 %collective-permute-done.23 = bf16[2,96,1536]{2,1,0:T(8,128)(2,1)} collective-permute-done((bf16[2,96,1536]{2,1,0:T(8,128)(2,1)S(1)}, bf16[2,96,1536]{2,1,0:T(8,128)(2,1)}, u32[]{:S(2)}, u32[]{:S(2)}) %collective-permute-start.23) | collective-permute-done | bytes 589856 | tf_op jit(solution)/shard_map/ppermute | solution.py:58
  240.9 31.7 %expert.5 = (f32[480,768]{1,0:T(8,128)}, f32[480,768]{1,0:T(8,128)}, f32[480,768]{1,0:T(8,128)}, f32[480,768]{1,0:T(8,128)}, bf16[480,768]{1,0:T(8,128)(2,1)}, /...) custom-call(s32[4]{0:T(128)} %pad_add_fusion.place_ref, bf16[768,128]{1,0:T(8,128)(2,1)} %pad.16.router_ref, ...), custom_call_target="tpu_custom_call" | custom-call | flops 28000000000 | bytes 100000 | tf_op jit(solution)/shard_map/expert/pallas_call | solution.py:594
  277.4 15.9 %collective-permute-done.25.refs_7_.refs_3_ = bf16[4,2,96,1536]{3,2,1,0:T(8,128)(2,1)} collective-permute-done((bf16[4,2,96,1536]{3,2,1,0:T(8,128)(2,1)}, bf16[4,2,96,1536]{3,2,1,0:T(8,128)(2,1)}, u32[]{:S(2)}, u32[]{:S(2)}) %collective-permute-start.25) | collective-permute-done | bytes 2359328 | tf_op jit(solution)/shard_map/ppermute | solution.py:58
  293.2 29.1 %expert.6 = (bf16[480,768]{1,0:T(8,128)(2,1)}, bf16[480,768]{1,0:T(8,128)(2,1)}, bf16[480,768]{1,0:T(8,128)(2,1)}, bf16[496,768]{1,0:T(8,128)(2,1)}, bf16[496,76...) custom-call(s32[4]{0:T(128)} %pad_add_fusion.place_ref, ...), custom_call_target="tpu_custom_call" | custom-call | flops 28000000000 | bytes 100000 | tf_op jit(solution)/shard_map/expert/pallas_call | solution.py:594
  327.0 27.4 %expert.7 = (bf16[480,768]{1,0:T(8,128)(2,1)}, bf16[496,768]{1,0:T(8,128)(2,1)}, bf16[2,768,1536]{2,1,0:T(8,128)(2,1)}) custom-call(s32[4]{0:T(128)} %pad_add_fusion.place_ref, bf16[768,128]{1,0:T(8,128)(2,1)} %pad.16.router_ref, bf16[480,768]{1,0:T(8,128)(2,1)} %get-tuple-element.91.refs_0_.refs_6_, bf16[480,768]{1,0:T(8,128)(2,1)} %get-tuple-element.92.refs_2_.refs_1_, ...), custom_call_target="tpu_custom_call" | custom-call | flops 28000000000 | bytes 100000 | tf_op jit(solution)/shard_map/expert/pallas_call | solution.py:594
  354.5 5.0 dynamic-slice_bitcast_fusion.1
  370.2 7.1 %unpack_grad.1 = (f32[768,768]{1,0:T(8,128)}, f32[768,128]{1,0:T(8,128)}) custom-call(bf16[496,768]{1,0:T(8,128)(2,1)} %get-tuple-element.123.refs_0_, bf16[496,768]{1,0:T(8,128)(2,1)} %collective-permute-done.31.refs_1_, bf16[496,768]{1,0:T(8,128)(2,1)} %collective-permute-done.32.refs_2_, bf16[496,768]{1,0:T(8,128)(2,1)} %collective-permute-done.33.refs_3_, ...), custom_call_target="tpu_custom_call" | custom-call | tf_op jit(solution)/shard_map/unpack_grad/pallas_call | solution.py:386
  386.6 12.5 %attend_back.2 = (bf16[768,384]{1,0:T(8,128)(2,1)}, bf16[1184,384]{1,0:T(8,128)(2,1)}, bf16[1184,384]{1,0:T(8,128)(2,1)}) custom-call(bf16[768,2304]{1,0:T(8,128)(2,1)} %copy-done.26, bf16[1184,1536]{1,0:T(8,128)(2,1)} %pad_maximum_fusion.k_ref.v_ref, bf16[1184,1536]{1,0:T(8,128)(2,1)} %pad_maximum_fusion.k_ref.v_ref, ...), custom_call_target="tpu_custom_call" | custom-call | flops 15000000512 | bytes 100000 | tf_op jit(solution)/shard_map/attend_back/pallas_call | solution.py:290
  410.2 9.2 %collective-permute-done.35 = bf16[2,4,96,1536]{3,2,1,0:T(8,128)(2,1)} collective-permute-done((bf16[2,4,96,1536]{3,2,1,0:T(8,128)(2,1)}, bf16[2,4,96,1536]{3,2,1,0:T(8,128)(2,1)}, u32[]{:S(2)}, u32[]{:S(2)}) %collective-permute-start.35) | collective-permute-done | bytes 2359328 | tf_op jit(solution)/shard_map/ppermute | solution.py:58
  425.0 12.5 %attend_back.3 = (bf16[768,384]{1,0:T(8,128)(2,1)}, bf16[1184,384]{1,0:T(8,128)(2,1)}, bf16[1184,384]{1,0:T(8,128)(2,1)}) custom-call(bf16[768,2304]{1,0:T(8,128)(2,1)} %copy-done.26, bf16[1184,1536]{1,0:T(8,128)(2,1)} %pad_maximum_fusion.k_ref.v_ref, bf16[1184,1536]{1,0:T(8,128)(2,1)} %pad_maximum_fusion.k_ref.v_ref, ...), custom_call_target="tpu_custom_call" | custom-call | flops 15000000512 | bytes 100000 | tf_op jit(solution)/shard_map/attend_back/pallas_call | solution.py:290
  448.6 7.0 %collective-permute-done.41 = bf16[208,768]{1,0:T(8,128)(2,1)S(1)} collective-permute-done((bf16[208,768]{1,0:T(8,128)(2,1)S(1)}, bf16[208,768]{1,0:T(8,128)(2,1)S(1)}, u32[]{:S(2)}, u32[]{:S(2)}) %collective-permute-start.41) | collective-permute-done | bytes 319520 | tf_op jit(solution)/shard_map/ppermute | solution.py:47
  465.2 7.8 %fusion.23 = (bf16[768]{0:T(1024)(128)(2,1)S(1)}, f32[768]{0:T(1024)S(1)}, f32[768]{0:T(1024)S(1)}, bf16[768]{0:T(1024)(128)(2,1)S(1)}, f32[768,768]{1,0:T(8,128)}) fusion(bf16[768,768]{1,0:T(8,128)(2,1)S(1)} %copy-done.10, f32[768]{0:T(1024)S(1)} %copy-done.63, f32[768]{0:T(1024)S(1)} %copy-done.57, f32[768]{0:T(1024)S(1)} %copy-done.61, ...), kind=kOutput, calls=%fused_computation.39 | convolution fusion | flops 2723804160 | bytes 10635264 | tf_op jit(solution)/shard_map/dot_general | solution.py:887
  490.6 6.9 %collective-permute-start.29 = (bf16[480,768]{1,0:T(8,128)(2,1)}, bf16[480,768]{1,0:T(8,128)(2,1)}, u32[]{:S(2)}, u32[]{:S(2)}) collective-permute-start(bf16[480,768]{1,0:T(8,128)(2,1)} %get-tuple-element.121), channel_id=1, source_target_pairs={{0,16},{8,24},{16,0},{24,8},{1,17},{9,25},{17,1},{25,9},{2,18},{10... | collective-permute-start | bytes 2211848 | tf_op jit(solution)/shard_map/ppermute | solution.py:36
  509.2 5.0 collective-permute-done.29.refs_2_
  514.2 16.3 %collective-permute-done.30.refs_3_ = bf16[480,768]{1,0:T(8,128)(2,1)} collective-permute-done((bf16[480,768]{1,0:T(8,128)(2,1)}, bf16[480,768]{1,0:T(8,128)(2,1)}, u32[]{:S(2)}, u32[]{:S(2)}) %collective-permute-start.30) | collective-permute-done | bytes 737312 | tf_op jit(solution)/shard_map/ppermute | solution.py:36
  530.5 7.1 %unpack_out.1 = bf16[768,768]{1,0:T(8,128)(2,1)} custom-call(f32[768,768]{1,0:T(8,128)} %copy-done, bf16[480,768]{1,0:T(8,128)(2,1)} %get-tuple-element.119.refs_0_, bf16[480,768]{1,0:T(8,128)(2,1)} %copy-done.50, bf16[480,768]{1,0:T(8,128)(2,1)} %collective-permute-done.29.refs_2_, bf16[480,768]{1,0:T(8,128)(2,1)} %collective-permute-done.30.refs_3_, ...), custom_call_target="tpu_custom_call" | custom-call | tf_op jit(solution)/shard_map/unpack_out/pallas_call | solution.py:412
  548.7 17.3 %collective-permute-done.52 = bf16[2,96,1536]{2,1,0:T(8,128)(2,1)S(1)} collective-permute-done((bf16[2,96,1536]{2,1,0:T(8,128)(2,1)}, bf16[2,96,1536]{2,1,0:T(8,128)(2,1)S(1)}, u32[]{:S(2)}, u32[]{:S(2)}) %collective-permute-start.52) | collective-permute-done | bytes 589856 | tf_op jit(solution)/shard_map/ppermute | solution.py:58
  572.3 9.5 %collective-permute-done.48 = bf16[96,1664]{1,0:T(8,128)(2,1)S(1)} collective-permute-done((bf16[96,1664]{1,0:T(8,128)(2,1)S(1)}, bf16[96,1664]{1,0:T(8,128)(2,1)S(1)}, u32[]{:S(2)}, u32[]{:S(2)}) %collective-permute-start.48) | collective-permute-done | bytes 319520 | tf_op jit(solution)/shard_map/ppermute | solution.py:58
  590.2 6.2 collective-permute-done.54.refs_7_
  598.5 4.7 collective-permute-done.49
  605.6 12.6 %update_experts.2 = (f32[4,96,3072]{2,1,0:T(8,128)}, f32[4,96,3072]{2,1,0:T(8,128)}, f32[4,96,3072]{2,1,0:T(8,128)}, f32[4,96,3072]{2,1,0:T(8,128)}, f32[4,96,3072]{2,1,0:T(8,128)}, /*index=5*/f32[4,96,3072]{2,1,0:T(8,128)}) custom-call(s32[1]{0:T(128)} %bitcast.3.mine_ref, f32[4,96,3072]{2,1,0:T(8,128)} %refs_0_.3, f32[4,96,3072]{2,1,0:T(8,128)} %refs_1_.3, ...), custom_call_target="tpu_custom_call" | custom-call | flops 10000000000 | bytes 100000 | tf_op jit(solution)/shard_map/update_experts/pallas_call | solution.py:654
  639.3 12.6 %update_experts.3 = (f32[4,96,3072]{2,1,0:T(8,128)}, f32[4,96,3072]{2,1,0:T(8,128)}, f32[4,96,3072]{2,1,0:T(8,128)}, f32[4,96,3072]{2,1,0:T(8,128)}, f32[4,96,3072]{2,1,0:T(8,128)}, /*index=5*/f32[4,96,3072]{2,1,0:T(8,128)}) custom-call(s32[1]{0:T(128)} %bitcast.3.mine_ref, ...), custom_call_target="tpu_custom_call", output_to_operand_aliasing={{0}: (11, {}), {1}: (12, {}), {2}: (13, {}), {3}: (14, {}),... | custom-call | flops 10000000000 | bytes 100000 | tf_op jit(solution)/shard_map/update_experts/pallas_call | solution.py:654
  (419 shorter events, 240.7 us)
Async XLA Ops:
  2.4 71.8 %collective-permute-start.9 = (bf16[96,512]{1,0:T(8,128)(2,1)}, bf16[96,512]{1,0:T(8,128)(2,1)S(1)}, u32[]{:S(2)}, u32[]{:S(2)}) collective-permute-start(bf16[96,512]{1,0:T(8,128)(2,1)} %get-tuple-element.322), channel_id=1, source_target_pairs={{0,4},{1,5},{2,6},{3,7},{4,0},{5,1},{6,2},{7,3},{8,12},{9,13},{10,... | collective-permute-start | bytes 294920 | tf_op jit(solution)/shard_map/ppermute | solution.py:58
  2.4 73.7 %collective-permute-start.8 = (bf16[96,512]{1,0:T(8,128)(2,1)}, bf16[96,512]{1,0:T(8,128)(2,1)}, u32[]{:S(2)}, u32[]{:S(2)}) collective-permute-start(bf16[96,512]{1,0:T(8,128)(2,1)} %get-tuple-element.322), channel_id=1, source_target_pairs={{0,2},{1,3},{2,0},{3,1},{4,6},{5,7},{6,4},{7,5},{8,10},{9,11},{10,... | collective-permute-start | bytes 294920 | tf_op jit(solution)/shard_map/ppermute | solution.py:58
  26.8 52.9 %collective-permute-start.10 = (bf16[96,512]{1,0:T(8,128)(2,1)}, bf16[96,512]{1,0:T(8,128)(2,1)}, u32[]{:S(2)}, u32[]{:S(2)}) collective-permute-start(bf16[96,512]{1,0:T(8,128)(2,1)} %get-tuple-element.322), channel_id=1, source_target_pairs={{0,6},{1,7},{2,4},{3,5},{4,2},{5,3},{6,0},{7,1},{8,14},{9,15},{10,... | collective-permute-start | bytes 294920 | tf_op jit(solution)/shard_map/ppermute | solution.py:58
  54.9 61.3 %collective-permute-start.15 = (bf16[2,96,1536]{2,1,0:T(8,128)(2,1)}, bf16[2,96,1536]{2,1,0:T(8,128)(2,1)S(1)}, u32[]{:S(2)}, u32[]{:S(2)}) collective-permute-start(bf16[2,96,1536]{2,1,0:T(8,128)(2,1)} %tie.8.refs_0_), channel_id=1, source_target_pairs={{0,6},{1,7},{2,4},{3,5},{4,2},{5,3},{6,0},{7,1},{8,14},{9,15},{10,... | collective-permute-start | bytes 1769480 | tf_op jit(solution)/shard_map/ppermute | solution.py:58
  58.7 58.7 %collective-permute-start.14 = (bf16[2,96,1536]{2,1,0:T(8,128)(2,1)}, bf16[2,96,1536]{2,1,0:T(8,128)(2,1)S(1)}, u32[]{:S(2)}, u32[]{:S(2)}) collective-permute-start(bf16[2,96,1536]{2,1,0:T(8,128)(2,1)} %tie.8.refs_0_), channel_id=1, source_target_pairs={{0,2},{1,3},{2,0},{3,1},{4,6},{5,7},{6,4},{7,5},{8,10},{9,11},{10,... | collective-permute-start | bytes 1769480 | tf_op jit(solution)/shard_map/ppermute | solution.py:58
  74.2 50.5 %collective-permute-start.6 = (bf16[208,1536]{1,0:T(8,128)(2,1)}, bf16[208,1536]{1,0:T(8,128)(2,1)}, u32[]{:S(2)}, u32[]{:S(2)}) collective-permute-start(bf16[208,1536]{1,0:T(8,128)(2,1)} %get-tuple-element.288), channel_id=1, source_target_pairs={{0,1},{1,2},{2,3},{3,4},{4,5},{5,6},{6,7},{7,8},{8,9},{9,10},{10,1... | collective-permute-start | bytes 1916936 | tf_op jit(solution)/shard_map/ppermute | solution.py:47
  76.1 48.6 %collective-permute-start.7 = (bf16[208,1536]{1,0:T(8,128)(2,1)S(1)}, bf16[208,1536]{1,0:T(8,128)(2,1)}, u32[]{:S(2)}, u32[]{:S(2)}) collective-permute-start(bf16[208,1536]{1,0:T(8,128)(2,1)S(1)} %get-tuple-element.289), channel_id=1, source_target_pairs={{1,0},{2,1},{3,2},{4,3},{5,4},{6,5},{7,6},{8,7},{9,8},{10,9},{11,1... | collective-permute-start | bytes 1916936 | tf_op jit(solution)/shard_map/ppermute | solution.py:47
  114.3 46.4 %collective-permute-start.12 = (bf16[4,96,512]{2,1,0:T(8,128)(2,1)S(1)}, bf16[4,96,512]{2,1,0:T(8,128)(2,1)}, u32[]{:S(2)}, u32[]{:S(2)}) collective-permute-start(bf16[4,96,512]{2,1,0:T(8,128)(2,1)S(1)} %pad_maximum_fusion.9.refs_0_), channel_id=1, source_target_pairs={{0,8},{8,0},{16,24},{24,16},{1,9},{9,1},{17,25},{25,17},{2,10},{10... | collective-permute-start | bytes 1179656 | tf_op jit(solution)/shard_map/ppermute | solution.py:36
  117.4 44.8 %collective-permute-start.13 = (bf16[4,96,512]{2,1,0:T(8,128)(2,1)}, bf16[4,96,512]{2,1,0:T(8,128)(2,1)}, u32[]{:S(2)}, u32[]{:S(2)}) collective-permute-start(bf16[4,96,512]{2,1,0:T(8,128)(2,1)} %collective-permute-done.11.refs_1_), channel_id=1, source_target_pairs={{0,8},{8,0},{16,24},{24,16},{1,9},{9,1},{17,25},{25,17},{2,10},{10... | collective-permute-start | bytes 1179656 | tf_op jit(solution)/shard_map/ppermute | solution.py:36
  124.7 38.0 %collective-permute-start.16 = (bf16[480,768]{1,0:T(8,128)(2,1)}, bf16[480,768]{1,0:T(8,128)(2,1)}, u32[]{:S(2)}, u32[]{:S(2)}) collective-permute-start(bf16[480,768]{1,0:T(8,128)(2,1)} %get-tuple-element.88), channel_id=1, source_target_pairs={{0,16},{8,24},{16,0},{24,8},{1,17},{9,25},{17,1},{25,9},{2,18},{10... | collective-permute-start | bytes 2211848 | tf_op jit(solution)/shard_map/ppermute | solution.py:36
  157.5 54.3 %collective-permute-start.22 = (bf16[4,2,96,1536]{3,2,1,0:T(8,128)(2,1)}, bf16[4,2,96,1536]{3,2,1,0:T(8,128)(2,1)}, u32[]{:S(2)}, u32[]{:S(2)}) collective-permute-start(bf16[4,2,96,1536]{3,2,1,0:T(8,128)(2,1)} %pad_maximum_fusion.1.refs_4_), channel_id=1, source_target_pairs={{0,1},{1,0},{2,3},{3,2},{4,5},{5,4},{6,7},{7,6},{8,9},{9,8},{10,11... | collective-permute-start | bytes 7077896 | tf_op jit(solution)/shard_map/ppermute | solution.py:58
  187.2 43.7 %collective-permute-start.24 = (bf16[2,96,1536]{2,1,0:T(8,128)(2,1)S(1)}, bf16[2,96,1536]{2,1,0:T(8,128)(2,1)S(1)}, u32[]{:S(2)}, u32[]{:S(2)}) collective-permute-start(bf16[2,96,1536]{2,1,0:T(8,128)(2,1)S(1)} %copy-done.17), channel_id=1, source_target_pairs={{0,6},{1,7},{2,4},{3,5},{4,2},{5,3},{6,0},{7,1},{8,14},{9,15},{10,... | collective-permute-start | bytes 1769480 | tf_op jit(solution)/shard_map/ppermute | solution.py:58
  187.3 50.7 %collective-permute-start.23 = (bf16[2,96,1536]{2,1,0:T(8,128)(2,1)S(1)}, bf16[2,96,1536]{2,1,0:T(8,128)(2,1)}, u32[]{:S(2)}, u32[]{:S(2)}) collective-permute-start(bf16[2,96,1536]{2,1,0:T(8,128)(2,1)S(1)} %copy-done.17), channel_id=1, source_target_pairs={{0,4},{1,5},{2,6},{3,7},{4,0},{5,1},{6,2},{7,3},{8,12},{9,13},{10,... | collective-permute-start | bytes 1769480 | tf_op jit(solution)/shard_map/ppermute | solution.py:58
  192.2 48.7 %collective-permute-start.26 = (bf16[480,768]{1,0:T(8,128)(2,1)}, bf16[480,768]{1,0:T(8,128)(2,1)}, u32[]{:S(2)}, u32[]{:S(2)}) collective-permute-start(bf16[480,768]{1,0:T(8,128)(2,1)} %get-tuple-element.98), channel_id=1, source_target_pairs={{0,16},{8,24},{16,0},{24,8},{1,17},{9,25},{17,1},{25,9},{2,18},{10... | collective-permute-start | bytes 2211848 | tf_op jit(solution)/shard_map/ppermute | solution.py:36
  192.5 48.4 %collective-permute-start.27 = (bf16[480,768]{1,0:T(8,128)(2,1)}, bf16[480,768]{1,0:T(8,128)(2,1)}, u32[]{:S(2)}, u32[]{:S(2)}) collective-permute-start(bf16[480,768]{1,0:T(8,128)(2,1)} %get-tuple-element.99), channel_id=1, source_target_pairs={{0,24},{8,16},{16,8},{24,0},{1,25},{9,17},{17,9},{25,1},{2,26},{10... | collective-permute-start | bytes 2211848 | tf_op jit(solution)/shard_map/ppermute | solution.py:36
  240.9 52.3 %collective-permute-start.25 = (bf16[4,2,96,1536]{3,2,1,0:T(8,128)(2,1)}, bf16[4,2,96,1536]{3,2,1,0:T(8,128)(2,1)}, u32[]{:S(2)}, u32[]{:S(2)}) collective-permute-start(bf16[4,2,96,1536]{3,2,1,0:T(8,128)(2,1)} %pad_maximum_fusion.2.refs_14_.refs_6_.refs_2_), channel_id=1, source_target_pairs={{0,1},{1,0},{2,3},{3,2},{4,5},{5,4},{6,7},{7,6},{8,9},{9,8},{10,11... | collective-permute-start | bytes 7077896 | tf_op jit(solution)/shard_map/ppermute | solution.py:58
  275.9 83.5 %collective-permute-start.34 = (bf16[2,4,96,1536]{3,2,1,0:T(8,128)(2,1)}, bf16[2,4,96,1536]{3,2,1,0:T(8,128)(2,1)}, u32[]{:S(2)}, u32[]{:S(2)}) collective-permute-start(bf16[2,4,96,1536]{3,2,1,0:T(8,128)(2,1)} %dynamic-slice_bitcast_fusion.2), channel_id=1, source_target_pairs={{0,1},{1,0},{2,3},{3,2},{4,5},{5,4},{6,7},{7,6},{8,9},{9,8},{10,11... | collective-permute-start | bytes 7077896 | tf_op jit(solution)/shard_map/ppermute | solution.py:58
  322.3 43.8 %collective-permute-start.31 = (bf16[496,768]{1,0:T(8,128)(2,1)}, bf16[496,768]{1,0:T(8,128)(2,1)}, u32[]{:S(2)}, u32[]{:S(2)}) collective-permute-start(bf16[496,768]{1,0:T(8,128)(2,1)} %get-tuple-element.124), channel_id=1, source_target_pairs={{0,8},{8,0},{16,24},{24,16},{1,9},{9,1},{17,25},{25,17},{2,10},{10... | collective-permute-start | bytes 2285576 | tf_op jit(solution)/shard_map/ppermute | solution.py:36
  325.3 44.9 %collective-permute-start.32 = (bf16[496,768]{1,0:T(8,128)(2,1)}, bf16[496,768]{1,0:T(8,128)(2,1)}, u32[]{:S(2)}, u32[]{:S(2)}) collective-permute-start(bf16[496,768]{1,0:T(8,128)(2,1)} %get-tuple-element.125), channel_id=1, source_target_pairs={{0,16},{8,24},{16,0},{24,8},{1,17},{9,25},{17,1},{25,9},{2,18},{10... | collective-permute-start | bytes 2285576 | tf_op jit(solution)/shard_map/ppermute | solution.py:36
  326.7 43.5 %collective-permute-start.33 = (bf16[496,768]{1,0:T(8,128)(2,1)}, bf16[496,768]{1,0:T(8,128)(2,1)}, u32[]{:S(2)}, u32[]{:S(2)}) collective-permute-start(bf16[496,768]{1,0:T(8,128)(2,1)} %get-tuple-element.126), channel_id=1, source_target_pairs={{0,24},{8,16},{16,8},{24,0},{1,25},{9,17},{17,9},{25,1},{2,26},{10... | collective-permute-start | bytes 2285576 | tf_op jit(solution)/shard_map/ppermute | solution.py:36
  359.5 59.9 %collective-permute-start.35 = (bf16[2,4,96,1536]{3,2,1,0:T(8,128)(2,1)}, bf16[2,4,96,1536]{3,2,1,0:T(8,128)(2,1)}, u32[]{:S(2)}, u32[]{:S(2)}) collective-permute-start(bf16[2,4,96,1536]{3,2,1,0:T(8,128)(2,1)} %get-tuple-element.285), channel_id=1, source_target_pairs={{0,1},{1,0},{2,3},{3,2},{4,5},{5,4},{6,7},{7,6},{8,9},{9,8},{10,11... | collective-permute-start | bytes 7077896 | tf_op jit(solution)/shard_map/ppermute | solution.py:58
  364.7 96.3 %collective-permute-start.42 = (bf16[2,96,1536]{2,1,0:T(8,128)(2,1)}, bf16[2,96,1536]{2,1,0:T(8,128)(2,1)S(1)}, u32[]{:S(2)}, u32[]{:S(2)}) collective-permute-start(bf16[2,96,1536]{2,1,0:T(8,128)(2,1)} %get-tuple-element.295), channel_id=1, source_target_pairs={{0,6},{1,7},{2,4},{3,5},{4,2},{5,3},{6,0},{7,1},{8,14},{9,15},{10,... | collective-permute-start | bytes 1769480 | tf_op jit(solution)/shard_map/ppermute | solution.py:58
  366.1 58.9 %collective-permute-start.37 = (bf16[2,96,1536]{2,1,0:T(8,128)(2,1)}, bf16[2,96,1536]{2,1,0:T(8,128)(2,1)}, u32[]{:S(2)}, u32[]{:S(2)}) collective-permute-start(bf16[2,96,1536]{2,1,0:T(8,128)(2,1)} %get-tuple-element.296), channel_id=1, source_target_pairs={{0,4},{1,5},{2,6},{3,7},{4,0},{5,1},{6,2},{7,3},{8,12},{9,13},{10,... | collective-permute-start | bytes 1769480 | tf_op jit(solution)/shard_map/ppermute | solution.py:58
  370.2 54.8 %collective-permute-start.36 = (bf16[2,96,1536]{2,1,0:T(8,128)(2,1)}, bf16[2,96,1536]{2,1,0:T(8,128)(2,1)}, u32[]{:S(2)}, u32[]{:S(2)}) collective-permute-start(bf16[2,96,1536]{2,1,0:T(8,128)(2,1)} %get-tuple-element.297), channel_id=1, source_target_pairs={{0,2},{1,3},{2,0},{3,1},{4,6},{5,7},{6,4},{7,5},{8,10},{9,11},{10,... | collective-permute-start | bytes 1769480 | tf_op jit(solution)/shard_map/ppermute | solution.py:58
  402.0 46.5 %collective-permute-start.39 = (bf16[208,768]{1,0:T(8,128)(2,1)}, bf16[208,768]{1,0:T(8,128)(2,1)S(1)}, u32[]{:S(2)}, u32[]{:S(2)}) collective-permute-start(bf16[208,768]{1,0:T(8,128)(2,1)} %pad_maximum_fusion.11), channel_id=1, source_target_pairs={{1,0},{2,1},{3,2},{4,3},{5,4},{6,5},{7,6},{8,7},{9,8},{10,9},{11,1... | collective-permute-start | bytes 958472 | tf_op jit(solution)/shard_map/ppermute | solution.py:47
  503.2 39.0 %collective-permute-start.45 = (bf16[4,96,1664]{2,1,0:T(8,128)(2,1)S(1)}, bf16[4,96,1664]{2,1,0:T(8,128)(2,1)S(1)}, u32[]{:S(2)}, u32[]{:S(2)}) collective-permute-start(bf16[4,96,1664]{2,1,0:T(8,128)(2,1)S(1)} %dynamic-slice_bitcast_fusion.3), channel_id=1, source_target_pairs={{0,1},{1,0},{2,3},{3,2},{4,5},{5,4},{6,7},{7,6},{8,9},{9,8},{10,11... | collective-permute-start | bytes 3833864 | tf_op jit(solution)/shard_map/ppermute | solution.py:58
  507.8 40.8 %collective-permute-start.53 = (bf16[2,96,1536]{2,1,0:T(8,128)(2,1)}, bf16[2,96,1536]{2,1,0:T(8,128)(2,1)S(1)}, u32[]{:S(2)}, u32[]{:S(2)}) collective-permute-start(bf16[2,96,1536]{2,1,0:T(8,128)(2,1)} %get-tuple-element.291), channel_id=1, source_target_pairs={{0,6},{1,7},{2,4},{3,5},{4,2},{5,3},{6,0},{7,1},{8,14},{9,15},{10,... | collective-permute-start | bytes 1769480 | tf_op jit(solution)/shard_map/ppermute | solution.py:58
  507.9 58.2 %collective-permute-start.52 = (bf16[2,96,1536]{2,1,0:T(8,128)(2,1)}, bf16[2,96,1536]{2,1,0:T(8,128)(2,1)S(1)}, u32[]{:S(2)}, u32[]{:S(2)}) collective-permute-start(bf16[2,96,1536]{2,1,0:T(8,128)(2,1)} %get-tuple-element.292), channel_id=1, source_target_pairs={{0,4},{1,5},{2,6},{3,7},{4,0},{5,1},{6,2},{7,3},{8,12},{9,13},{10,... | collective-permute-start | bytes 1769480 | tf_op jit(solution)/shard_map/ppermute | solution.py:58
  540.6 63.9 %collective-permute-start.57 = (bf16[2,96,1536]{2,1,0:T(8,128)(2,1)S(1)}, bf16[2,96,1536]{2,1,0:T(8,128)(2,1)S(1)}, u32[]{:S(2)}, u32[]{:S(2)}) collective-permute-start(bf16[2,96,1536]{2,1,0:T(8,128)(2,1)S(1)} %add_convert_fusion.3.refs_6_), channel_id=1, source_target_pairs={{0,8},{8,0},{16,24},{24,16},{1,9},{9,1},{17,25},{25,17},{2,10},{10... | collective-permute-start | bytes 1769480 | tf_op jit(solution)/shard_map/ppermute | solution.py:36
  540.7 49.1 %collective-permute-start.51 = (bf16[2,96,1536]{2,1,0:T(8,128)(2,1)S(1)}, bf16[2,96,1536]{2,1,0:T(8,128)(2,1)}, u32[]{:S(2)}, u32[]{:S(2)}) collective-permute-start(bf16[2,96,1536]{2,1,0:T(8,128)(2,1)S(1)} %add_convert_fusion.3.refs_6_), channel_id=1, source_target_pairs={{0,16},{8,24},{16,0},{24,8},{1,17},{9,25},{17,1},{25,9},{2,18},{10... | collective-permute-start | bytes 1769480 | tf_op jit(solution)/shard_map/ppermute | solution.py:36
  589.7 49.6 %collective-permute-start.55 = (bf16[2,96,1536]{2,1,0:T(8,128)(2,1)}, bf16[2,96,1536]{2,1,0:T(8,128)(2,1)}, u32[]{:S(2)}, u32[]{:S(2)}) collective-permute-start(bf16[2,96,1536]{2,1,0:T(8,128)(2,1)} %collective-permute-done.51.refs_6_), channel_id=1, source_target_pairs={{0,8},{8,0},{16,24},{24,16},{1,9},{9,1},{17,25},{25,17},{2,10},{10... | collective-permute-start | bytes 1769480 | tf_op jit(solution)/shard_map/ppermute | solution.py:36
  596.4 42.9 %collective-permute-start.56 = (bf16[2,96,1536]{2,1,0:T(8,128)(2,1)}, bf16[2,96,1536]{2,1,0:T(8,128)(2,1)}, u32[]{:S(2)}, u32[]{:S(2)}) collective-permute-start(bf16[2,96,1536]{2,1,0:T(8,128)(2,1)} %collective-permute-done.54.refs_7_), channel_id=1, source_target_pairs={{0,8},{8,0},{16,24},{24,16},{1,9},{9,1},{17,25},{25,17},{2,10},{10... | collective-permute-start | bytes 1769480 | tf_op jit(solution)/shard_map/ppermute | solution.py:36
  (105 other events, 1488.5 us)

commit v6 on v5

--- a/solution.py
+++ b/solution.py
@@ -710,8 +710,7 @@
         half = lax.dynamic_slice_in_dim(matrix, core * cut_to, cut_to, axis=1)
         return gather_far(jnp.concatenate([half, side], axis=1).astype(BF16))
 
-    def dense_place(pieces, after=()):
-        own = gather_near(jnp.stack(pieces))
+    def dense_place(own, after=()):
         return place_pieces(own, [swap(block, CORE_BIT) for block in own], place, after)
 
     small = jnp.concatenate([norm_weight.T, router_weight], axis=1)
@@ -745,11 +744,8 @@
     group = far * near
     far_pieces = [gather_far(tie(expert_cut(0), qkv_far[-1]))]
     far_pieces.append(gather_far(tie(expert_cut(1), far_pieces[0][-1])))
-    dy_parts = exchange(
-        pack(out_grad, ranks, capacity, (far_pieces[0][1], far_pieces[0][3]))
-    )
-    qkv_full, small_full = dense_place(qkv_far)
-    proj_full, _ = dense_place(proj_far, tuple(dy_parts[2:]))
+    qkv_near, proj_near = [gather_near(jnp.stack(pieces)) for pieces in (qkv_far, proj_far)]
+    qkv_full, small_full = dense_place(qkv_near, tuple(proj_near[1:]))
     small_rows = small_full[:, :8].T
     norm_full = small_rows[:4].astype(F32)
     router_t = small_rows[4:8]
@@ -759,6 +755,8 @@
     normed_one, scale_one = standardize(x_float)
     first_in = (normed_one * norm_full[0] + norm_full[1]).astype(BF16)
     qkv_rows = jnp.dot(first_in, qkv_full, preferred_element_type=F32).astype(BF16)
+    dy_parts = exchange(pack(out_grad, ranks, capacity, (*far_pieces[0][1:], qkv_rows)))
+    proj_full, _ = dense_place(proj_near, tuple(dy_parts[2:]))
     kv_rows = qkv_rows[:, width:]
     below, above = shift(kv_rows[:HALO], kv_rows[row_count - HALO :], ("replica", "group"))
     kv_window = jnp.concatenate([below, kv_rows, above], axis=0)
@@ -770,7 +768,7 @@
     first_key = jnp.tile(first_key.reshape(-1, QB), (1, 2))
     last_key = jnp.tile(last_key.reshape(-1, QB), (1, 2))
     context, lse = attend(qkv_rows, kv_window, first_key, last_key, scale)
-    sources = [gather_near(jnp.stack([tie(far_pieces[0][0], context), *far_pieces[0][1:]]))]
+    sources = [gather_near(jnp.stack(far_pieces[0]))]
     residual = x_float + jnp.dot(context, proj_full, preferred_element_type=F32)
     normed_two, scale_two = standardize(residual)
     second_in = (normed_two * norm_full[2] + norm_full[3]).astype(BF16)
@@ -896,6 +894,7 @@
     small_grad = jnp.pad(small_grad, ((0, 0), (0, LANES - small_grad.shape[1]))).astype(BF16)
     columns = 3 * width // 2
     qkv_grad, proj_grad = qkv_grad.astype(BF16), proj_grad.astype(BF16)
+    qkv_grad = tie(qkv_grad, high_parts[2])
     dense_grads = jnp.stack(
         [
             jnp.concatenate([qkv_grad[:, :columns], proj_grad[:, : width // 2], small_grad], axis=1),

time: 662 us -> 663 us (level)
  starting transfers between devices: 89.5 us -> 102 us
  waiting for transfers between devices: 196 us -> 184 us
    ppermute x28, starting transfers between devices: 32.8 us -> 39.7 us  [group_swap(): return lax.ppermute(block, 'group', [(g, g ^ flip) for g in range(count)])]
    unnamed x169 -> x183, local copies, waits for them, and re-layouts: 23.4 us -> 20.6 us
  transfers between devices with their start and end apart: 59 -> 59, of which waited for: 21 -> 21; matrix products, arithmetic and copies ran while one was open for 19% -> 20% of each run, Pallas kernels for 31% -> 30%
where the time goes in v6:
time: 663 us; the launch traced here: 656 us
  Pallas kernels  212 us (32%)
  waiting for transfers between devices  184 us (28%)
  starting transfers between devices  102 us (15%)
  local copies, waits for them, and re-layouts  72.9 us (11%)
  other arithmetic  53.2 us (8%)
  matrix products  28.9 us (4%)
    ppermute x28, waiting for transfers between devices, group_swap(): return lax.ppermute(block, 'group', [(g, g ^ flip) for g in range(count)])  148 us
    pallas_call x4, Pallas kernels, expert(): pl.pallas_call(partial(expert_kernel, count, others, near, first, expert_...  107 us
    ppermute x25, starting transfers between devices, swap(): return lax.ppermute(block, 'replica', [(r, r ^ bit) for r in range(count)])  45.5 us
    ppermute x28, starting transfers between devices, group_swap(): return lax.ppermute(block, 'group', [(g, g ^ flip) for g in range(count)])  39.7 us
    ppermute x25, waiting for transfers between devices, swap(): return lax.ppermute(block, 'replica', [(r, r ^ bit) for r in range(count)])  27.3 us
    pallas_call x2, Pallas kernels, update_experts(): pl.pallas_call(partial(update_kernel, base), grid_spec=pltpu.PrefetchScal...  25.2 us
    pallas_call x2, Pallas kernels, attend_back(): pl.pallas_call(partial(attend_back_kernel, scale), grid=(count,), in_spec...  25.1 us
    pallas_call x1, Pallas kernels, attend(): pl.pallas_call(partial(attend_kernel, scale), grid=(pairs,), in_specs=[pl...  23.9 us
  transfers between devices with their start and end apart: 59, of which 21 were waited for; matrix products, arithmetic and copies ran while one was open for 20% of the time, Pallas kernels for 30%

profile of v6, /device:TPU:23, one launch (start us, length us, event | category | flops | bytes accessed | tf_op | source)
XLA Modules:
  0.0 656.1 jit_solution(298418988381943169)
XLA Ops:
  13.2 13.5 %collective-permute-done.2.refs_1_ = bf16[96,1280]{1,0:T(8,128)(2,1)S(1)} collective-permute-done((bf16[96,1280]{1,0:T(8,128)(2,1)S(1)}, bf16[96,1280]{1,0:T(8,128)(2,1)S(1)}, u32[]{:S(2)}, u32[]{:S(2)}) %collective-permute-start.2) | collective-permute-done | bytes 245792 | tf_op jit(solution)/shard_map/ppermute | solution.py:58
  37.1 13.6 %collective-permute-done.3.refs_1_ = bf16[4,96,1280]{2,1,0:T(8,128)(2,1)} collective-permute-done((bf16[4,96,1280]{2,1,0:T(8,128)(2,1)S(1)}, bf16[4,96,1280]{2,1,0:T(8,128)(2,1)}, u32[]{:S(2)}, u32[]{:S(2)}) %collective-permute-start.3) | collective-permute-done | bytes 983072 | tf_op jit(solution)/shard_map/ppermute | solution.py:58
  67.7 5.7 collective-permute-start.14
  79.5 5.5 convolution_convert_fusion.1.q_ref.refs_3_
  94.8 6.5 collective-permute-done.16.refs_2_.refs_1_
  102.4 21.2 %collective-permute-done.15.refs_1_ = bf16[2,96,1536]{2,1,0:T(8,128)(2,1)S(1)} collective-permute-done((bf16[2,96,1536]{2,1,0:T(8,128)(2,1)}, bf16[2,96,1536]{2,1,0:T(8,128)(2,1)S(1)}, u32[]{:S(2)}, u32[]{:S(2)}) %collective-permute-start.15) | collective-permute-done | bytes 589856 | tf_op jit(solution)/shard_map/ppermute | solution.py:58
  137.6 23.9 %attend.1 = (bf16[768,768]{1,0:T(8,128)(2,1)}, f32[6,8,256]{2,1,0:T(8,128)}) custom-call(bf16[768,2304]{1,0:T(8,128)(2,1)} %copy-done.7, bf16[1184,1536]{1,0:T(8,128)(2,1)} %pad_maximum_fusion.k_ref.v_ref, bf16[1184,1536]{1,0:T(8,128)(2,1)} %pad_maximum_fusion.k_ref.v_ref, s32[6,256]{1,0:T(8,128)} %bitcast.207, s32[6,256]{1,0:T(8,128)} %bitcast.204), custom_call_target="tpu_custom_call" | custom-call | flops 30000001024 | bytes 100000 | tf_op jit(solution)/shard_map/attend/pallas_call | solution.py:258
  198.4 19.1 %expert.4 = (f32[480,768]{1,0:T(8,128)}, f32[480,768]{1,0:T(8,128)}, f32[480,768]{1,0:T(8,128)}, f32[480,768]{1,0:T(8,128)}, bf16[480,768]{1,0:T(8,128)(2,1)}, /...) custom-call(s32[4]{0:T(128)} %pad_add_fusion.place_ref, ...), custom_call_target="tpu_custom_call" | custom-call | flops 28000000000 | bytes 100000 | tf_op jit(solution)/shard_map/expert/pallas_call | solution.py:594
  217.5 13.8 %collective-permute-done.24 = bf16[2,96,1536]{2,1,0:T(8,128)(2,1)S(1)} collective-permute-done((bf16[2,96,1536]{2,1,0:T(8,128)(2,1)S(1)}, bf16[2,96,1536]{2,1,0:T(8,128)(2,1)S(1)}, u32[]{:S(2)}, u32[]{:S(2)}) %collective-permute-start.24) | collective-permute-done | bytes 589856 | tf_op jit(solution)/shard_map/ppermute | solution.py:58
  231.3 10.7 %collective-permute-done.23 = bf16[2,96,1536]{2,1,0:T(8,128)(2,1)} collective-permute-done((bf16[2,96,1536]{2,1,0:T(8,128)(2,1)S(1)}, bf16[2,96,1536]{2,1,0:T(8,128)(2,1)}, u32[]{:S(2)}, u32[]{:S(2)}) %collective-permute-start.23) | collective-permute-done | bytes 589856 | tf_op jit(solution)/shard_map/ppermute | solution.py:58
  245.0 31.7 %expert.5 = (f32[480,768]{1,0:T(8,128)}, f32[480,768]{1,0:T(8,128)}, f32[480,768]{1,0:T(8,128)}, f32[480,768]{1,0:T(8,128)}, bf16[480,768]{1,0:T(8,128)(2,1)}, /...) custom-call(s32[4]{0:T(128)} %pad_add_fusion.place_ref, bf16[768,128]{1,0:T(8,128)(2,1)} %pad.16.router_ref, ...), custom_call_target="tpu_custom_call" | custom-call | flops 28000000000 | bytes 100000 | tf_op jit(solution)/shard_map/expert/pallas_call | solution.py:594
  281.2 16.1 %collective-permute-done.25.refs_7_.refs_3_ = bf16[4,2,96,1536]{3,2,1,0:T(8,128)(2,1)} collective-permute-done((bf16[4,2,96,1536]{3,2,1,0:T(8,128)(2,1)}, bf16[4,2,96,1536]{3,2,1,0:T(8,128)(2,1)}, u32[]{:S(2)}, u32[]{:S(2)}) %collective-permute-start.25) | collective-permute-done | bytes 2359328 | tf_op jit(solution)/shard_map/ppermute | solution.py:58
  297.4 29.1 %expert.6 = (bf16[480,768]{1,0:T(8,128)(2,1)}, bf16[480,768]{1,0:T(8,128)(2,1)}, bf16[480,768]{1,0:T(8,128)(2,1)}, bf16[496,768]{1,0:T(8,128)(2,1)}, bf16[496,76...) custom-call(s32[4]{0:T(128)} %pad_add_fusion.place_ref, ...), custom_call_target="tpu_custom_call" | custom-call | flops 28000000000 | bytes 100000 | tf_op jit(solution)/shard_map/expert/pallas_call | solution.py:594
  330.9 27.4 %expert.7 = (bf16[480,768]{1,0:T(8,128)(2,1)}, bf16[496,768]{1,0:T(8,128)(2,1)}, bf16[2,768,1536]{2,1,0:T(8,128)(2,1)}) custom-call(s32[4]{0:T(128)} %pad_add_fusion.place_ref, bf16[768,128]{1,0:T(8,128)(2,1)} %pad.16.router_ref, bf16[480,768]{1,0:T(8,128)(2,1)} %get-tuple-element.91.refs_0_.refs_6_, bf16[480,768]{1,0:T(8,128)(2,1)} %get-tuple-element.92.refs_2_.refs_1_, ...), custom_call_target="tpu_custom_call" | custom-call | flops 28000000000 | bytes 100000 | tf_op jit(solution)/shard_map/expert/pallas_call | solution.py:594
  358.3 4.9 dynamic-slice_bitcast_fusion.1
  374.1 7.1 %unpack_grad.1 = (f32[768,768]{1,0:T(8,128)}, f32[768,128]{1,0:T(8,128)}) custom-call(bf16[496,768]{1,0:T(8,128)(2,1)} %get-tuple-element.123.refs_0_, bf16[496,768]{1,0:T(8,128)(2,1)} %copy-done.48, bf16[496,768]{1,0:T(8,128)(2,1)} %collective-permute-done.32.refs_2_, bf16[496,768]{1,0:T(8,128)(2,1)} %collective-permute-done.33.refs_3_, ...), custom_call_target="tpu_custom_call" | custom-call | tf_op jit(solution)/shard_map/unpack_grad/pallas_call | solution.py:386
  390.7 12.5 %attend_back.2 = (bf16[768,384]{1,0:T(8,128)(2,1)}, bf16[1184,384]{1,0:T(8,128)(2,1)}, bf16[1184,384]{1,0:T(8,128)(2,1)}) custom-call(bf16[768,2304]{1,0:T(8,128)(2,1)} %copy-done.7, bf16[1184,1536]{1,0:T(8,128)(2,1)} %pad_maximum_fusion.k_ref.v_ref, bf16[1184,1536]{1,0:T(8,128)(2,1)} %pad_maximum_fusion.k_ref.v_ref, ...), custom_call_target="tpu_custom_call" | custom-call | flops 15000000512 | bytes 100000 | tf_op jit(solution)/shard_map/attend_back/pallas_call | solution.py:290
  413.9 9.2 %collective-permute-done.35 = bf16[2,4,96,1536]{3,2,1,0:T(8,128)(2,1)} collective-permute-done((bf16[2,4,96,1536]{3,2,1,0:T(8,128)(2,1)}, bf16[2,4,96,1536]{3,2,1,0:T(8,128)(2,1)}, u32[]{:S(2)}, u32[]{:S(2)}) %collective-permute-start.35) | collective-permute-done | bytes 2359328 | tf_op jit(solution)/shard_map/ppermute | solution.py:58
  428.8 12.5 %attend_back.3 = (bf16[768,384]{1,0:T(8,128)(2,1)}, bf16[1184,384]{1,0:T(8,128)(2,1)}, bf16[1184,384]{1,0:T(8,128)(2,1)}) custom-call(bf16[768,2304]{1,0:T(8,128)(2,1)} %copy-done.7, bf16[1184,1536]{1,0:T(8,128)(2,1)} %pad_maximum_fusion.k_ref.v_ref, bf16[1184,1536]{1,0:T(8,128)(2,1)} %pad_maximum_fusion.k_ref.v_ref, ...), custom_call_target="tpu_custom_call" | custom-call | flops 15000000512 | bytes 100000 | tf_op jit(solution)/shard_map/attend_back/pallas_call | solution.py:290
  457.5 5.2 collective-permute-done.40
  465.7 14.9 %collective-permute-done.43.refs_2_ = bf16[2,96,1536]{2,1,0:T(8,128)(2,1)S(1)} collective-permute-done((bf16[2,96,1536]{2,1,0:T(8,128)(2,1)S(1)}, bf16[2,96,1536]{2,1,0:T(8,128)(2,1)S(1)}, u32[]{:S(2)}, u32[]{:S(2)}) %collective-permute-start.43) | collective-permute-done | bytes 589856 | tf_op jit(solution)/shard_map/ppermute | solution.py:58
  481.5 7.8 %fusion.23 = (bf16[768]{0:T(1024)(128)(2,1)S(1)}, f32[768]{0:T(1024)S(1)}, f32[768]{0:T(1024)S(1)}, bf16[768]{0:T(1024)(128)(2,1)S(1)}, f32[768,768]{1,0:T(8,128)}) fusion(bf16[768,768]{1,0:T(8,128)(2,1)S(1)} %copy-done.10, f32[768]{0:T(1024)S(1)} %copy-done.68, f32[768]{0:T(1024)S(1)} %copy-done.59, f32[768]{0:T(1024)S(1)} %copy-done.65, ...), kind=kOutput, calls=%fused_computation.39 | convolution fusion | flops 2723804160 | bytes 10635264 | tf_op jit(solution)/shard_map/dot_general | solution.py:885
  489.3 4.9 convolution_convert_fusion.refs_0_
  509.9 6.2 collective-permute-start.29
  526.5 6.4 collective-permute-done.29.refs_2_
  532.9 16.3 %collective-permute-done.30.refs_3_ = bf16[480,768]{1,0:T(8,128)(2,1)} collective-permute-done((bf16[480,768]{1,0:T(8,128)(2,1)}, bf16[480,768]{1,0:T(8,128)(2,1)}, u32[]{:S(2)}, u32[]{:S(2)}) %collective-permute-start.30) | collective-permute-done | bytes 737312 | tf_op jit(solution)/shard_map/ppermute | solution.py:36
  549.2 7.1 %unpack_out.1 = bf16[768,768]{1,0:T(8,128)(2,1)} custom-call(f32[768,768]{1,0:T(8,128)} %copy-done, bf16[480,768]{1,0:T(8,128)(2,1)} %get-tuple-element.119.refs_0_, bf16[480,768]{1,0:T(8,128)(2,1)} %copy-done.51, bf16[480,768]{1,0:T(8,128)(2,1)} %collective-permute-done.29.refs_2_, bf16[480,768]{1,0:T(8,128)(2,1)} %collective-permute-done.30.refs_3_, ...), custom_call_target="tpu_custom_call" | custom-call | tf_op jit(solution)/shard_map/unpack_out/pallas_call | solution.py:412
  567.8 8.4 %collective-permute-done.47 = bf16[96,1664]{1,0:T(8,128)(2,1)S(1)} collective-permute-done((bf16[96,1664]{1,0:T(8,128)(2,1)S(1)}, bf16[96,1664]{1,0:T(8,128)(2,1)S(1)}, u32[]{:S(2)}, u32[]{:S(2)}) %collective-permute-start.47) | collective-permute-done | bytes 319520 | tf_op jit(solution)/shard_map/ppermute | solution.py:58
  577.5 7.5 %collective-permute-done.49 = bf16[96,1664]{1,0:T(8,128)(2,1)S(1)} collective-permute-done((bf16[96,1664]{1,0:T(8,128)(2,1)S(1)}, bf16[96,1664]{1,0:T(8,128)(2,1)S(1)}, u32[]{:S(2)}, u32[]{:S(2)}) %collective-permute-start.49) | collective-permute-done | bytes 319520 | tf_op jit(solution)/shard_map/ppermute | solution.py:58
  597.1 7.0 %collective-permute-start.56 = (bf16[2,96,1536]{2,1,0:T(8,128)(2,1)}, bf16[2,96,1536]{2,1,0:T(8,128)(2,1)}, u32[]{:S(2)}, u32[]{:S(2)}) collective-permute-start(bf16[2,96,1536]{2,1,0:T(8,128)(2,1)} %collective-permute-done.54.refs_7_), channel_id=1, source_target_pairs={{0,8},{8,0},{16,24},{24,16},{1,9},{9,1},{17,25},{25,17},{2,10},{10... | collective-permute-start | bytes 1769480 | tf_op jit(solution)/shard_map/ppermute | solution.py:36
  608.8 12.6 %update_experts.2 = (f32[4,96,3072]{2,1,0:T(8,128)}, f32[4,96,3072]{2,1,0:T(8,128)}, f32[4,96,3072]{2,1,0:T(8,128)}, f32[4,96,3072]{2,1,0:T(8,128)}, f32[4,96,3072]{2,1,0:T(8,128)}, /*index=5*/f32[4,96,3072]{2,1,0:T(8,128)}) custom-call(s32[1]{0:T(128)} %bitcast.3.mine_ref, f32[4,96,3072]{2,1,0:T(8,128)} %refs_0_.3, f32[4,96,3072]{2,1,0:T(8,128)} %refs_1_.3, ...), custom_call_target="tpu_custom_call" | custom-call | flops 10000000000 | bytes 100000 | tf_op jit(solution)/shard_map/update_experts/pallas_call | solution.py:654
  643.0 12.6 %update_experts.3 = (f32[4,96,3072]{2,1,0:T(8,128)}, f32[4,96,3072]{2,1,0:T(8,128)}, f32[4,96,3072]{2,1,0:T(8,128)}, f32[4,96,3072]{2,1,0:T(8,128)}, f32[4,96,3072]{2,1,0:T(8,128)}, /*index=5*/f32[4,96,3072]{2,1,0:T(8,128)}) custom-call(s32[1]{0:T(128)} %bitcast.3.mine_ref, ...), custom_call_target="tpu_custom_call", output_to_operand_aliasing={{0}: (11, {}), {1}: (12, {}), {2}: (13, {}), {3}: (14, {}),... | custom-call | flops 10000000000 | bytes 100000 | tf_op jit(solution)/shard_map/update_experts/pallas_call | solution.py:654
  (434 shorter events, 252.3 us)
Async XLA Ops:
  2.3 52.6 %collective-permute-start.7 = (bf16[96,512]{1,0:T(8,128)(2,1)}, bf16[96,512]{1,0:T(8,128)(2,1)S(1)}, u32[]{:S(2)}, u32[]{:S(2)}) collective-permute-start(bf16[96,512]{1,0:T(8,128)(2,1)} %get-tuple-element.322), channel_id=1, source_target_pairs={{0,4},{1,5},{2,6},{3,7},{4,0},{5,1},{6,2},{7,3},{8,12},{9,13},{10,... | collective-permute-start | bytes 294920 | tf_op jit(solution)/shard_map/ppermute | solution.py:58
  2.3 52.6 %collective-permute-start.6 = (bf16[96,512]{1,0:T(8,128)(2,1)}, bf16[96,512]{1,0:T(8,128)(2,1)S(1)}, u32[]{:S(2)}, u32[]{:S(2)}) collective-permute-start(bf16[96,512]{1,0:T(8,128)(2,1)} %get-tuple-element.322), channel_id=1, source_target_pairs={{0,2},{1,3},{2,0},{3,1},{4,6},{5,7},{6,4},{7,5},{8,10},{9,11},{10,... | collective-permute-start | bytes 294920 | tf_op jit(solution)/shard_map/ppermute | solution.py:58
  33.6 39.8 %collective-permute-start.4 = (bf16[4,96,1280]{2,1,0:T(8,128)(2,1)S(1)}, bf16[4,96,1280]{2,1,0:T(8,128)(2,1)}, u32[]{:S(2)}, u32[]{:S(2)}) collective-permute-start(bf16[4,96,1280]{2,1,0:T(8,128)(2,1)S(1)} %pad_maximum_fusion.5.refs_0_), channel_id=1, source_target_pairs={{0,8},{8,0},{16,24},{24,16},{1,9},{9,1},{17,25},{25,17},{2,10},{10... | collective-permute-start | bytes 2949128 | tf_op jit(solution)/shard_map/ppermute | solution.py:36
  58.4 42.9 %collective-permute-start.16 = (bf16[2,96,1536]{2,1,0:T(8,128)(2,1)}, bf16[2,96,1536]{2,1,0:T(8,128)(2,1)S(1)}, u32[]{:S(2)}, u32[]{:S(2)}) collective-permute-start(bf16[2,96,1536]{2,1,0:T(8,128)(2,1)} %tie.8), channel_id=1, source_target_pairs={{0,6},{1,7},{2,4},{3,5},{4,2},{5,3},{6,0},{7,1},{8,14},{9,15},{10,... | collective-permute-start | bytes 1769480 | tf_op jit(solution)/shard_map/ppermute | solution.py:58
  62.2 61.4 %collective-permute-start.15 = (bf16[2,96,1536]{2,1,0:T(8,128)(2,1)}, bf16[2,96,1536]{2,1,0:T(8,128)(2,1)S(1)}, u32[]{:S(2)}, u32[]{:S(2)}) collective-permute-start(bf16[2,96,1536]{2,1,0:T(8,128)(2,1)} %tie.8), channel_id=1, source_target_pairs={{0,4},{1,5},{2,6},{3,7},{4,0},{5,1},{6,2},{7,3},{8,12},{9,13},{10,... | collective-permute-start | bytes 1769480 | tf_op jit(solution)/shard_map/ppermute | solution.py:58
  67.7 57.1 %collective-permute-start.14 = (bf16[2,96,1536]{2,1,0:T(8,128)(2,1)}, bf16[2,96,1536]{2,1,0:T(8,128)(2,1)S(1)}, u32[]{:S(2)}, u32[]{:S(2)}) collective-permute-start(bf16[2,96,1536]{2,1,0:T(8,128)(2,1)} %tie.8), channel_id=1, source_target_pairs={{0,2},{1,3},{2,0},{3,1},{4,6},{5,7},{6,4},{7,5},{8,10},{9,11},{10,... | collective-permute-start | bytes 1769480 | tf_op jit(solution)/shard_map/ppermute | solution.py:58
  86.2 45.1 %collective-permute-start.10 = (bf16[208,1536]{1,0:T(8,128)(2,1)}, bf16[208,1536]{1,0:T(8,128)(2,1)}, u32[]{:S(2)}, u32[]{:S(2)}) collective-permute-start(bf16[208,1536]{1,0:T(8,128)(2,1)} %get-tuple-element.288), channel_id=1, source_target_pairs={{0,1},{1,2},{2,3},{3,4},{4,5},{5,6},{6,7},{7,8},{8,9},{9,10},{10,1... | collective-permute-start | bytes 1916936 | tf_op jit(solution)/shard_map/ppermute | solution.py:47
  88.3 46.3 %collective-permute-start.11 = (bf16[208,1536]{1,0:T(8,128)(2,1)}, bf16[208,1536]{1,0:T(8,128)(2,1)}, u32[]{:S(2)}, u32[]{:S(2)}) collective-permute-start(bf16[208,1536]{1,0:T(8,128)(2,1)} %get-tuple-element.289), channel_id=1, source_target_pairs={{1,0},{2,1},{3,2},{4,3},{5,4},{6,5},{7,6},{8,7},{9,8},{10,9},{11,1... | collective-permute-start | bytes 1916936 | tf_op jit(solution)/shard_map/ppermute | solution.py:47
  101.3 60.2 %collective-permute-start.12 = (bf16[4,96,512]{2,1,0:T(8,128)(2,1)}, bf16[4,96,512]{2,1,0:T(8,128)(2,1)}, u32[]{:S(2)}, u32[]{:S(2)}) collective-permute-start(bf16[4,96,512]{2,1,0:T(8,128)(2,1)} %pad_maximum_fusion.9.refs_0_), channel_id=1, source_target_pairs={{0,8},{8,0},{16,24},{24,16},{1,9},{9,1},{17,25},{25,17},{2,10},{10... | collective-permute-start | bytes 1179656 | tf_op jit(solution)/shard_map/ppermute | solution.py:36
  123.6 42.7 %collective-permute-start.13 = (bf16[4,96,512]{2,1,0:T(8,128)(2,1)}, bf16[4,96,512]{2,1,0:T(8,128)(2,1)}, u32[]{:S(2)}, u32[]{:S(2)}) collective-permute-start(bf16[4,96,512]{2,1,0:T(8,128)(2,1)} %collective-permute-done.9.refs_4_.refs_1_), channel_id=1, source_target_pairs={{0,8},{8,0},{16,24},{24,16},{1,9},{9,1},{17,25},{25,17},{2,10},{10... | collective-permute-start | bytes 1179656 | tf_op jit(solution)/shard_map/ppermute | solution.py:36
  126.5 69.7 %collective-permute-start.22 = (bf16[4,2,96,1536]{3,2,1,0:T(8,128)(2,1)}, bf16[4,2,96,1536]{3,2,1,0:T(8,128)(2,1)}, u32[]{:S(2)}, u32[]{:S(2)}) collective-permute-start(bf16[4,2,96,1536]{3,2,1,0:T(8,128)(2,1)} %pad_maximum_fusion.1.refs_4_), channel_id=1, source_target_pairs={{0,1},{1,0},{2,3},{3,2},{4,5},{5,4},{6,7},{7,6},{8,9},{9,8},{10,11... | collective-permute-start | bytes 7077896 | tf_op jit(solution)/shard_map/ppermute | solution.py:58
  131.3 35.1 %collective-permute-start.17 = (bf16[480,768]{1,0:T(8,128)(2,1)}, bf16[480,768]{1,0:T(8,128)(2,1)S(1)}, u32[]{:S(2)}, u32[]{:S(2)}) collective-permute-start(bf16[480,768]{1,0:T(8,128)(2,1)} %get-tuple-element.88), channel_id=1, source_target_pairs={{0,16},{8,24},{16,0},{24,8},{1,17},{9,25},{17,1},{25,9},{2,18},{10... | collective-permute-start | bytes 2211848 | tf_op jit(solution)/shard_map/ppermute | solution.py:36
  191.1 40.2 %collective-permute-start.24 = (bf16[2,96,1536]{2,1,0:T(8,128)(2,1)S(1)}, bf16[2,96,1536]{2,1,0:T(8,128)(2,1)S(1)}, u32[]{:S(2)}, u32[]{:S(2)}) collective-permute-start(bf16[2,96,1536]{2,1,0:T(8,128)(2,1)S(1)} %copy-done.17), channel_id=1, source_target_pairs={{0,6},{1,7},{2,4},{3,5},{4,2},{5,3},{6,0},{7,1},{8,14},{9,15},{10,... | collective-permute-start | bytes 1769480 | tf_op jit(solution)/shard_map/ppermute | solution.py:58
  191.1 50.8 %collective-permute-start.23 = (bf16[2,96,1536]{2,1,0:T(8,128)(2,1)S(1)}, bf16[2,96,1536]{2,1,0:T(8,128)(2,1)}, u32[]{:S(2)}, u32[]{:S(2)}) collective-permute-start(bf16[2,96,1536]{2,1,0:T(8,128)(2,1)S(1)} %copy-done.17), channel_id=1, source_target_pairs={{0,4},{1,5},{2,6},{3,7},{4,0},{5,1},{6,2},{7,3},{8,12},{9,13},{10,... | collective-permute-start | bytes 1769480 | tf_op jit(solution)/shard_map/ppermute | solution.py:58
  196.1 48.9 %collective-permute-start.26 = (bf16[480,768]{1,0:T(8,128)(2,1)}, bf16[480,768]{1,0:T(8,128)(2,1)}, u32[]{:S(2)}, u32[]{:S(2)}) collective-permute-start(bf16[480,768]{1,0:T(8,128)(2,1)} %get-tuple-element.98), channel_id=1, source_target_pairs={{0,16},{8,24},{16,0},{24,8},{1,17},{9,25},{17,1},{25,9},{2,18},{10... | collective-permute-start | bytes 2211848 | tf_op jit(solution)/shard_map/ppermute | solution.py:36
  196.2 48.8 %collective-permute-start.27 = (bf16[480,768]{1,0:T(8,128)(2,1)}, bf16[480,768]{1,0:T(8,128)(2,1)}, u32[]{:S(2)}, u32[]{:S(2)}) collective-permute-start(bf16[480,768]{1,0:T(8,128)(2,1)} %get-tuple-element.99), channel_id=1, source_target_pairs={{0,24},{8,16},{16,8},{24,0},{1,25},{9,17},{17,9},{25,1},{2,26},{10... | collective-permute-start | bytes 2211848 | tf_op jit(solution)/shard_map/ppermute | solution.py:36
  244.9 52.5 %collective-permute-start.25 = (bf16[4,2,96,1536]{3,2,1,0:T(8,128)(2,1)}, bf16[4,2,96,1536]{3,2,1,0:T(8,128)(2,1)}, u32[]{:S(2)}, u32[]{:S(2)}) collective-permute-start(bf16[4,2,96,1536]{3,2,1,0:T(8,128)(2,1)} %pad_maximum_fusion.2.refs_14_.refs_6_.refs_2_), channel_id=1, source_target_pairs={{0,1},{1,0},{2,3},{3,2},{4,5},{5,4},{6,7},{7,6},{8,9},{9,8},{10,11... | collective-permute-start | bytes 7077896 | tf_op jit(solution)/shard_map/ppermute | solution.py:58
  279.9 83.7 %collective-permute-start.34 = (bf16[2,4,96,1536]{3,2,1,0:T(8,128)(2,1)}, bf16[2,4,96,1536]{3,2,1,0:T(8,128)(2,1)}, u32[]{:S(2)}, u32[]{:S(2)}) collective-permute-start(bf16[2,4,96,1536]{3,2,1,0:T(8,128)(2,1)} %dynamic-slice_bitcast_fusion.2), channel_id=1, source_target_pairs={{0,1},{1,0},{2,3},{3,2},{4,5},{5,4},{6,7},{7,6},{8,9},{9,8},{10,11... | collective-permute-start | bytes 7077896 | tf_op jit(solution)/shard_map/ppermute | solution.py:58
  326.5 43.5 %collective-permute-start.31 = (bf16[496,768]{1,0:T(8,128)(2,1)}, bf16[496,768]{1,0:T(8,128)(2,1)S(1)}, u32[]{:S(2)}, u32[]{:S(2)}) collective-permute-start(bf16[496,768]{1,0:T(8,128)(2,1)} %get-tuple-element.124), channel_id=1, source_target_pairs={{0,8},{8,0},{16,24},{24,16},{1,9},{9,1},{17,25},{25,17},{2,10},{10... | collective-permute-start | bytes 2285576 | tf_op jit(solution)/shard_map/ppermute | solution.py:36
  329.2 44.9 %collective-permute-start.32 = (bf16[496,768]{1,0:T(8,128)(2,1)}, bf16[496,768]{1,0:T(8,128)(2,1)}, u32[]{:S(2)}, u32[]{:S(2)}) collective-permute-start(bf16[496,768]{1,0:T(8,128)(2,1)} %get-tuple-element.125), channel_id=1, source_target_pairs={{0,16},{8,24},{16,0},{24,8},{1,17},{9,25},{17,1},{25,9},{2,18},{10... | collective-permute-start | bytes 2285576 | tf_op jit(solution)/shard_map/ppermute | solution.py:36
  329.4 44.6 %collective-permute-start.33 = (bf16[496,768]{1,0:T(8,128)(2,1)}, bf16[496,768]{1,0:T(8,128)(2,1)}, u32[]{:S(2)}, u32[]{:S(2)}) collective-permute-start(bf16[496,768]{1,0:T(8,128)(2,1)} %get-tuple-element.126), channel_id=1, source_target_pairs={{0,24},{8,16},{16,8},{24,0},{1,25},{9,17},{17,9},{25,1},{2,26},{10... | collective-permute-start | bytes 2285576 | tf_op jit(solution)/shard_map/ppermute | solution.py:36
  363.2 59.9 %collective-permute-start.35 = (bf16[2,4,96,1536]{3,2,1,0:T(8,128)(2,1)}, bf16[2,4,96,1536]{3,2,1,0:T(8,128)(2,1)}, u32[]{:S(2)}, u32[]{:S(2)}) collective-permute-start(bf16[2,4,96,1536]{3,2,1,0:T(8,128)(2,1)} %get-tuple-element.285), channel_id=1, source_target_pairs={{0,1},{1,0},{2,3},{3,2},{4,5},{5,4},{6,7},{7,6},{8,9},{9,8},{10,11... | collective-permute-start | bytes 7077896 | tf_op jit(solution)/shard_map/ppermute | solution.py:58
  368.8 96.9 %collective-permute-start.42 = (bf16[2,96,1536]{2,1,0:T(8,128)(2,1)}, bf16[2,96,1536]{2,1,0:T(8,128)(2,1)}, u32[]{:S(2)}, u32[]{:S(2)}) collective-permute-start(bf16[2,96,1536]{2,1,0:T(8,128)(2,1)} %get-tuple-element.295), channel_id=1, source_target_pairs={{0,6},{1,7},{2,4},{3,5},{4,2},{5,3},{6,0},{7,1},{8,14},{9,15},{10,... | collective-permute-start | bytes 1769480 | tf_op jit(solution)/shard_map/ppermute | solution.py:58
  370.0 58.8 %collective-permute-start.37 = (bf16[2,96,1536]{2,1,0:T(8,128)(2,1)}, bf16[2,96,1536]{2,1,0:T(8,128)(2,1)}, u32[]{:S(2)}, u32[]{:S(2)}) collective-permute-start(bf16[2,96,1536]{2,1,0:T(8,128)(2,1)} %get-tuple-element.296), channel_id=1, source_target_pairs={{0,4},{1,5},{2,6},{3,7},{4,0},{5,1},{6,2},{7,3},{8,12},{9,13},{10,... | collective-permute-start | bytes 1769480 | tf_op jit(solution)/shard_map/ppermute | solution.py:58
  374.1 54.7 %collective-permute-start.36 = (bf16[2,96,1536]{2,1,0:T(8,128)(2,1)}, bf16[2,96,1536]{2,1,0:T(8,128)(2,1)}, u32[]{:S(2)}, u32[]{:S(2)}) collective-permute-start(bf16[2,96,1536]{2,1,0:T(8,128)(2,1)} %get-tuple-element.297), channel_id=1, source_target_pairs={{0,2},{1,3},{2,0},{3,1},{4,6},{5,7},{6,4},{7,5},{8,10},{9,11},{10,... | collective-permute-start | bytes 1769480 | tf_op jit(solution)/shard_map/ppermute | solution.py:58
  406.1 46.1 %collective-permute-start.39 = (bf16[208,768]{1,0:T(8,128)(2,1)}, bf16[208,768]{1,0:T(8,128)(2,1)}, u32[]{:S(2)}, u32[]{:S(2)}) collective-permute-start(bf16[208,768]{1,0:T(8,128)(2,1)} %pad_maximum_fusion.11), channel_id=1, source_target_pairs={{1,0},{2,1},{3,2},{4,3},{5,4},{6,5},{7,6},{8,7},{9,8},{10,9},{11,1... | collective-permute-start | bytes 958472 | tf_op jit(solution)/shard_map/ppermute | solution.py:47
  452.2 42.0 %collective-permute-start.44 = (bf16[2,96,1536]{2,1,0:T(8,128)(2,1)}, bf16[2,96,1536]{2,1,0:T(8,128)(2,1)S(1)}, u32[]{:S(2)}, u32[]{:S(2)}) collective-permute-start(bf16[2,96,1536]{2,1,0:T(8,128)(2,1)} %get-tuple-element.292), channel_id=1, source_target_pairs={{0,4},{1,5},{2,6},{3,7},{4,0},{5,1},{6,2},{7,3},{8,12},{9,13},{10,... | collective-permute-start | bytes 1769480 | tf_op jit(solution)/shard_map/ppermute | solution.py:58
  521.9 38.1 %collective-permute-start.46 = (bf16[4,96,1664]{2,1,0:T(8,128)(2,1)S(1)}, bf16[4,96,1664]{2,1,0:T(8,128)(2,1)S(1)}, u32[]{:S(2)}, u32[]{:S(2)}) collective-permute-start(bf16[4,96,1664]{2,1,0:T(8,128)(2,1)S(1)} %dynamic-slice_bitcast_fusion.3), channel_id=1, source_target_pairs={{0,1},{1,0},{2,3},{3,2},{4,5},{5,4},{6,7},{7,6},{8,9},{9,8},{10,11... | collective-permute-start | bytes 3833864 | tf_op jit(solution)/shard_map/ppermute | solution.py:58
  526.5 36.5 %collective-permute-start.53 = (bf16[2,96,1536]{2,1,0:T(8,128)(2,1)}, bf16[2,96,1536]{2,1,0:T(8,128)(2,1)S(1)}, u32[]{:S(2)}, u32[]{:S(2)}) collective-permute-start(bf16[2,96,1536]{2,1,0:T(8,128)(2,1)} %get-tuple-element.291), channel_id=1, source_target_pairs={{0,6},{1,7},{2,4},{3,5},{4,2},{5,3},{6,0},{7,1},{8,14},{9,15},{10,... | collective-permute-start | bytes 1769480 | tf_op jit(solution)/shard_map/ppermute | solution.py:58
  558.4 49.4 %collective-permute-start.57 = (bf16[2,96,1536]{2,1,0:T(8,128)(2,1)S(1)}, bf16[2,96,1536]{2,1,0:T(8,128)(2,1)S(1)}, u32[]{:S(2)}, u32[]{:S(2)}) collective-permute-start(bf16[2,96,1536]{2,1,0:T(8,128)(2,1)S(1)} %add_convert_fusion.3.refs_6_), channel_id=1, source_target_pairs={{0,8},{8,0},{16,24},{24,16},{1,9},{9,1},{17,25},{25,17},{2,10},{10... | collective-permute-start | bytes 1769480 | tf_op jit(solution)/shard_map/ppermute | solution.py:36
  592.5 50.5 %collective-permute-start.55 = (bf16[2,96,1536]{2,1,0:T(8,128)(2,1)}, bf16[2,96,1536]{2,1,0:T(8,128)(2,1)}, u32[]{:S(2)}, u32[]{:S(2)}) collective-permute-start(bf16[2,96,1536]{2,1,0:T(8,128)(2,1)} %collective-permute-done.52.refs_6_), channel_id=1, source_target_pairs={{0,8},{8,0},{16,24},{24,16},{1,9},{9,1},{17,25},{25,17},{2,10},{10... | collective-permute-start | bytes 1769480 | tf_op jit(solution)/shard_map/ppermute | solution.py:36
  597.1 45.8 %collective-permute-start.56 = (bf16[2,96,1536]{2,1,0:T(8,128)(2,1)}, bf16[2,96,1536]{2,1,0:T(8,128)(2,1)}, u32[]{:S(2)}, u32[]{:S(2)}) collective-permute-start(bf16[2,96,1536]{2,1,0:T(8,128)(2,1)} %collective-permute-done.54.refs_7_), channel_id=1, source_target_pairs={{0,8},{8,0},{16,24},{24,16},{1,9},{9,1},{17,25},{25,17},{2,10},{10... | collective-permute-start | bytes 1769480 | tf_op jit(solution)/shard_map/ppermute | solution.py:36
  (113 other events, 1548.8 us)
